TPU v7x, 128 devices: a whole 4x4x4 slice. The times are simulated.
128 devices in a mesh: row: 8 (over y_hi, x), col: 16 (over y_lo, z, core).
Axes of the slice: x: 4, y: 4 (y_hi: 2, y_lo: 2; y = y_hi * 2 + y_lo), z: 4, core: 2. Of those that a mesh axis runs over, the one named last changes fastest.
Arguments:
- matrix: float32 [16384, 16384], P('row', 'col'), may hold values from -8 to 8, as said below
Outputs:
- next_matrix: float32 [16384, 16384], P('row', 'col')
Inputs may be any that keep to these rules, and one draw needn't show every extreme that they name: matrix is symmetric; within each diagonal pair block (rows and columns 2 * 512 * p to 2 * 512 * (p + 1) - 1) any two diagonal entries differ by at least 4 / 512.
All inputs are finite; a program needn't handle non-finite values.
Results may differ from a plain program's by a relative error of at most 0.000098.
Values sent between devices are 32-bit elements; how exact they have to be, the bound alone decides.
No kernel may reach another device: no remote copies, remote signals or barrier semaphores. Data moves between devices by JAX's collectives and lax.ppermute only.
A program may use at most 128 MiB of HBM per device.

v0:
```python
import jax
import jax.numpy as jnp
from jax import lax
from jax.sharding import PartitionSpec as P

highest = lax.Precision.HIGHEST


def from_root(shard, axis, root):
    mine = lax.axis_index(axis) == root
    return lax.psum(jnp.where(mine, shard, jnp.zeros_like(shard)), axis)


def with_halo(cells, sides, width):
    for axis, dim in sides:
        count = lax.axis_size(axis)
        ends = count - 1
        head = lax.slice_in_dim(cells, 0, width, axis=dim)
        tail = lax.slice_in_dim(cells, cells.shape[dim] - width, cells.shape[dim], axis=dim)
        cells = jnp.concatenate(
            [
                lax.ppermute(tail, axis, [(i, (i + 1) % count) for i in range(ends)]),
                cells,
                lax.ppermute(head, axis, [((i + 1) % count, i) for i in range(ends)]),
            ],
            axis=dim,
        )
    return cells


def first_guess_of(pair_block):
    matrix_order = pair_block.shape[0]
    diagonal = jnp.diagonal(pair_block)
    spacing = diagonal[None, :] - diagonal[:, None]
    identity = jnp.eye(matrix_order, dtype=jnp.float32)
    correction = jnp.where(identity > 0, 0.0, pair_block / (spacing + identity))
    return identity + correction


def rotation_of(pair_block):
    first_guess = first_guess_of(pair_block)
    identity = jnp.eye(pair_block.shape[0], dtype=jnp.float32)
    correlation = jnp.dot(
        first_guess.T, first_guess, precision=highest, preferred_element_type=jnp.float32
    )
    return jnp.dot(
        first_guess,
        1.5 * identity - 0.5 * correlation,
        precision=highest,
        preferred_element_type=jnp.float32,
    )


def nothing_here(pair_block):
    return jnp.zeros_like(pair_block)


def reorder_blocks(matrix_part, axis_dim, local_slots, first_slot, slot_total, transfer):
    block_width = matrix_part.shape[axis_dim] // (2 * local_slots)

    def block_at(position):
        return lax.slice_in_dim(
            matrix_part, position * block_width, (position + 1) * block_width, axis=axis_dim
        )

    outgoing = jnp.where(
        first_slot + local_slots - 1 == 0,
        block_at(2 * local_slots - 1),
        block_at(2 * local_slots - 2),
    )
    padded = transfer(jnp.concatenate([block_at(1), outgoing], axis=axis_dim))
    padded_width = padded.shape[axis_dim]
    from_before = lax.slice_in_dim(padded, 0, block_width, axis=axis_dim)
    from_after = lax.slice_in_dim(padded, padded_width - block_width, padded_width, axis=axis_dim)
    new_blocks = []
    for slot_offset in range(local_slots):
        global_slot = first_slot + slot_offset
        if slot_offset == 0:
            new_top = jnp.where(global_slot == 0, block_at(0), from_before)
        else:
            new_top = jnp.where(
                global_slot == 1, block_at(2 * slot_offset - 1), block_at(2 * slot_offset - 2)
            )
        if slot_offset < local_slots - 1:
            later_block = block_at(2 * slot_offset + 3)
        else:
            later_block = from_after
        new_bottom = jnp.where(
            global_slot == slot_total - 1, block_at(2 * slot_offset), later_block
        )
        new_blocks.append(new_top)
        new_blocks.append(new_bottom)
    return jnp.concatenate(new_blocks, axis=axis_dim)


def local(matrix):
    row_count = lax.axis_size("row")
    col_count = lax.axis_size("col")
    local_slots = col_count // row_count
    pair_width = matrix.shape[1]
    block_width = pair_width // 2
    row_index = lax.axis_index("row")
    col_index = lax.axis_index("col")
    local_slot = col_index - row_index * local_slots
    is_owner = (local_slot >= 0) & (local_slot < local_slots)
    safe_slot = jnp.clip(local_slot, 0, local_slots - 1)
    pair_block = lax.dynamic_slice_in_dim(matrix, safe_slot * pair_width, pair_width, 0)
    holder_row = col_index // local_slots
    own_rotation = lax.cond(is_owner, rotation_of, nothing_here, pair_block)
    column_rotation = from_root(own_rotation, "row", holder_row)
    slot_numbers = jnp.arange(local_slots, dtype=jnp.int32)
    selector = (slot_numbers == local_slot).astype(jnp.float32)
    contribution = selector[:, None, None] * column_rotation[None]
    row_rotations = lax.psum(contribution, "col")
    strips = matrix.reshape(local_slots, pair_width, pair_width)
    left_done = jnp.einsum("sji,sjk->sik", row_rotations, strips, precision=highest)
    rotated = jnp.dot(
        left_done.reshape(local_slots * pair_width, pair_width),
        column_rotation,
        precision=highest,
        preferred_element_type=jnp.float32,
    )
    row_moved = reorder_blocks(
        rotated,
        0,
        local_slots,
        row_index * local_slots,
        col_count,
        lambda edge_blocks: with_halo(edge_blocks, (("row", 0),), block_width),
    )
    result = reorder_blocks(
        row_moved,
        1,
        1,
        col_index,
        col_count,
        lambda edge_blocks: with_halo(edge_blocks, (("col", 1),), block_width),
    )
    return result


def solution(mesh):
    in_specs = (P("row", "col"),)
    out_specs = P("row", "col")
    return jax.shard_map(local, mesh=mesh, in_specs=in_specs, out_specs=out_specs, check_vma=False)
```

profile of v0, /device:TPU:103, one launch (start us, length us, event | category | flops | bytes accessed | tf_op | source)
XLA Modules:
  0.0 541.2 jit_solution(13627637778979994432)
XLA Ops:
  6.5 0.0 all-reduce.3.cloned.1.call-start
  6.5 60.5 %conditional.1 = (f32[1024,1024]{1,0:T(8,128)}) conditional(s32[]{:T(128)} %convert_element_type.20, () %tuple.15, (s32[]{:T(128)}, f32[2048,1024]{1,0:T(8,128)}, s32[]{:T(128)}, s32[]{:T(128)}) %tuple.19), branch_computations={%region_0.1_spmd, %region_1.2_spmd.clone} | conditional | flops 25790779392 | bytes 46166128 | solution.py:109
  6.5 4.8 constant_dynamic-slice_fusion
  11.3 17.6 %gather_fusion = f32[1024]{0:T(1024)S(1)} fusion(f32[1024,1024]{1,0:T(8,128)} %constant_dynamic-slice_fusion, s32[1024]{0:T(1024)S(1)} %bitcast.7), kind=kCustom, calls=%fused_computation | custom fusion | bytes 16384 | tf_op jit(solution)/shard_map/cond/branch_1_fun/jit(diagonal)/cond/branch_0_fun/gather | solution.py:33
  28.9 0.0 copy-start.2
  29.0 20.7 %fusion.12 = f32[1024,1024]{1,0:T(8,128)S(1)} fusion(f32[1024,1024]{1,0:T(8,128)} %constant_dynamic-slice_fusion, f32[1024]{0:T(1024)S(1)} %gather_fusion), kind=kOutput, calls=%fused_computation.19 | convolution fusion | flops 12893290496 | bytes 8392704 | tf_op jit(solution)/shard_map/cond/branch_1_fun/dot_general | solution.py:43
  49.7 0.0 copy-done.2
  49.7 16.8 %fusion.2 = f32[1024,1024]{1,0:T(8,128)} fusion(f32[1024,1024]{1,0:T(8,128)S(1)} %fusion.12, f32[1024,1024]{1,0:T(8,128)S(1)} %copy-done.2, f32[1024]{0:T(1024)S(1)} %gather_fusion), kind=kOutput, calls=%fused_computation.6 | convolution fusion | flops 12897484800 | bytes 12587008 | tf_op jit(solution)/shard_map/cond/branch_1_fun/dot_general | solution.py:46
  67.0 5.0 broadcast_select_fusion
  72.1 0.0 all-reduce.3.cloned.1.call-update
  72.1 0.0 all-reduce.5.cloned.1.call-start
  72.1 108.4 %all-reduce.3.cloned.1.call-done = f32[1024,1024]{1,0:T(8,128)} async-done(((f32[1024,1024]{1,0:T(8,128)}), f32[1024,1024]{1,0:T(8,128)}) %all-reduce.3.cloned.1.call-update) | async-done | bytes 4194320 | tf_op jit(solution)/shard_map/psum | solution.py:11
  180.6 5.4 copy.3
  185.9 7.1 %broadcast_multiply_fusion = f32[2,1024,1024]{1,2,0:T(8,128)} fusion(f32[1024,1024]{0,1:T(8,128)} %copy.3, f32[2]{0:T(128)S(1)} %compare_convert_fusion), kind=kLoop, calls=%fused_computation.22 | loop fusion | flops 2097152 | bytes 12582920 | tf_op jit(solution)/shard_map/mul | solution.py:113
  193.0 0.0 all-reduce.5.cloned.1.call-update
  193.1 143.8 %all-reduce.5.cloned.1.call-done = f32[2,1024,1024]{1,2,0:T(8,128)} async-done(((f32[2,1024,1024]{1,2,0:T(8,128)}), f32[2,1024,1024]{1,2,0:T(8,128)}) %all-reduce.5.cloned.1.call-update) | async-done | bytes 8388624 | tf_op jit(solution)/shard_map/psum | solution.py:114
  336.9 0.0 copy-start.3
  336.9 29.9 %fusion.13 = f32[2,1024,1024]{2,1,0:T(8,128)S(1)} fusion(f32[2,1024,1024]{1,2,0:T(8,128)} %all-reduce.5.cloned.1.call-done, f32[2,1024,1024]{2,1,0:T(8,128)} %bitcast.8), kind=kOutput, calls=%fused_computation.33 | convolution fusion | flops 25769803776 | bytes 25165824 | tf_op jit(solution)/shard_map/sji,sjk->sik/dot_general | solution.py:116
  366.8 0.0 copy-done.3
  366.8 28.0 %fusion.14 = f32[2048,1024]{1,0:T(8,128)S(1)} fusion(f32[2048,1024]{1,0:T(8,128)S(1)} %bitcast.9, f32[1024,1024]{1,0:T(8,128)S(1)} %copy-done.3), kind=kOutput, calls=%fused_computation.34 | convolution fusion | flops 25769803776 | bytes 20971520 | tf_op jit(solution)/shard_map/dot_general | solution.py:117
  394.8 0.0 copy-start.1
  394.8 2.5 slice_select_fusion.4
  397.3 1.5 copy-done.1
  398.8 4.6 collective-permute-start
  403.5 1.9 collective-permute-start.1
  405.4 41.2 %collective-permute-done = f32[512,1024]{1,0:T(8,128)} collective-permute-done((f32[512,1024]{1,0:T(8,128)}, f32[512,1024]{1,0:T(8,128)}, u32[]{:S(2)}, u32[]{:S(2)}) %collective-permute-start) | collective-permute-done | bytes 2097184 | tf_op jit(solution)/shard_map/ppermute | solution.py:22
  446.6 7.5 %collective-permute-done.1 = f32[512,1024]{1,0:T(8,128)} collective-permute-done((f32[512,1024]{1,0:T(8,128)S(1)}, f32[512,1024]{1,0:T(8,128)}, u32[]{:S(2)}, u32[]{:S(2)}) %collective-permute-start.1) | collective-permute-done | bytes 2097184 | tf_op jit(solution)/shard_map/ppermute | solution.py:24
  454.2 6.2 %slice_select_fusion.7 = (f32[512,1024]{1,0:T(8,128)S(1)}, f32[512,1024]{1,0:T(8,128)S(1)}, f32[512,1024]{1,0:T(8,128)S(1)}, f32[512,1024]{1,0:T(8,128)S(1)}) fusion(f32[512,1024]{1,0:T(8,128)} %collective-permute-done, f32[2048,1024]{1,0:T(8,128)} %copy-done.1, pred[]{:T(512)S(6)} %eq.47, pred[]{:T(512)S(6)} %eq.53, f32[512,1024]{1,0:T(8,128)} %collective-permute-done.1, ...), kind=kLoop, calls=%fused_computation.31 | loop fusion | flops 2097152 | bytes 20971524 | tf_op jit(solution)/shard_map/jit(_where)/select_n | solution.py:79
  460.3 1.8 pad_maximum_fusion
  462.1 0.0 copy-start
  462.1 4.7 slice_select_fusion.2
  466.8 1.2 copy-done
  468.0 3.0 collective-permute-start.2
  471.1 2.1 collective-permute-start.3
  473.2 43.6 %collective-permute-done.2 = f32[2048,512]{1,0:T(8,128)} collective-permute-done((f32[2048,512]{1,0:T(8,128)}, f32[2048,512]{1,0:T(8,128)}, u32[]{:S(2)}, u32[]{:S(2)}) %collective-permute-start.2) | collective-permute-done | bytes 4194336 | tf_op jit(solution)/shard_map/ppermute | solution.py:22
  516.8 6.5 %collective-permute-done.3 = f32[2048,512]{1,0:T(8,128)} collective-permute-done((f32[2048,512]{1,0:T(8,128)}, f32[2048,512]{1,0:T(8,128)}, u32[]{:S(2)}, u32[]{:S(2)}) %collective-permute-start.3) | collective-permute-done | bytes 4194336 | tf_op jit(solution)/shard_map/ppermute | solution.py:24
  523.3 6.2 %slice_select_fusion.1 = (f32[2048,512]{1,0:T(8,128)S(1)}, f32[2048,512]{1,0:T(8,128)S(1)}) fusion(f32[2048,512]{1,0:T(8,128)} %collective-permute-done.2, f32[2048,1024]{1,0:T(8,128)} %copy-done, pred[]{:T(512)S(6)} %eq.46, f32[2048,512]{1,0:T(8,128)} %collective-permute-done.3, pred[]{:T(512)S(6)} %eq.55), kind=kLoop, calls=%fused_computation.24 | loop fusion | flops 2097152 | bytes 20971522 | tf_op jit(solution)/shard_map/jit(_where)/select_n | solution.py:79
  529.5 4.6 pad_maximum_fusion.1
  (2 shorter events, 0.0 us)
Async XLA Ops:
  6.5 174.0 %all-reduce.3.cloned.1.call-start = ((), (), s32[]{:S(2)}) async-start(), calls=%async_computation | async-start | bytes 8388608 | tf_op jit(solution)/shard_map/psum | solution.py:11
  28.9 20.8 %copy-start.2 = (f32[1024,1024]{1,0:T(8,128)S(1)}, f32[1024,1024]{1,0:T(8,128)}, u32[]{:S(2)}) copy-start(f32[1024,1024]{1,0:T(8,128)} %constant_dynamic-slice_fusion) | copy-start | bytes 12582916 | tf_op jit(solution)/shard_map/cond
  72.1 264.8 %all-reduce.5.cloned.1.call-start = ((), (), s32[]{:S(2)}) async-start(), calls=%async_computation.1 | async-start | bytes 16777216 | tf_op jit(solution)/shard_map/psum | solution.py:114
  336.9 29.9 %copy-start.3 = (f32[1024,1024]{1,0:T(8,128)S(1)}, f32[1024,1024]{1,0:T(8,128)}, u32[]{:S(2)}) copy-start(f32[1024,1024]{1,0:T(8,128)} %all-reduce.3.cloned.1.call-done) | copy-start | bytes 12582916
  394.8 4.0 copy-start.1
  398.8 47.8 %collective-permute-start = (f32[512,1024]{1,0:T(8,128)}, f32[512,1024]{1,0:T(8,128)}, u32[]{:S(2)}, u32[]{:S(2)}) collective-permute-start(f32[512,1024]{1,0:T(8,128)} %get-tuple-element.56), channel_id=1, source_target_pairs={{0,16},{16,32},{32,48},{48,64},{64,80},{80,96},{96,112},{1,17},{17... | collective-permute-start | bytes 6291464 | tf_op jit(solution)/shard_map/ppermute | solution.py:22
  403.5 50.7 %collective-permute-start.1 = (f32[512,1024]{1,0:T(8,128)S(1)}, f32[512,1024]{1,0:T(8,128)}, u32[]{:S(2)}, u32[]{:S(2)}) collective-permute-start(f32[512,1024]{1,0:T(8,128)S(1)} %get-tuple-element.57), channel_id=1, source_target_pairs={{16,0},{32,16},{48,32},{64,48},{80,64},{96,80},{112,96},{17,1},{33... | collective-permute-start | bytes 6291464 | tf_op jit(solution)/shard_map/ppermute | solution.py:24
  462.1 5.9 %copy-start = (f32[2048,1024]{1,0:T(8,128)}, f32[2048,1024]{1,0:T(8,128)S(1)}, u32[]{:S(2)}) copy-start(f32[2048,1024]{1,0:T(8,128)S(1)} %pad_maximum_fusion) | copy-start | bytes 25165828
  468.0 48.8 %collective-permute-start.2 = (f32[2048,512]{1,0:T(8,128)}, f32[2048,512]{1,0:T(8,128)}, u32[]{:S(2)}, u32[]{:S(2)}) collective-permute-start(f32[2048,512]{1,0:T(8,128)} %get-tuple-element.50), channel_id=1, source_target_pairs={{0,1},{1,2},{2,3},{3,4},{4,5},{5,6},{6,7},{7,8},{8,9},{9,10},{10,1... | collective-permute-start | bytes 12582920 | tf_op jit(solution)/shard_map/ppermute | solution.py:22
  471.1 52.2 %collective-permute-start.3 = (f32[2048,512]{1,0:T(8,128)}, f32[2048,512]{1,0:T(8,128)}, u32[]{:S(2)}, u32[]{:S(2)}) collective-permute-start(f32[2048,512]{1,0:T(8,128)} %get-tuple-element.51), channel_id=1, source_target_pairs={{1,0},{2,1},{3,2},{4,3},{5,4},{6,5},{7,6},{8,7},{9,8},{10,9},{11,1... | collective-permute-start | bytes 12582920 | tf_op jit(solution)/shard_map/ppermute | solution.py:24
Sparse Core Ops, SparseCore 0:
  72.2 108.3 all-reduce.2
  193.2 143.6 all-reduce.4
where the time goes:
time: 550 us; the launch traced here: 541 us
  waiting for transfers between devices  351 us (64%)
  matrix products  95.5 us (17%)
  other arithmetic  38.2 us (7%)
  local copies, waits for them, and re-layouts  30.4 us (6%)
  between operations  13.8 us (3%)
  starting transfers between devices  11.8 us (2%)
    psum x1, waiting for transfers between devices, local(): row_rotations = lax.psum(contribution, 'col')  144 us
    psum x1, waiting for transfers between devices, from_root(): return lax.psum(jnp.where(mine, shard, jnp.zeros_like(shard)), axis)  108 us
    ppermute x2, waiting for transfers between devices, with_halo(): lax.ppermute(tail, axis, [(i, (i + 1) % count) for i in range(ends)])  84.8 us
    dot_general x1, matrix products, local(): jnp.einsum('sji,sjk->sik', row_rotations, strips, precision=highest)  29.9 us
    dot_general x1, matrix products, local(): jnp.dot(left_done.reshape(local_slots * pair_width, pair_width), column_r...  28 us
    dot_general x1, matrix products, rotation_of(): jnp.dot(first_guess.T, first_guess, precision=highest, preferred_element_...  20.7 us
    gather x1, local copies, waits for them, and re-layouts, first_guess_of(): diagonal = jnp.diagonal(pair_block)  17.6 us
    dot_general x1, matrix products, rotation_of(): jnp.dot(first_guess, 1.5 * identity - 0.5 * correlation, precision=highes...  16.8 us
  transfers between devices with their start and end apart: 6, of which 6 were waited for; matrix products, arithmetic and copies ran while one was open for 0% of the time, Pallas kernels for 0%

commit v1 on v0

v1 whole, which is shorter than its diff:
```python
import functools

import jax
import jax.numpy as jnp
from jax import lax
from jax.experimental import pallas as pl
from jax.experimental.pallas import tpu as pltpu
from jax.sharding import PartitionSpec as P

f32, bf16, i32 = jnp.float32, jnp.bfloat16, jnp.int32
AXES = ("row", "col")
VMEM_LIMIT = 56 * 1024 * 1024


def cost(flops, nbytes):
    return pl.CostEstimate(flops=flops, bytes_accessed=nbytes, transcendentals=0)


def split(value):
    high = value.astype(bf16)
    return high, (value - high.astype(f32)).astype(bf16)


def dot(a, b):
    return jnp.dot(a, b, preferred_element_type=f32)


def dot3(a_high, a_low, b_high, b_low):
    return dot(a_high, b_high) + (dot(a_high, b_low) + dot(a_low, b_high))


def pack_kernel(info_ref, block_ref, packed_ref):
    width = block_ref.shape[0]
    half = width // 2
    rows = lax.broadcasted_iota(i32, (half, half), 0)
    cols = lax.broadcasted_iota(i32, (half, half), 1)
    on_diagonal = rows == cols
    top = block_ref[:half, :half]
    bottom = block_ref[half:, half:]
    top_only = jnp.where(on_diagonal, top, 0.0)
    bottom_only = jnp.where(on_diagonal, bottom, 0.0)
    top_down = jnp.sum(top_only, axis=1, keepdims=True)
    top_across = jnp.sum(top_only, axis=0, keepdims=True)
    bottom_down = jnp.sum(bottom_only, axis=1, keepdims=True)
    bottom_across = jnp.sum(bottom_only, axis=0, keepdims=True)
    above = rows < cols
    value = jnp.where(above, top, bottom)
    spacing = jnp.where(above, top_across - top_down, bottom_across - bottom_down)
    packed_ref[:, :half] = jnp.where(
        on_diagonal, 0.0, value / jnp.where(on_diagonal, 1.0, spacing)
    )
    packed_ref[:, half:] = block_ref[:half, half:] / (bottom_across - top_down)


def pack(info, matrix):
    width = matrix.shape[1]
    half = width // 2
    return pl.pallas_call(
        pack_kernel,
        out_shape=jax.ShapeDtypeStruct((half, width), f32),
        grid_spec=pltpu.PrefetchScalarGridSpec(
            num_scalar_prefetch=1,
            grid=(1,),
            in_specs=[pl.BlockSpec((width, width), lambda i, info: (info[0], 0))],
            out_specs=pl.BlockSpec((half, width), lambda i, info: (0, 0)),
        ),
        compiler_params=pltpu.CompilerParams(vmem_limit_bytes=VMEM_LIMIT),
        cost_estimate=cost(8 * width * width, 6 * width * width),
        name="pack",
    )(info, matrix)


def rotation_kernel(sign, place_ref, *refs):
    count = 8
    pieces = refs[:count]
    outs = refs[count:-5]
    packed, e_high, e_low, t_high, t_low = refs[-5:]
    depth, width = pieces[0].shape
    half = width // 2
    for k in range(count):
        packed[pl.ds(pl.multiple_of(place_ref[k] * depth, depth), depth), :] = pieces[k][...]
    rows = lax.broadcasted_iota(i32, (half, half), 0)
    cols = lax.broadcasted_iota(i32, (half, half), 1)
    triangles = packed[:, :half]
    flipped = -triangles.T
    corner = packed[:, half:]

    def put(r, c, value):
        if sign < 0:
            value = -value
        high, low = split(value)
        e_high[r * half : (r + 1) * half, c * half : (c + 1) * half] = high
        e_low[r * half : (r + 1) * half, c * half : (c + 1) * half] = low

    put(0, 0, jnp.where(rows < cols, triangles, flipped))
    put(1, 1, jnp.where(rows > cols, triangles, flipped))
    put(0, 1, corner)
    put(1, 0, -corner.T)
    tile = 256

    @pl.loop(0, width // tile)
    def _(n):
        at = pl.ds(pl.multiple_of(n * tile, tile), tile)
        square = dot3(e_high[...], e_low[...], e_high[:, at], e_low[:, at])
        high, low = split(0.5 * square)
        t_high[:, at] = high
        t_low[:, at] = low

    @pl.loop(0, width // tile)
    def _(n):
        at = pl.ds(pl.multiple_of(n * tile, tile), tile)
        cube = dot3(e_high[...], e_low[...], t_high[:, at], t_low[:, at])
        here = lax.broadcasted_iota(i32, (width, tile), 0)
        there = lax.broadcasted_iota(i32, (width, tile), 1) + n * tile
        total = cube + (t_high[:, at].astype(f32) + t_low[:, at].astype(f32))
        total = total + (e_high[:, at].astype(f32) + e_low[:, at].astype(f32))
        total = total + jnp.where(here == there, 1.0, 0.0)
        if len(outs) == 1:
            outs[0][:, at] = total
        else:
            high, low = split(total)
            outs[0][:, at] = high
            outs[1][:, at] = low


def rotation(place, pieces, sign, in_parts, name):
    depth, width = pieces[0].shape
    square = (width, width)
    if in_parts:
        shapes = [jax.ShapeDtypeStruct(square, bf16)] * 2
    else:
        shapes = [jax.ShapeDtypeStruct(square, f32)]
    return pl.pallas_call(
        functools.partial(rotation_kernel, sign),
        out_shape=shapes,
        in_specs=[pl.BlockSpec(memory_space=pltpu.SMEM)]
        + [pl.BlockSpec(memory_space=pltpu.VMEM)] * len(pieces),
        out_specs=[pl.BlockSpec(memory_space=pltpu.VMEM)] * len(shapes),
        scratch_shapes=[pltpu.VMEM((width // 2, width), f32)] + [pltpu.VMEM(square, bf16)] * 4,
        compiler_params=pltpu.CompilerParams(vmem_limit_bytes=VMEM_LIMIT),
        cost_estimate=cost(12 * width**3, 6 * width * width),
        name=name,
    )(place, *pieces)


def right_kernel(info_ref, m_ref, high_ref, low_ref, out_ref):
    m_high, m_low = split(m_ref[...])
    out_ref[...] = dot3(m_high, m_low, high_ref[...], low_ref[...])


def right(info, matrix, r_high, r_low, name):
    width = matrix.shape[1]
    half = width // 2
    tile = 256
    per_slot = width // tile
    return pl.pallas_call(
        right_kernel,
        out_shape=jax.ShapeDtypeStruct((width, half), f32),
        grid_spec=pltpu.PrefetchScalarGridSpec(
            num_scalar_prefetch=1,
            grid=(per_slot,),
            in_specs=[
                pl.BlockSpec((tile, width), lambda i, info: (info[0] * per_slot + i, 0)),
                pl.BlockSpec((width, half), lambda i, info: (0, info[1])),
                pl.BlockSpec((width, half), lambda i, info: (0, info[1])),
            ],
            out_specs=pl.BlockSpec((tile, half), lambda i, info: (i, 0)),
        ),
        compiler_params=pltpu.CompilerParams(vmem_limit_bytes=VMEM_LIMIT),
        cost_estimate=cost(3 * width**3, 8 * width * width),
        name=name,
    )(info, matrix, r_high, r_low)


def left_kernel(info_ref, *refs):
    turned_ref, part_ref = refs[:2]
    moved_ref, kept_ref, part_high, part_low = refs[-4:]
    step = pl.program_id(0)
    steps = pl.num_programs(0)

    @pl.when(step == 0)
    def _():
        high, low = split(part_ref[...])
        part_high[...] = high
        part_low[...] = low

    t_high, t_low = split(turned_ref[...])
    value = dot3(t_high, t_low, part_high[...], part_low[...])

    @pl.when(step < steps // 2)
    def _():
        moved_ref[...] = value

    @pl.when(step >= steps // 2)
    def _():
        kept_ref[...] = value


def left(info, turned, part, result, out_rows, name):
    width = turned.shape[0]
    half = width // 2
    tile = 256
    per_half = half // tile
    out_shape = jax.ShapeDtypeStruct((out_rows, width), f32)

    def row_tile(i, info):
        which = jnp.where(i < per_half, info[0], 1 - info[0])
        return (which * per_half + lax.rem(i, per_half), 0)

    operands = [turned, part]
    in_specs = [
        pl.BlockSpec((tile, width), row_tile),
        pl.BlockSpec((width, half), lambda i, info: (0, 0)),
    ]
    aliases = {}
    if result is not None:
        operands.append(result)
        in_specs.append(pl.BlockSpec(memory_space=pl.ANY))
        aliases = {3: 1}
    return pl.pallas_call(
        left_kernel,
        out_shape=[jax.ShapeDtypeStruct((half, half), f32), out_shape],
        grid_spec=pltpu.PrefetchScalarGridSpec(
            num_scalar_prefetch=1,
            grid=(2 * per_half,),
            in_specs=in_specs,
            out_specs=[
                pl.BlockSpec((tile, half), lambda i, info: (jnp.minimum(i, per_half - 1), 0)),
                pl.BlockSpec(
                    (tile, half),
                    lambda i, info: (info[1] * per_half + jnp.maximum(i - per_half, 0), info[2]),
                ),
            ],
            scratch_shapes=[pltpu.VMEM((width, half), bf16)] * 2,
        ),
        input_output_aliases=aliases,
        compiler_params=pltpu.CompilerParams(vmem_limit_bytes=VMEM_LIMIT),
        cost_estimate=cost(3 * width**3, 10 * width * width),
        name=name,
    )(info, *operands)


def land_kernel(info_ref, arrived_ref, own_ref, result_ref, out_ref):
    out_ref[...] = jnp.where(info_ref[2] > 0, own_ref[...], arrived_ref[...])


def land(info, arrived, own, result, name):
    half = arrived.shape[0]
    tile = 256
    per_half = half // tile
    part = pl.BlockSpec((tile, half), lambda i, info: (i, 0))
    return pl.pallas_call(
        land_kernel,
        out_shape=jax.ShapeDtypeStruct(result.shape, f32),
        grid_spec=pltpu.PrefetchScalarGridSpec(
            num_scalar_prefetch=1,
            grid=(per_half,),
            in_specs=[part, part, pl.BlockSpec(memory_space=pl.ANY)],
            out_specs=pl.BlockSpec(
                (tile, half), lambda i, info: (info[0] * per_half + i, info[1])
            ),
        ),
        input_output_aliases={3: 0},
        compiler_params=pltpu.CompilerParams(vmem_limit_bytes=VMEM_LIMIT),
        cost_estimate=cost(half * half, 12 * half * half),
        name=name,
    )(info, arrived, own, result)


OFFSETS = [(1, 0), (3, 0), (2, 0), (0, 1), (1, 1), (3, 1), (2, 1)]


def shifted(member, offset):
    ring, plane = offset
    return (member // 4 ^ plane) * 4 + (member + ring) % 4


def group_pairs(group, offset, only_source):
    pairs = []
    for row in range(8):
        for col in range(16):
            chip, core = col // 2, col % 2
            if only_source and row != chip:
                continue
            if group == "row":
                target = (shifted(row, offset), col)
            else:
                target = (row, 2 * shifted(chip, offset) + core)
            pairs.append((row * 16 + col, target[0] * 16 + target[1]))
    return pairs


def spread(packed, group, member, is_source):
    depth = packed.shape[0] // 8

    def piece(at):
        return lax.dynamic_slice_in_dim(packed, at * depth, depth, 0)

    arrived = [
        lax.ppermute(piece(shifted(member, offset)), AXES, group_pairs(group, offset, True))
        for offset in OFFSETS
    ]
    own = jnp.where(is_source, piece(member), sum(arrived[1:], arrived[0]))
    pieces = [own]
    places = [member]
    for ring, plane in OFFSETS:
        pieces.append(lax.ppermute(own, AXES, group_pairs(group, (ring, plane), False)))
        places.append(shifted(member, (4 - ring, plane)))
    return pieces, jnp.stack(places).astype(i32)


def local(matrix):
    row = lax.axis_index("row")
    col = lax.axis_index("col")
    chip = col // 2
    core = col % 2
    is_source = row == chip
    rows_here = matrix.shape[0]

    def scalars(*values):
        return jnp.stack([jnp.asarray(v, i32) for v in values])

    packed = pack(scalars(core), matrix)
    col_pieces, col_places = spread(packed, "row", row, is_source)
    row_pieces, row_places = spread(packed, "col", chip, is_source)

    r_high, r_low = rotation(col_places, col_pieces, 1, True, "column_rotation")
    near_half = jnp.where((core == 1) | (col == 0), 1, 0)
    swap = [(i, i ^ 1) for i in range(16)]
    chips = [(0, 0), (15, 15)]
    chips += [(i, i - 1) for i in range(2, 16, 2)] + [(i, i + 1) for i in range(1, 15, 2)]
    first, second = 1 - core, core
    at_end = (col == 0) | (col == 15)
    end_first, end_second = jnp.where(at_end, core, first), jnp.where(at_end, first, core)
    far_first = right(scalars(end_first, 1 - near_half), matrix, r_high, r_low, "right_far_first")
    far_first = lax.ppermute(far_first, "col", chips)
    near_first = right(scalars(first, near_half), matrix, r_high, r_low, "right_near_first")
    near_first = lax.ppermute(near_first, "col", swap)
    near_second = right(scalars(second, near_half), matrix, r_high, r_low, "right_near_second")
    near_second = lax.ppermute(near_second, "col", swap)
    far_second = right(scalars(end_second, 1 - near_half), matrix, r_high, r_low, "right_far_second")
    far_second = lax.ppermute(far_second, "col", chips)

    (turned,) = rotation(row_places, row_pieces, -1, False, "row_rotation")
    other_turned = lax.ppermute(turned, "col", swap)

    def out_half(slot):
        return jnp.where(slot == 0, jnp.where(row == 0, 0, 1), 0)

    near_block, far_block = 1 - core, core
    kept_row_first = jnp.where(core == 0, 2, 1)
    kept_row_second = jnp.where(core == 0, 1, 2)
    land_row_first = jnp.where(core == 0, 3, 0)
    land_row_second = jnp.where(core == 0, 0, 3)
    end_first = jnp.where(core == 0, row == 7, row == 0)
    end_second = jnp.where(core == 0, row == 0, row == 7)

    def row_pairs(down_core):
        pairs = []
        for r in range(8):
            for c in range(16):
                target = r - 1 if c % 2 == down_core else r + 1
                if 0 <= target < 8:
                    pairs.append((r * 16 + c, target * 16 + c))
        return pairs

    result = None
    parts = {}
    for place, part, block in (
        ("near", (near_first, near_second), near_block),
        ("far", (far_first, far_second), far_block),
    ):
        for order in range(2):
            slot = (core, 1 - core)[order]
            kept_row = (kept_row_first, kept_row_second)[order]
            moved, result = left(
                scalars(out_half(slot), kept_row, block),
                (turned, other_turned)[order],
                part[order],
                result,
                rows_here,
                "left_%s_%d" % (place, order),
            )
            arrived = lax.ppermute(moved, AXES, row_pairs(order))
            parts[place, order] = moved, arrived
    for place, block in (("near", near_block), ("far", far_block)):
        for order in range(2):
            end = (end_first, end_second)[order]
            land_row = (land_row_first, land_row_second)[order]
            result = land(
                scalars(land_row, block, end),
                parts[place, order][1],
                parts[place, 1 - order][0],
                result,
                "land_%s_%d" % (place, order),
            )
    return result


def solution(mesh):
    return jax.shard_map(
        local, mesh=mesh, in_specs=(P("row", "col"),), out_specs=P("row", "col"), check_vma=False
    )
```

time: 550 us -> 315 us (0.57)
  the two profiles are of different devices: /device:TPU:103 before, /device:TPU:8 now
where the time goes in v1:
time: 315 us; the launch traced here: 311 us
  Pallas kernels  120 us (38%)
  waiting for transfers between devices  89 us (28%)
  starting transfers between devices  80.9 us (26%)
  other arithmetic  10.6 us (3%)
  local copies, waits for them, and re-layouts  9.8 us (3%)
    ppermute x14, starting transfers between devices, spread(): lax.ppermute(own, AXES, group_pairs(group, (ring, plane), False))  48.2 us
    ppermute x1, waiting for transfers between devices, local(): far_second = lax.ppermute(far_second, 'col', chips)  44.3 us
    pallas_call x2, Pallas kernels, rotation(): pl.pallas_call(functools.partial(rotation_kernel, sign), out_shape=shapes...  39.1 us
    ppermute x14, waiting for transfers between devices, spread(): lax.ppermute(piece(shifted(member, offset)), AXES, group_pairs(group, off...  35.5 us
    pallas_call x4, Pallas kernels, left(): pl.pallas_call(left_kernel, out_shape=[jax.ShapeDtypeStruct((half, half),...  33.6 us
    pallas_call x4, Pallas kernels, right(): pl.pallas_call(right_kernel, out_shape=jax.ShapeDtypeStruct((width, half)...  31.4 us
    ppermute x14, starting transfers between devices, spread(): lax.ppermute(piece(shifted(member, offset)), AXES, group_pairs(group, off...  14.2 us
    pallas_call x4, Pallas kernels, land(): pl.pallas_call(land_kernel, out_shape=jax.ShapeDtypeStruct(result.shape,...  12.2 us
  transfers between devices with their start and end apart: 37, of which 9 were waited for; matrix products, arithmetic and copies ran while one was open for 3% of the time, Pallas kernels for 36%

profile of v1, /device:TPU:8, one launch (start us, length us, event | category | flops | bytes accessed | tf_op | source)
XLA Modules:
  0.0 310.8 jit_solution(15264725926922684648)
XLA Ops:
  0.0 3.9 %pack.1 = f32[512,1024]{1,0:T(8,128)} custom-call(s32[1]{0:T(128)} %bitcast.1.info_ref, f32[2048,1024]{1,0:T(8,128)} %m_ref.7), custom_call_target="tpu_custom_call" | custom-call | flops 8388608 | bytes 6291456 | tf_op jit(solution)/shard_map/pack/pallas_call | solution.py:58
  3.9 2.7 constant_dynamic-slice_fusion.5
  6.6 0.7 collective-permute-start.16
  7.3 0.7 collective-permute-start.21
  7.9 0.7 collective-permute-start.20
  8.6 0.7 collective-permute-start.19
  9.3 1.3 collective-permute-start.18
  10.6 1.4 collective-permute-start.17
  12.0 1.4 collective-permute-start.15
  13.4 11.9 %collective-permute-done.18 = f32[64,1024]{1,0:T(8,128)S(1)} collective-permute-done((f32[64,1024]{1,0:T(8,128)}, f32[64,1024]{1,0:T(8,128)S(1)}, u32[]{:S(2)}, u32[]{:S(2)}) %collective-permute-start.18) | collective-permute-done | bytes 262176 | tf_op jit(solution)/shard_map/ppermute | solution.py:300
  25.3 0.7 copy-done.5
  26.0 2.3 add_select_fusion
  28.3 0.7 collective-permute-start.6
  29.0 0.7 collective-permute-start.5
  29.7 0.7 collective-permute-start.4
  30.4 1.3 collective-permute-start.3
  31.7 1.4 collective-permute-start.2
  33.1 1.4 collective-permute-start.1
  34.4 1.4 collective-permute-start
  35.8 9.9 %collective-permute-start.28 = (f32[64,1024]{1,0:T(8,128)S(1)}, f32[64,1024]{1,0:T(8,128)S(1)}, u32[]{:S(2)}, u32[]{:S(2)}) collective-permute-start(f32[64,1024]{1,0:T(8,128)S(1)} %get-tuple-element.25.refs_0_), channel_id=1, source_target_pairs={{0,96},{1,97},{2,98},{3,99},{4,100},{5,101},{6,102},{7,103},{8,104... | collective-permute-start | bytes 786440 | tf_op jit(solution)/shard_map/ppermute | solution.py:307
  45.8 23.5 %collective-permute-done.3 = f32[64,1024]{1,0:T(8,128)S(1)} collective-permute-done((f32[64,1024]{1,0:T(8,128)}, f32[64,1024]{1,0:T(8,128)S(1)}, u32[]{:S(2)}, u32[]{:S(2)}) %collective-permute-start.3) | collective-permute-done | bytes 262176 | tf_op jit(solution)/shard_map/ppermute | solution.py:300
  69.3 5.8 %collective-permute-start.27 = (f32[64,1024]{1,0:T(8,128)S(1)}, f32[64,1024]{1,0:T(8,128)S(1)}, u32[]{:S(2)}, u32[]{:S(2)}) collective-permute-start(f32[64,1024]{1,0:T(8,128)S(1)} %get-tuple-element.25.refs_0_), channel_id=1, source_target_pairs={{0,112},{1,113},{2,114},{3,115},{4,116},{5,117},{6,118},{7,119},{8... | collective-permute-start | bytes 786440 | tf_op jit(solution)/shard_map/ppermute | solution.py:307
  75.1 1.3 add_select_fusion.1.refs_0_
  76.4 3.4 %collective-permute-start.13 = (f32[64,1024]{1,0:T(8,128)S(1)}, f32[64,1024]{1,0:T(8,128)S(1)}, u32[]{:S(2)}, u32[]{:S(2)}) collective-permute-start(f32[64,1024]{1,0:T(8,128)S(1)} %add_select_fusion.1.refs_0_), channel_id=1, source_target_pairs={{0,12},{1,13},{2,14},{3,15},{4,8},{5,9},{6,10},{7,11},{8,4},{9,5},... | collective-permute-start | bytes 786440 | tf_op jit(solution)/shard_map/ppermute | solution.py:307
  79.9 1.9 collective-permute-start.12
  81.7 1.1 collective-permute-start.11
  82.8 1.5 collective-permute-start.10
  84.8 3.5 %collective-permute-start.9 = (f32[64,1024]{1,0:T(8,128)S(1)}, f32[64,1024]{1,0:T(8,128)S(1)}, u32[]{:S(2)}, u32[]{:S(2)}) collective-permute-start(f32[64,1024]{1,0:T(8,128)S(1)} %add_select_fusion.1.refs_0_), channel_id=1, source_target_pairs={{0,4},{1,5},{2,6},{3,7},{4,0},{5,1},{6,2},{7,3},{8,12},{9,13},{10,... | collective-permute-start | bytes 786440 | tf_op jit(solution)/shard_map/ppermute | solution.py:307
  88.3 3.4 %collective-permute-done.13.refs_7_ = f32[64,1024]{1,0:T(8,128)S(1)} collective-permute-done((f32[64,1024]{1,0:T(8,128)S(1)}, f32[64,1024]{1,0:T(8,128)S(1)}, u32[]{:S(2)}, u32[]{:S(2)}) %collective-permute-start.13) | collective-permute-done | bytes 262176 | tf_op jit(solution)/shard_map/ppermute | solution.py:307
  91.7 1.9 collective-permute-start.8
  93.6 1.9 collective-permute-done.12.refs_6_
  95.5 2.8 collective-permute-start.7
  98.4 0.7 stack.173.place_ref
  99.1 0.7 stack.185.place_ref
  100.3 2.6 collective-permute-done.11.refs_5_
  102.9 3.4 %collective-permute-start.26 = (f32[64,1024]{1,0:T(8,128)S(1)}, f32[64,1024]{1,0:T(8,128)S(1)}, u32[]{:S(2)}, u32[]{:S(2)}) collective-permute-start(f32[64,1024]{1,0:T(8,128)S(1)} %get-tuple-element.25.refs_0_), channel_id=1, source_target_pairs={{0,80},{1,81},{2,82},{3,83},{4,84},{5,85},{6,86},{7,87},{8,88},{9,... | collective-permute-start | bytes 786440 | tf_op jit(solution)/shard_map/ppermute | solution.py:307
  106.7 2.5 collective-permute-start.25
  109.2 8.3 %collective-permute-start.24 = (f32[64,1024]{1,0:T(8,128)S(1)}, f32[64,1024]{1,0:T(8,128)S(1)}, u32[]{:S(2)}, u32[]{:S(2)}) collective-permute-start(f32[64,1024]{1,0:T(8,128)S(1)} %get-tuple-element.25.refs_0_), channel_id=1, source_target_pairs={{0,32},{1,33},{2,34},{3,35},{4,36},{5,37},{6,38},{7,39},{8,40},{9,... | collective-permute-start | bytes 786440 | tf_op jit(solution)/shard_map/ppermute | solution.py:307
  117.5 1.4 collective-permute-start.23
  119.7 19.3 %row_rotation.1.refs_0_ = f32[1024,1024]{1,0:T(8,128)} custom-call(s32[8]{0:T(128)} %stack.173.place_ref, f32[64,1024]{1,0:T(8,128)} %copy-done.6, f32[64,1024]{1,0:T(8,128)} %copy-done.16, f32[64,1024]{1,0:T(8,128)} %copy-done.15, f32[64,1024]{1,0:T(8,128)} %copy-done.14, f32[64,1024]{1,0:T(8,128)} %copy-done.13, f32[64,1024]{1,0:T(8,128)} %copy-done.12, ...), custom_call_target="tpu_custom_call" | custom-call | flops 12884901888 | bytes 6291456 | tf_op jit(solution)/shard_map/row_rotation/pallas_call | solution.py:133
  141.4 0.7 copy-done.21
  142.2 19.8 %column_rotation.1 = (bf16[1024,1024]{1,0:T(8,128)(2,1)}, bf16[1024,1024]{1,0:T(8,128)(2,1)}) custom-call(s32[8]{0:T(128)} %stack.185.place_ref, f32[64,1024]{1,0:T(8,128)} %copy-done.4, f32[64,1024]{1,0:T(8,128)} %copy-done.21, f32[64,1024]{1,0:T(8,128)} %copy-done.20, f32[64,1024]{1,0:T(8,128)} %copy-done.19, f32[64,1024]{1,0:T(8,128)} %copy-done.18, ...), custom_call_target="tpu_custom_call" | custom-call | flops 12884901888 | bytes 6291456 | tf_op jit(solution)/shard_map/column_rotation/pallas_call | solution.py:133
  161.9 7.9 %right_near_first.1 = f32[1024,512]{1,0:T(8,128)} custom-call(s32[2]{0:T(128)} %pad_add_fusion.5.info_ref, f32[2048,1024]{1,0:T(8,128)} %m_ref.7, bf16[1024,1024]{1,0:T(8,128)(2,1)} %get-tuple-element.15.high_ref, bf16[1024,1024]{1,0:T(8,128)(2,1)} %get-tuple-element.16.low_ref), custom_call_target="tpu_custom_call" | custom-call | flops 3221225472 | bytes 8388608 | tf_op jit(solution)/shard_map/right_near_first/pallas_call | solution.py:156
  170.3 7.8 %right_near_second.1 = f32[1024,512]{1,0:T(8,128)} custom-call(s32[2]{0:T(128)} %pad_add_fusion.4.info_ref, f32[2048,1024]{1,0:T(8,128)} %m_ref.7, bf16[1024,1024]{1,0:T(8,128)(2,1)} %get-tuple-element.15.high_ref, bf16[1024,1024]{1,0:T(8,128)(2,1)} %get-tuple-element.16.low_ref), custom_call_target="tpu_custom_call" | custom-call | flops 3221225472 | bytes 8388608 | tf_op jit(solution)/shard_map/right_near_second/pallas_call | solution.py:156
  178.1 7.8 %right_far_first.1 = f32[1024,512]{1,0:T(8,128)} custom-call(s32[2]{0:T(128)} %pad_add_fusion.3.info_ref, f32[2048,1024]{1,0:T(8,128)} %m_ref.7, bf16[1024,1024]{1,0:T(8,128)(2,1)} %get-tuple-element.15.high_ref, bf16[1024,1024]{1,0:T(8,128)(2,1)} %get-tuple-element.16.low_ref), custom_call_target="tpu_custom_call" | custom-call | flops 3221225472 | bytes 8388608 | tf_op jit(solution)/shard_map/right_far_first/pallas_call | solution.py:156
  186.0 5.6 %collective-permute-start.30 = (f32[1024,512]{1,0:T(8,128)}, f32[1024,512]{1,0:T(8,128)}, u32[]{:S(2)}, u32[]{:S(2)}) collective-permute-start(f32[1024,512]{1,0:T(8,128)} %right_far_first.1), channel_id=1, source_target_pairs={{0,0},{15,15},{2,1},{4,3},{6,5},{8,7},{10,9},{12,11},{14,13},{1,2}... | collective-permute-start | bytes 6291464 | tf_op jit(solution)/shard_map/ppermute | solution.py:336
  192.3 7.8 %right_far_second.1 = f32[1024,512]{1,0:T(8,128)} custom-call(s32[2]{0:T(128)} %pad_add_fusion.1.info_ref, f32[2048,1024]{1,0:T(8,128)} %m_ref.7, bf16[1024,1024]{1,0:T(8,128)(2,1)} %get-tuple-element.15.high_ref, bf16[1024,1024]{1,0:T(8,128)(2,1)} %get-tuple-element.16.low_ref), custom_call_target="tpu_custom_call" | custom-call | flops 3221225472 | bytes 8388608 | tf_op jit(solution)/shard_map/right_far_second/pallas_call | solution.py:156
  200.1 2.0 collective-permute-start.29
  204.7 8.4 %left_near_0.1 = (f32[512,512]{1,0:T(8,128)}, f32[2048,1024]{1,0:T(8,128)}) custom-call(s32[3]{0:T(128)} %pad_add_fusion.8.info_ref, f32[1024,1024]{1,0:T(8,128)} %row_rotation.1.refs_0_, f32[1024,512]{1,0:T(8,128)} %collective-permute-done.32.refs_1_), custom_call_target="tpu_custom_call" | custom-call | flops 3221225472 | bytes 10485760 | tf_op jit(solution)/shard_map/left_near_0/pallas_call | solution.py:220
  213.1 1.3 collective-permute-start.36
  214.4 8.4 %left_near_1.1 = (f32[512,512]{1,0:T(8,128)}, f32[2048,1024]{1,0:T(8,128)}) custom-call(s32[3]{0:T(128)} %pad_add_fusion.9.info_ref, f32[1024,1024]{1,0:T(8,128)} %collective-permute-done.14.refs_0_, f32[1024,512]{1,0:T(8,128)} %collective-permute-done.31.refs_1_, f32[2048,1024]{1,0:T(8,128)} %get-tuple-element.17.refs_2_), custom_call_target="tpu_custom_call", output_to_operand_aliasing={{1}: (3, {})} | custom-call | flops 3221225472 | bytes 10485760 | tf_op jit(solution)/shard_map/left_near_1/pallas_call | solution.py:220
  222.9 8.4 %left_far_0.1 = (f32[512,512]{1,0:T(8,128)}, f32[2048,1024]{1,0:T(8,128)}) custom-call(s32[3]{0:T(128)} %pad_add_fusion.6.info_ref, f32[1024,1024]{1,0:T(8,128)} %row_rotation.1.refs_0_, f32[1024,512]{1,0:T(8,128)} %collective-permute-done.30.refs_1_, f32[2048,1024]{1,0:T(8,128)} %get-tuple-element.18.refs_2_), custom_call_target="tpu_custom_call", output_to_operand_aliasing={{1}: (3, {})} | custom-call | flops 3221225472 | bytes 10485760 | tf_op jit(solution)/shard_map/left_far_0/pallas_call | solution.py:220
  231.3 1.3 collective-permute-start.34
  232.5 6.2 %collective-permute-start.35 = (f32[512,512]{1,0:T(8,128)}, f32[512,512]{1,0:T(8,128)}, u32[]{:S(2)}, u32[]{:S(2)}) collective-permute-start(f32[512,512]{1,0:T(8,128)} %get-tuple-element.22.own_ref), channel_id=1, source_target_pairs={{0,16},{2,18},{4,20},{6,22},{8,24},{10,26},{12,28},{14,30},{16,32}... | collective-permute-start | bytes 3145736 | tf_op jit(solution)/shard_map/ppermute | solution.py:384
  238.8 44.3 %collective-permute-done.29.refs_1_ = f32[1024,512]{1,0:T(8,128)S(1)} collective-permute-done((f32[1024,512]{1,0:T(8,128)}, f32[1024,512]{1,0:T(8,128)S(1)}, u32[]{:S(2)}, u32[]{:S(2)}) %collective-permute-start.29) | collective-permute-done | bytes 2097184 | tf_op jit(solution)/shard_map/ppermute | solution.py:342
  283.1 1.3 copy-done.1
  284.4 8.4 %left_far_1.1 = (f32[512,512]{1,0:T(8,128)}, f32[2048,1024]{1,0:T(8,128)}) custom-call(s32[3]{0:T(128)} %pad_add_fusion.7.info_ref, f32[1024,1024]{1,0:T(8,128)} %collective-permute-done.14.refs_0_, f32[1024,512]{1,0:T(8,128)} %copy-done.1, f32[2048,1024]{1,0:T(8,128)} %get-tuple-element.19.refs_2_), custom_call_target="tpu_custom_call", output_to_operand_aliasing={{1}: (3, {})} | custom-call | flops 3221225472 | bytes 10485760 | tf_op jit(solution)/shard_map/left_far_1/pallas_call | solution.py:220
  292.8 1.3 collective-permute-start.33
  296.1 1.0 copy-done.2
  297.1 3.0 land_near_0.1.result_ref
  300.2 3.0 land_near_1.1.result_ref
  303.2 3.0 land_far_0.1.result_ref
  306.7 1.0 copy-done.3
  307.7 3.0 land_far_1.1
  (85 shorter events, 10.7 us)
Async XLA Ops:
  3.9 22.1 %copy-start = (f32[512,1024]{1,0:T(8,128)S(1)}, f32[512,1024]{1,0:T(8,128)}, u32[]{:S(2)}) copy-start(f32[512,1024]{1,0:T(8,128)} %pack.1) | copy-start | bytes 6291460
  6.6 4.0 %collective-permute-start.16 = (f32[64,1024]{1,0:T(8,128)S(1)}, f32[64,1024]{1,0:T(8,128)S(1)}, u32[]{:S(2)}, u32[]{:S(2)}) collective-permute-start(f32[64,1024]{1,0:T(8,128)S(1)} %get-tuple-element.33), channel_id=1, source_target_pairs={{0,48},{1,49},{18,2},{19,3},{36,20},{37,21},{54,38},{55,39},{72,12... | collective-permute-start | bytes 786440 | tf_op jit(solution)/shard_map/ppermute | solution.py:300
  7.3 4.7 %collective-permute-start.21 = (f32[64,1024]{1,0:T(8,128)S(1)}, f32[64,1024]{1,0:T(8,128)S(1)}, u32[]{:S(2)}, u32[]{:S(2)}) collective-permute-start(f32[64,1024]{1,0:T(8,128)S(1)} %get-tuple-element.34), channel_id=1, source_target_pairs={{0,96},{1,97},{18,114},{19,115},{36,68},{37,69},{54,86},{55,87},{7... | collective-permute-start | bytes 786440 | tf_op jit(solution)/shard_map/ppermute | solution.py:300
  7.9 5.4 %collective-permute-start.20 = (f32[64,1024]{1,0:T(8,128)}, f32[64,1024]{1,0:T(8,128)S(1)}, u32[]{:S(2)}, u32[]{:S(2)}) collective-permute-start(f32[64,1024]{1,0:T(8,128)} %get-tuple-element.35), channel_id=1, source_target_pairs={{0,112},{1,113},{18,66},{19,67},{36,84},{37,85},{54,102},{55,103},... | collective-permute-start | bytes 786440 | tf_op jit(solution)/shard_map/ppermute | solution.py:300
  8.6 4.7 %collective-permute-start.19 = (f32[64,1024]{1,0:T(8,128)}, f32[64,1024]{1,0:T(8,128)S(1)}, u32[]{:S(2)}, u32[]{:S(2)}) collective-permute-start(f32[64,1024]{1,0:T(8,128)} %get-tuple-element.36), channel_id=1, source_target_pairs={{0,80},{1,81},{18,98},{19,99},{36,116},{37,117},{54,70},{55,71},{7... | collective-permute-start | bytes 786440 | tf_op jit(solution)/shard_map/ppermute | solution.py:300
  9.3 16.0 %collective-permute-start.18 = (f32[64,1024]{1,0:T(8,128)}, f32[64,1024]{1,0:T(8,128)S(1)}, u32[]{:S(2)}, u32[]{:S(2)}) collective-permute-start(f32[64,1024]{1,0:T(8,128)} %get-tuple-element.37), channel_id=1, source_target_pairs={{0,64},{1,65},{18,82},{19,83},{36,100},{37,101},{54,118},{55,119},... | collective-permute-start | bytes 786440 | tf_op jit(solution)/shard_map/ppermute | solution.py:300
  10.6 14.7 %collective-permute-start.17 = (f32[64,1024]{1,0:T(8,128)}, f32[64,1024]{1,0:T(8,128)}, u32[]{:S(2)}, u32[]{:S(2)}) collective-permute-start(f32[64,1024]{1,0:T(8,128)} %get-tuple-element.38), channel_id=1, source_target_pairs={{0,32},{1,33},{18,50},{19,51},{36,4},{37,5},{54,22},{55,23},{72,10... | collective-permute-start | bytes 786440 | tf_op jit(solution)/shard_map/ppermute | solution.py:300
  12.0 14.0 %collective-permute-start.15 = (f32[64,1024]{1,0:T(8,128)}, f32[64,1024]{1,0:T(8,128)}, u32[]{:S(2)}, u32[]{:S(2)}) collective-permute-start(f32[64,1024]{1,0:T(8,128)} %get-tuple-element.39), channel_id=1, source_target_pairs={{0,16},{1,17},{18,34},{19,35},{36,52},{37,53},{54,6},{55,7},{72,88... | collective-permute-start | bytes 786440 | tf_op jit(solution)/shard_map/ppermute | solution.py:300
  25.3 0.7 copy-start.5
  28.3 110.7 %copy-start.4 = (f32[64,1024]{1,0:T(8,128)}, f32[64,1024]{1,0:T(8,128)S(1)}, u32[]{:S(2)}) copy-start(f32[64,1024]{1,0:T(8,128)S(1)} %get-tuple-element.25.refs_0_) | copy-start | bytes 786436
  28.3 4.7 %collective-permute-start.6 = (f32[64,1024]{1,0:T(8,128)S(1)}, f32[64,1024]{1,0:T(8,128)S(1)}, u32[]{:S(2)}, u32[]{:S(2)}) collective-permute-start(f32[64,1024]{1,0:T(8,128)S(1)} %get-tuple-element.26), channel_id=1, source_target_pairs={{0,12},{1,13},{18,30},{19,31},{36,40},{37,41},{54,58},{55,59},{72,... | collective-permute-start | bytes 786440 | tf_op jit(solution)/shard_map/ppermute | solution.py:300
  29.0 5.4 %collective-permute-start.5 = (f32[64,1024]{1,0:T(8,128)S(1)}, f32[64,1024]{1,0:T(8,128)S(1)}, u32[]{:S(2)}, u32[]{:S(2)}) collective-permute-start(f32[64,1024]{1,0:T(8,128)S(1)} %get-tuple-element.27), channel_id=1, source_target_pairs={{0,14},{1,15},{18,24},{19,25},{36,42},{37,43},{54,60},{55,61},{72,... | collective-permute-start | bytes 786440 | tf_op jit(solution)/shard_map/ppermute | solution.py:300
  29.7 6.1 %collective-permute-start.4 = (f32[64,1024]{1,0:T(8,128)}, f32[64,1024]{1,0:T(8,128)S(1)}, u32[]{:S(2)}, u32[]{:S(2)}) collective-permute-start(f32[64,1024]{1,0:T(8,128)} %get-tuple-element.28), channel_id=1, source_target_pairs={{0,10},{1,11},{18,28},{19,29},{36,46},{37,47},{54,56},{55,57},{72,... | collective-permute-start | bytes 786440 | tf_op jit(solution)/shard_map/ppermute | solution.py:300
  30.4 38.9 %collective-permute-start.3 = (f32[64,1024]{1,0:T(8,128)}, f32[64,1024]{1,0:T(8,128)S(1)}, u32[]{:S(2)}, u32[]{:S(2)}) collective-permute-start(f32[64,1024]{1,0:T(8,128)} %get-tuple-element.29), channel_id=1, source_target_pairs={{0,8},{1,9},{18,26},{19,27},{36,44},{37,45},{54,62},{55,63},{72,64... | collective-permute-start | bytes 786440 | tf_op jit(solution)/shard_map/ppermute | solution.py:300
  31.7 43.4 %collective-permute-start.2 = (f32[64,1024]{1,0:T(8,128)}, f32[64,1024]{1,0:T(8,128)}, u32[]{:S(2)}, u32[]{:S(2)}) collective-permute-start(f32[64,1024]{1,0:T(8,128)} %get-tuple-element.30), channel_id=1, source_target_pairs={{0,4},{1,5},{18,22},{19,23},{36,32},{37,33},{54,50},{55,51},{72,76... | collective-permute-start | bytes 786440 | tf_op jit(solution)/shard_map/ppermute | solution.py:300
  33.1 42.0 %collective-permute-start.1 = (f32[64,1024]{1,0:T(8,128)}, f32[64,1024]{1,0:T(8,128)}, u32[]{:S(2)}, u32[]{:S(2)}) collective-permute-start(f32[64,1024]{1,0:T(8,128)} %get-tuple-element.31), channel_id=1, source_target_pairs={{0,6},{1,7},{18,16},{19,17},{36,34},{37,35},{54,52},{55,53},{72,78... | collective-permute-start | bytes 786440 | tf_op jit(solution)/shard_map/ppermute | solution.py:300
  34.4 40.6 %collective-permute-start = (f32[64,1024]{1,0:T(8,128)}, f32[64,1024]{1,0:T(8,128)}, u32[]{:S(2)}, u32[]{:S(2)}) collective-permute-start(f32[64,1024]{1,0:T(8,128)} %get-tuple-element.32), channel_id=1, source_target_pairs={{0,2},{1,3},{18,20},{19,21},{36,38},{37,39},{54,48},{55,49},{72,74... | collective-permute-start | bytes 786440 | tf_op jit(solution)/shard_map/ppermute | solution.py:300
  35.8 47.0 %collective-permute-start.28 = (f32[64,1024]{1,0:T(8,128)S(1)}, f32[64,1024]{1,0:T(8,128)S(1)}, u32[]{:S(2)}, u32[]{:S(2)}) collective-permute-start(f32[64,1024]{1,0:T(8,128)S(1)} %get-tuple-element.25.refs_0_), channel_id=1, source_target_pairs={{0,96},{1,97},{2,98},{3,99},{4,100},{5,101},{6,102},{7,103},{8,104... | collective-permute-start | bytes 786440 | tf_op jit(solution)/shard_map/ppermute | solution.py:307
  69.3 5.8 %copy-start.7 = (f32[64,1024]{1,0:T(8,128)}, f32[64,1024]{1,0:T(8,128)S(1)}, u32[]{:S(2)}) copy-start(f32[64,1024]{1,0:T(8,128)S(1)} %collective-permute-done.3) | copy-start | bytes 786436
  69.3 15.5 %collective-permute-start.27 = (f32[64,1024]{1,0:T(8,128)S(1)}, f32[64,1024]{1,0:T(8,128)S(1)}, u32[]{:S(2)}, u32[]{:S(2)}) collective-permute-start(f32[64,1024]{1,0:T(8,128)S(1)} %get-tuple-element.25.refs_0_), channel_id=1, source_target_pairs={{0,112},{1,113},{2,114},{3,115},{4,116},{5,117},{6,118},{7,119},{8... | collective-permute-start | bytes 786440 | tf_op jit(solution)/shard_map/ppermute | solution.py:307
  76.4 43.1 %copy-start.6 = (f32[64,1024]{1,0:T(8,128)}, f32[64,1024]{1,0:T(8,128)S(1)}, u32[]{:S(2)}) copy-start(f32[64,1024]{1,0:T(8,128)S(1)} %add_select_fusion.1.refs_0_) | copy-start | bytes 786436
  76.4 15.2 %collective-permute-start.13 = (f32[64,1024]{1,0:T(8,128)S(1)}, f32[64,1024]{1,0:T(8,128)S(1)}, u32[]{:S(2)}, u32[]{:S(2)}) collective-permute-start(f32[64,1024]{1,0:T(8,128)S(1)} %add_select_fusion.1.refs_0_), channel_id=1, source_target_pairs={{0,12},{1,13},{2,14},{3,15},{4,8},{5,9},{6,10},{7,11},{8,4},{9,5},... | collective-permute-start | bytes 786440 | tf_op jit(solution)/shard_map/ppermute | solution.py:307
  79.9 15.7 %collective-permute-start.12 = (f32[64,1024]{1,0:T(8,128)S(1)}, f32[64,1024]{1,0:T(8,128)S(1)}, u32[]{:S(2)}, u32[]{:S(2)}) collective-permute-start(f32[64,1024]{1,0:T(8,128)S(1)} %add_select_fusion.1.refs_0_), channel_id=1, source_target_pairs={{0,14},{1,15},{2,8},{3,9},{4,10},{5,11},{6,12},{7,13},{8,6},{9,7},... | collective-permute-start | bytes 786440 | tf_op jit(solution)/shard_map/ppermute | solution.py:307
  81.7 21.2 %collective-permute-start.11 = (f32[64,1024]{1,0:T(8,128)S(1)}, f32[64,1024]{1,0:T(8,128)S(1)}, u32[]{:S(2)}, u32[]{:S(2)}) collective-permute-start(f32[64,1024]{1,0:T(8,128)S(1)} %add_select_fusion.1.refs_0_), channel_id=1, source_target_pairs={{0,10},{1,11},{2,12},{3,13},{4,14},{5,15},{6,8},{7,9},{8,2},{9,3},... | collective-permute-start | bytes 786440 | tf_op jit(solution)/shard_map/ppermute | solution.py:307
  82.8 12.7 %copy-start.8 = (f32[64,1024]{1,0:T(8,128)}, f32[64,1024]{1,0:T(8,128)S(1)}, u32[]{:S(2)}) copy-start(f32[64,1024]{1,0:T(8,128)S(1)} %collective-permute-done.28.refs_7_) | copy-start | bytes 786436
  82.8 23.9 %collective-permute-start.10 = (f32[64,1024]{1,0:T(8,128)S(1)}, f32[64,1024]{1,0:T(8,128)S(1)}, u32[]{:S(2)}, u32[]{:S(2)}) collective-permute-start(f32[64,1024]{1,0:T(8,128)S(1)} %add_select_fusion.1.refs_0_), channel_id=1, source_target_pairs={{0,8},{1,9},{2,10},{3,11},{4,12},{5,13},{6,14},{7,15},{8,0},{9,1},... | collective-permute-start | bytes 786440 | tf_op jit(solution)/shard_map/ppermute | solution.py:307
  84.8 10.7 %copy-start.9 = (f32[64,1024]{1,0:T(8,128)}, f32[64,1024]{1,0:T(8,128)S(1)}, u32[]{:S(2)}) copy-start(f32[64,1024]{1,0:T(8,128)S(1)} %collective-permute-done.27.refs_6_) | copy-start | bytes 786436
  84.8 24.4 %collective-permute-start.9 = (f32[64,1024]{1,0:T(8,128)S(1)}, f32[64,1024]{1,0:T(8,128)S(1)}, u32[]{:S(2)}, u32[]{:S(2)}) collective-permute-start(f32[64,1024]{1,0:T(8,128)S(1)} %add_select_fusion.1.refs_0_), channel_id=1, source_target_pairs={{0,4},{1,5},{2,6},{3,7},{4,0},{5,1},{6,2},{7,3},{8,12},{9,13},{10,... | collective-permute-start | bytes 786440 | tf_op jit(solution)/shard_map/ppermute | solution.py:307
  91.7 27.9 %copy-start.10 = (f32[64,1024]{1,0:T(8,128)}, f32[64,1024]{1,0:T(8,128)S(1)}, u32[]{:S(2)}) copy-start(f32[64,1024]{1,0:T(8,128)S(1)} %collective-permute-done.13.refs_7_) | copy-start | bytes 786436
  91.7 25.8 %collective-permute-start.8 = (f32[64,1024]{1,0:T(8,128)S(1)}, f32[64,1024]{1,0:T(8,128)S(1)}, u32[]{:S(2)}, u32[]{:S(2)}) collective-permute-start(f32[64,1024]{1,0:T(8,128)S(1)} %add_select_fusion.1.refs_0_), channel_id=1, source_target_pairs={{0,6},{1,7},{2,0},{3,1},{4,2},{5,3},{6,4},{7,5},{8,14},{9,15},{10,... | collective-permute-start | bytes 786440 | tf_op jit(solution)/shard_map/ppermute | solution.py:307
  95.5 24.0 %copy-start.11 = (f32[64,1024]{1,0:T(8,128)}, f32[64,1024]{1,0:T(8,128)S(1)}, u32[]{:S(2)}) copy-start(f32[64,1024]{1,0:T(8,128)S(1)} %collective-permute-done.12.refs_6_) | copy-start | bytes 786436
  95.5 23.4 %collective-permute-start.7 = (f32[64,1024]{1,0:T(8,128)S(1)}, f32[64,1024]{1,0:T(8,128)S(1)}, u32[]{:S(2)}, u32[]{:S(2)}) collective-permute-start(f32[64,1024]{1,0:T(8,128)S(1)} %add_select_fusion.1.refs_0_), channel_id=1, source_target_pairs={{0,2},{1,3},{2,4},{3,5},{4,6},{5,7},{6,0},{7,1},{8,10},{9,11},{10,... | collective-permute-start | bytes 786440 | tf_op jit(solution)/shard_map/ppermute | solution.py:307
  102.9 16.6 %copy-start.12 = (f32[64,1024]{1,0:T(8,128)}, f32[64,1024]{1,0:T(8,128)S(1)}, u32[]{:S(2)}) copy-start(f32[64,1024]{1,0:T(8,128)S(1)} %collective-permute-done.11.refs_5_) | copy-start | bytes 786436
  102.9 36.1 %collective-permute-start.26 = (f32[64,1024]{1,0:T(8,128)S(1)}, f32[64,1024]{1,0:T(8,128)S(1)}, u32[]{:S(2)}, u32[]{:S(2)}) collective-permute-start(f32[64,1024]{1,0:T(8,128)S(1)} %get-tuple-element.25.refs_0_), channel_id=1, source_target_pairs={{0,80},{1,81},{2,82},{3,83},{4,84},{5,85},{6,86},{7,87},{8,88},{9,... | collective-permute-start | bytes 786440 | tf_op jit(solution)/shard_map/ppermute | solution.py:307
  106.7 12.9 %copy-start.13 = (f32[64,1024]{1,0:T(8,128)}, f32[64,1024]{1,0:T(8,128)S(1)}, u32[]{:S(2)}) copy-start(f32[64,1024]{1,0:T(8,128)S(1)} %collective-permute-done.10.refs_4_) | copy-start | bytes 786436
  106.7 33.8 %collective-permute-start.25 = (f32[64,1024]{1,0:T(8,128)S(1)}, f32[64,1024]{1,0:T(8,128)S(1)}, u32[]{:S(2)}, u32[]{:S(2)}) collective-permute-start(f32[64,1024]{1,0:T(8,128)S(1)} %get-tuple-element.25.refs_0_), channel_id=1, source_target_pairs={{0,64},{1,65},{2,66},{3,67},{4,68},{5,69},{6,70},{7,71},{8,72},{9,... | collective-permute-start | bytes 786440 | tf_op jit(solution)/shard_map/ppermute | solution.py:307
  109.2 10.4 %copy-start.14 = (f32[64,1024]{1,0:T(8,128)}, f32[64,1024]{1,0:T(8,128)S(1)}, u32[]{:S(2)}) copy-start(f32[64,1024]{1,0:T(8,128)S(1)} %collective-permute-done.9.refs_3_) | copy-start | bytes 786436
  109.2 31.4 %collective-permute-start.24 = (f32[64,1024]{1,0:T(8,128)S(1)}, f32[64,1024]{1,0:T(8,128)S(1)}, u32[]{:S(2)}, u32[]{:S(2)}) collective-permute-start(f32[64,1024]{1,0:T(8,128)S(1)} %get-tuple-element.25.refs_0_), channel_id=1, source_target_pairs={{0,32},{1,33},{2,34},{3,35},{4,36},{5,37},{6,38},{7,39},{8,40},{9,... | collective-permute-start | bytes 786440 | tf_op jit(solution)/shard_map/ppermute | solution.py:307
  117.5 2.1 copy-start.15
  117.5 23.0 %collective-permute-start.23 = (f32[64,1024]{1,0:T(8,128)S(1)}, f32[64,1024]{1,0:T(8,128)S(1)}, u32[]{:S(2)}, u32[]{:S(2)}) collective-permute-start(f32[64,1024]{1,0:T(8,128)S(1)} %get-tuple-element.25.refs_0_), channel_id=1, source_target_pairs={{0,48},{1,49},{2,50},{3,51},{4,52},{5,53},{6,54},{7,55},{8,56},{9,... | collective-permute-start | bytes 786440 | tf_op jit(solution)/shard_map/ppermute | solution.py:307
  119.0 0.7 copy-start.16
  119.0 21.6 %collective-permute-start.22 = (f32[64,1024]{1,0:T(8,128)S(1)}, f32[64,1024]{1,0:T(8,128)S(1)}, u32[]{:S(2)}, u32[]{:S(2)}) collective-permute-start(f32[64,1024]{1,0:T(8,128)S(1)} %get-tuple-element.25.refs_0_), channel_id=1, source_target_pairs={{0,16},{1,17},{2,18},{3,19},{4,20},{5,21},{6,22},{7,23},{8,24},{9,... | collective-permute-start | bytes 786440 | tf_op jit(solution)/shard_map/ppermute | solution.py:307
  139.0 1.6 copy-start.17
  139.0 75.4 %collective-permute-start.14 = (f32[1024,1024]{1,0:T(8,128)}, f32[1024,1024]{1,0:T(8,128)}, u32[]{:S(2)}, u32[]{:S(2)}) collective-permute-start(f32[1024,1024]{1,0:T(8,128)} %row_rotation.1.refs_0_), channel_id=1, source_target_pairs={{0,1},{1,0},{2,3},{3,2},{4,5},{5,4},{6,7},{7,6},{8,9},{9,8},{10,11... | collective-permute-start | bytes 12582920 | tf_op jit(solution)/shard_map/ppermute | solution.py:345
  140.5 0.7 copy-start.18
  140.5 0.8 copy-start.19
  140.6 0.9 copy-start.20
  141.4 0.7 copy-start.21
  169.8 34.9 %collective-permute-start.32 = (f32[1024,512]{1,0:T(8,128)}, f32[1024,512]{1,0:T(8,128)}, u32[]{:S(2)}, u32[]{:S(2)}) collective-permute-start(f32[1024,512]{1,0:T(8,128)} %right_near_first.1), channel_id=1, source_target_pairs={{0,1},{1,0},{2,3},{3,2},{4,5},{5,4},{6,7},{7,6},{8,9},{9,8},{10,11... | collective-permute-start | bytes 6291464 | tf_op jit(solution)/shard_map/ppermute | solution.py:338
  178.1 36.3 %collective-permute-start.31 = (f32[1024,512]{1,0:T(8,128)}, f32[1024,512]{1,0:T(8,128)}, u32[]{:S(2)}, u32[]{:S(2)}) collective-permute-start(f32[1024,512]{1,0:T(8,128)} %right_near_second.1), channel_id=1, source_target_pairs={{0,1},{1,0},{2,3},{3,2},{4,5},{5,4},{6,7},{7,6},{8,9},{9,8},{10,11... | collective-permute-start | bytes 6291464 | tf_op jit(solution)/shard_map/ppermute | solution.py:340
  186.0 36.9 %collective-permute-start.30 = (f32[1024,512]{1,0:T(8,128)}, f32[1024,512]{1,0:T(8,128)}, u32[]{:S(2)}, u32[]{:S(2)}) collective-permute-start(f32[1024,512]{1,0:T(8,128)} %right_far_first.1), channel_id=1, source_target_pairs={{0,0},{15,15},{2,1},{4,3},{6,5},{8,7},{10,9},{12,11},{14,13},{1,2}... | collective-permute-start | bytes 6291464 | tf_op jit(solution)/shard_map/ppermute | solution.py:336
  200.1 83.0 %collective-permute-start.29 = (f32[1024,512]{1,0:T(8,128)}, f32[1024,512]{1,0:T(8,128)S(1)}, u32[]{:S(2)}, u32[]{:S(2)}) collective-permute-start(f32[1024,512]{1,0:T(8,128)} %right_far_second.1), channel_id=1, source_target_pairs={{0,0},{15,15},{2,1},{4,3},{6,5},{8,7},{10,9},{12,11},{14,13},{1,2}... | collective-permute-start | bytes 6291464 | tf_op jit(solution)/shard_map/ppermute | solution.py:342
  213.1 83.0 %collective-permute-start.36 = (f32[512,512]{1,0:T(8,128)}, f32[512,512]{1,0:T(8,128)S(1)}, u32[]{:S(2)}, u32[]{:S(2)}) collective-permute-start(f32[512,512]{1,0:T(8,128)} %get-tuple-element.23.own_ref), channel_id=1, source_target_pairs={{1,17},{3,19},{5,21},{7,23},{9,25},{11,27},{13,29},{15,31},{16,0},... | collective-permute-start | bytes 3145736 | tf_op jit(solution)/shard_map/ppermute | solution.py:384
  231.3 72.0 %collective-permute-start.34 = (f32[512,512]{1,0:T(8,128)}, f32[512,512]{1,0:T(8,128)}, u32[]{:S(2)}, u32[]{:S(2)}) collective-permute-start(f32[512,512]{1,0:T(8,128)} %get-tuple-element.21.own_ref), channel_id=1, source_target_pairs={{1,17},{3,19},{5,21},{7,23},{9,25},{11,27},{13,29},{15,31},{16,0},... | collective-permute-start | bytes 3145736 | tf_op jit(solution)/shard_map/ppermute | solution.py:384
  232.5 67.6 %collective-permute-start.35 = (f32[512,512]{1,0:T(8,128)}, f32[512,512]{1,0:T(8,128)}, u32[]{:S(2)}, u32[]{:S(2)}) collective-permute-start(f32[512,512]{1,0:T(8,128)} %get-tuple-element.22.own_ref), channel_id=1, source_target_pairs={{0,16},{2,18},{4,20},{6,22},{8,24},{10,26},{12,28},{14,30},{16,32}... | collective-permute-start | bytes 3145736 | tf_op jit(solution)/shard_map/ppermute | solution.py:384
  283.1 1.3 copy-start.1
  292.8 13.9 %collective-permute-start.33 = (f32[512,512]{1,0:T(8,128)}, f32[512,512]{1,0:T(8,128)S(1)}, u32[]{:S(2)}, u32[]{:S(2)}) collective-permute-start(f32[512,512]{1,0:T(8,128)} %get-tuple-element.20.own_ref), channel_id=1, source_target_pairs={{0,16},{2,18},{4,20},{6,22},{8,24},{10,26},{12,28},{14,30},{16,32}... | collective-permute-start | bytes 3145736 | tf_op jit(solution)/shard_map/ppermute | solution.py:384
  296.1 1.0 copy-start.2
  306.7 1.0 copy-start.3

commit v2 on v1

v2 whole, which is shorter than its diff:
```python
import functools

import jax
import jax.numpy as jnp
from jax import lax
from jax.experimental import pallas as pl
from jax.experimental.pallas import tpu as pltpu
from jax.sharding import PartitionSpec as P

f32, bf16, i32 = jnp.float32, jnp.bfloat16, jnp.int32
AXES = ("row", "col")
VMEM_LIMIT = 56 * 1024 * 1024


def cost(flops, nbytes):
    return pl.CostEstimate(flops=flops, bytes_accessed=nbytes, transcendentals=0)


def split(value):
    high = value.astype(bf16)
    return high, (value - high.astype(f32)).astype(bf16)


def dot(a, b):
    return jnp.dot(a, b, preferred_element_type=f32)


def dot3(a_high, a_low, b_high, b_low):
    return dot(a_high, b_high) + (dot(a_high, b_low) + dot(a_low, b_high))


CORE, SOURCE, FAR_FIRST, FAR_SECOND, FAR_HALF, NEAR_HALF, NEAR_FIRST, NEAR_SECOND = range(8)
OUT_FIRST, OUT_SECOND, KEPT_FIRST, KEPT_SECOND, NEAR_BLOCK, FAR_BLOCK = range(8, 14)
LAND_FIRST, LAND_SECOND, END_FIRST, END_SECOND = range(14, 18)
PLACES = 18


def pack_kernel(info_ref, block_ref, packed_ref, masked_ref):
    width = block_ref.shape[0]
    half = width // 2
    rows = lax.broadcasted_iota(i32, (half, half), 0)
    cols = lax.broadcasted_iota(i32, (half, half), 1)
    on_diagonal = rows == cols
    top = block_ref[:half, :half]
    bottom = block_ref[half:, half:]
    top_only = jnp.where(on_diagonal, top, 0.0)
    bottom_only = jnp.where(on_diagonal, bottom, 0.0)
    top_down = jnp.sum(top_only, axis=1, keepdims=True)
    top_across = jnp.sum(top_only, axis=0, keepdims=True)
    bottom_down = jnp.sum(bottom_only, axis=1, keepdims=True)
    bottom_across = jnp.sum(bottom_only, axis=0, keepdims=True)
    above = rows < cols
    value = jnp.where(above, top, bottom)
    spacing = jnp.where(above, top_across - top_down, bottom_across - bottom_down)
    triangles = jnp.where(on_diagonal, 0.0, value / jnp.where(on_diagonal, 1.0, spacing))
    corner = block_ref[:half, half:] / (bottom_across - top_down)
    here = info_ref[SOURCE] > 0
    packed_ref[:, :half] = triangles
    packed_ref[:, half:] = corner
    masked_ref[:, :half] = jnp.where(here, triangles, 0.0)
    masked_ref[:, half:] = jnp.where(here, corner, 0.0)


def pack(info, matrix):
    width = matrix.shape[1]
    half = width // 2
    out = jax.ShapeDtypeStruct((half, width), f32)
    out_spec = pl.BlockSpec((half, width), lambda i, info: (0, 0))
    return pl.pallas_call(
        pack_kernel,
        out_shape=[out, out],
        grid_spec=pltpu.PrefetchScalarGridSpec(
            num_scalar_prefetch=1,
            grid=(1,),
            in_specs=[pl.BlockSpec((width, width), lambda i, info: (info[CORE], 0))],
            out_specs=[out_spec, out_spec],
        ),
        compiler_params=pltpu.CompilerParams(vmem_limit_bytes=VMEM_LIMIT),
        cost_estimate=cost(8 * width * width, 8 * width * width),
        name="pack",
    )(info, matrix)


def rotation_kernel(sign, count, in_parts, info_ref, *refs):
    pieces = refs[:count]
    outs = refs[-7:-5] if in_parts else refs[-6:-5]
    packed, e_high, e_low, t_high, t_low = refs[-5:]
    depth, width = pieces[0].shape
    half = width // 2
    if count == 1:
        packed = pieces[0]
    else:
        for k in range(count):
            at = pl.multiple_of(info_ref[PLACES + k] * depth, depth)
            packed[pl.ds(at, depth), :] = pieces[k][...]
    rows = lax.broadcasted_iota(i32, (half, half), 0)
    cols = lax.broadcasted_iota(i32, (half, half), 1)
    triangles = packed[:, :half]
    flipped = -triangles.T
    corner = packed[:, half:]

    def put(r, c, value):
        if sign < 0:
            value = -value
        high, low = split(value)
        e_high[r * half : (r + 1) * half, c * half : (c + 1) * half] = high
        e_low[r * half : (r + 1) * half, c * half : (c + 1) * half] = low

    put(0, 0, jnp.where(rows < cols, triangles, flipped))
    put(1, 1, jnp.where(rows > cols, triangles, flipped))
    put(0, 1, corner)
    put(1, 0, -corner.T)
    tile = 256

    for n in range(width // tile):
        lo, hi = n * tile, (n + 1) * tile
        square = 0.5 * dot3(e_high[:hi, :], e_low[:hi, :], e_high[:, lo:hi], e_low[:, lo:hi])
        t_high[:hi, lo:hi], t_low[:hi, lo:hi] = split(square)
        if n > 0:
            t_high[lo:hi, :lo], t_low[lo:hi, :lo] = split(square[:lo].T)

    def store(r0, r1, c0, c1, value):
        if in_parts:
            outs[0][r0:r1, c0:c1], outs[1][r0:r1, c0:c1] = split(value)
        else:
            outs[0][r0:r1, c0:c1] = value

    for n in range(width // tile):
        lo, hi = n * tile, (n + 1) * tile
        odd = dot3(e_high[:hi, :], e_low[:hi, :], t_high[:, lo:hi], t_low[:, lo:hi])
        odd = odd + (e_high[:hi, lo:hi].astype(f32) + e_low[:hi, lo:hi].astype(f32))
        even = t_high[:hi, lo:hi].astype(f32) + t_low[:hi, lo:hi].astype(f32)
        here = lax.broadcasted_iota(i32, (hi, tile), 0)
        there = lax.broadcasted_iota(i32, (hi, tile), 1) + lo
        store(0, hi, lo, hi, even + odd + jnp.where(here == there, 1.0, 0.0))
        if n > 0:
            store(lo, hi, 0, lo, (even[:lo] - odd[:lo]).T)


def rotation(info, pieces, sign, in_parts, after, name):
    depth, width = pieces[0].shape
    square = (width, width)
    if in_parts:
        shapes = [jax.ShapeDtypeStruct(square, bf16)] * 2
    else:
        shapes = [jax.ShapeDtypeStruct(square, f32)]
    return pl.pallas_call(
        functools.partial(rotation_kernel, sign, len(pieces), in_parts),
        out_shape=shapes,
        in_specs=[pl.BlockSpec(memory_space=pltpu.SMEM)]
        + [pl.BlockSpec(memory_space=pltpu.VMEM)] * len(pieces)
        + [pl.BlockSpec(memory_space=pl.ANY)] * len(after),
        out_specs=[pl.BlockSpec(memory_space=pltpu.VMEM)] * len(shapes),
        scratch_shapes=[pltpu.VMEM((width // 2, width), f32)] + [pltpu.VMEM(square, bf16)] * 4,
        compiler_params=pltpu.CompilerParams(vmem_limit_bytes=VMEM_LIMIT),
        cost_estimate=cost(12 * width**3, 6 * width * width),
        name=name,
    )(info, *pieces, *after)


def right_kernel(info_ref, m_ref, high_ref, low_ref, *refs):
    m_high, m_low = split(m_ref[...])
    refs[-1][...] = dot3(m_high, m_low, high_ref[...], low_ref[...])


def right(info, slots, which, matrix, r_high, r_low, after, name):
    width = matrix.shape[1]
    half = width // 2
    tile = 512
    per_slot = width // tile

    def from_matrix(i, info):
        slot = info[slots[0]]
        if len(slots) > 1:
            slot = jnp.where(i < per_slot, slot, info[slots[1]])
        return (slot * per_slot + lax.rem(i, per_slot), 0)

    return pl.pallas_call(
        right_kernel,
        out_shape=jax.ShapeDtypeStruct((len(slots) * width, half), f32),
        grid_spec=pltpu.PrefetchScalarGridSpec(
            num_scalar_prefetch=1,
            grid=(per_slot * len(slots),),
            in_specs=[
                pl.BlockSpec((tile, width), from_matrix),
                pl.BlockSpec((width, half), lambda i, info: (0, info[which])),
                pl.BlockSpec((width, half), lambda i, info: (0, info[which])),
            ]
            + [pl.BlockSpec(memory_space=pl.ANY)] * len(after),
            out_specs=pl.BlockSpec((tile, half), lambda i, info: (i, 0)),
        ),
        compiler_params=pltpu.CompilerParams(vmem_limit_bytes=VMEM_LIMIT),
        cost_estimate=cost(3 * len(slots) * width**3, 8 * width * width),
        name=name,
    )(info, matrix, r_high, r_low, *after)


def left_kernel(info_ref, *refs):
    turned_ref, part_ref = refs[:2]
    moved_ref, kept_ref, part_high, part_low = refs[-4:]
    step = pl.program_id(0)

    @pl.when(step == 0)
    def _():
        part_high[...], part_low[...] = split(part_ref[...])

    t_high, t_low = split(turned_ref[...])
    value = dot3(t_high, t_low, part_high[...], part_low[...])

    @pl.when(step == 0)
    def _():
        moved_ref[...] = value

    @pl.when(step == 1)
    def _():
        kept_ref[...] = value


def left(info, out_half, kept_row, block, turned, part, part_at, result, out_rows, name):
    width = turned.shape[0]
    half = width // 2
    operands = [turned, part]
    in_specs = [
        pl.BlockSpec(
            (half, width), lambda i, info: (jnp.where(i == 0, info[out_half], 1 - info[out_half]), 0)
        ),
        pl.BlockSpec((width, half), lambda i, info: (part_at, 0)),
    ]
    aliases = {}
    if result is not None:
        operands.append(result)
        in_specs.append(pl.BlockSpec(memory_space=pl.ANY))
        aliases = {3: 1}
    return pl.pallas_call(
        left_kernel,
        out_shape=[
            jax.ShapeDtypeStruct((half, half), f32),
            jax.ShapeDtypeStruct((out_rows, width), f32),
        ],
        grid_spec=pltpu.PrefetchScalarGridSpec(
            num_scalar_prefetch=1,
            grid=(2,),
            in_specs=in_specs,
            out_specs=[
                pl.BlockSpec((half, half), lambda i, info: (0, 0)),
                pl.BlockSpec((half, half), lambda i, info: (info[kept_row], info[block])),
            ],
            scratch_shapes=[pltpu.VMEM((width, half), bf16)] * 2,
        ),
        input_output_aliases=aliases,
        compiler_params=pltpu.CompilerParams(vmem_limit_bytes=VMEM_LIMIT),
        cost_estimate=cost(3 * width**3, 10 * width * width),
        name=name,
    )(info, *operands)


def land_kernel(parts, info_ref, *refs):
    count = len(parts)
    out_ref, sems = refs[-2:]
    half = refs[0].shape[0]

    def copy(k, source):
        row, block, _ = parts[k]
        rows = pl.ds(pl.multiple_of(info_ref[row] * half, half), half)
        cols = pl.ds(pl.multiple_of(info_ref[block] * half, half), half)
        return pltpu.make_async_copy(source, out_ref.at[rows, cols], sems.at[k])

    for k in range(count):
        own = info_ref[parts[k][2]] > 0

        @pl.when(own)
        def _():
            copy(k, refs[count + k]).start()

        @pl.when(jnp.logical_not(own))
        def _():
            copy(k, refs[k]).start()

    for k in range(count):
        copy(k, refs[k]).wait()


def land(info, parts, arrived, own, result, name):
    half = arrived[0].shape[0]
    anywhere = pl.BlockSpec(memory_space=pl.ANY)
    count = len(parts)
    return pl.pallas_call(
        functools.partial(land_kernel, parts),
        out_shape=jax.ShapeDtypeStruct(result.shape, f32),
        in_specs=[pl.BlockSpec(memory_space=pltpu.SMEM)] + [anywhere] * (2 * count + 1),
        out_specs=anywhere,
        scratch_shapes=[pltpu.SemaphoreType.DMA((count,))],
        input_output_aliases={2 * count + 1: 0},
        compiler_params=pltpu.CompilerParams(vmem_limit_bytes=VMEM_LIMIT),
        cost_estimate=cost(half * half, 8 * count * half * half),
        name=name,
    )(info, *arrived, *own, result)


OFFSETS = [(1, 0), (3, 0), (2, 0), (0, 1), (1, 1), (3, 1), (2, 1)]


def shifted(member, offset):
    ring, plane = offset
    return (member // 4 ^ plane) * 4 + (member + ring) % 4


def group_pairs(group, offset, only_source):
    pairs = []
    for row in range(8):
        for col in range(16):
            chip, core = col // 2, col % 2
            if only_source and row != chip:
                continue
            if group == "row":
                target = (shifted(row, offset), col)
            else:
                target = (row, 2 * shifted(chip, offset) + core)
            pairs.append((row * 16 + col, target[0] * 16 + target[1]))
    return pairs


def spread(packed, group, member, is_source):
    depth = packed.shape[0] // 8

    def piece(at):
        return lax.dynamic_slice_in_dim(packed, at * depth, depth, 0)

    arrived = [
        lax.ppermute(piece(shifted(member, offset)), AXES, group_pairs(group, offset, True))
        for offset in OFFSETS
    ]
    own = jnp.where(is_source, piece(member), sum(arrived[1:], arrived[0]))
    return [own] + [
        lax.ppermute(own, AXES, group_pairs(group, offset, False)) for offset in OFFSETS
    ]


def local(matrix):
    row = lax.axis_index("row")
    col = lax.axis_index("col")
    chip = col // 2
    core = col % 2
    is_source = row == chip
    rows_here = matrix.shape[0]
    at_end = (col == 0) | (col == 15)
    near_half = jnp.where((core == 1) | (col == 0), 1, 0)
    out_top = jnp.where(row == 0, 0, 1)
    values = {
        CORE: core,
        SOURCE: is_source,
        FAR_FIRST: jnp.where(at_end, core, 1 - core),
        FAR_SECOND: jnp.where(at_end, 1 - core, core),
        FAR_HALF: 1 - near_half,
        NEAR_HALF: near_half,
        NEAR_FIRST: 1 - core,
        NEAR_SECOND: core,
        OUT_FIRST: jnp.where(core == 0, out_top, 0),
        OUT_SECOND: jnp.where(core == 0, 0, out_top),
        KEPT_FIRST: jnp.where(core == 0, 2, 1),
        KEPT_SECOND: jnp.where(core == 0, 1, 2),
        NEAR_BLOCK: 1 - core,
        FAR_BLOCK: core,
        LAND_FIRST: jnp.where(core == 0, 3, 0),
        LAND_SECOND: jnp.where(core == 0, 0, 3),
        END_FIRST: jnp.where(core == 0, row == 7, row == 0),
        END_SECOND: jnp.where(core == 0, row == 0, row == 7),
        PLACES: row,
    }
    for k, (ring, plane) in enumerate(OFFSETS):
        values[PLACES + 1 + k] = shifted(row, (4 - ring, plane))
    info = jnp.stack([jnp.asarray(values[k], i32) for k in range(len(values))])

    packed, masked = pack(info, matrix)
    alike = [list(range(0, 16, 2)), list(range(1, 16, 2))]
    row_packed = lax.psum(masked, "col", axis_index_groups=alike)
    col_pieces = spread(packed, "row", row, is_source)

    r_high, r_low = rotation(info, col_pieces, 1, True, [], "column_rotation")
    swap = [(i, i ^ 1) for i in range(16)]
    chips = [(0, 0), (15, 15)]
    chips += [(i, i - 1) for i in range(2, 16, 2)] + [(i, i + 1) for i in range(1, 15, 2)]
    to_send = right(
        info, [FAR_FIRST], FAR_HALF, matrix, r_high, r_low, [], "right_far_first"
    )
    far_first = lax.ppermute(to_send, "col", chips)
    to_send = right(
        info, [NEAR_FIRST, NEAR_SECOND], NEAR_HALF, matrix, r_high, r_low, [to_send], "right_near"
    )
    near = lax.ppermute(to_send, "col", swap)
    to_send = right(
        info, [FAR_SECOND], FAR_HALF, matrix, r_high, r_low, [to_send], "right_far_second"
    )
    far_second = lax.ppermute(to_send, "col", chips)

    (turned,) = rotation(info, [row_packed], -1, False, [to_send], "row_rotation")
    other_turned = lax.ppermute(turned, "col", swap)

    def row_pairs(down_core):
        pairs = []
        for r in range(8):
            for c in range(16):
                target = r - 1 if c % 2 == down_core else r + 1
                if 0 <= target < 8:
                    pairs.append((r * 16 + c, target * 16 + c))
        return pairs

    result = None
    moved, arrived = [], []
    for name, order, block, part, part_at in (
        ("left_near_first", 0, NEAR_BLOCK, near, 0),
        ("left_far_first", 0, FAR_BLOCK, far_first, 0),
        ("left_near_second", 1, NEAR_BLOCK, near, 1),
        ("left_far_second", 1, FAR_BLOCK, far_second, 0),
    ):
        leaving, result = left(
            info,
            (OUT_FIRST, OUT_SECOND)[order],
            (KEPT_FIRST, KEPT_SECOND)[order],
            block,
            (turned, other_turned)[order],
            part,
            part_at,
            result,
            rows_here,
            name,
        )
        moved.append(leaving)
        arrived.append(lax.ppermute(leaving, AXES, row_pairs(order)))
    first, second = (LAND_FIRST, END_FIRST), (LAND_SECOND, END_SECOND)
    parts = [
        (order[0], block, order[1])
        for order in (first, second)
        for block in (NEAR_BLOCK, FAR_BLOCK)
    ]
    own = moved[2:] + moved[:2]
    result = land(info, parts[:3], arrived[:3], own[:3], result, "land_three")
    return land(info, parts[3:], arrived[3:], own[3:], result, "land_last")


def solution(mesh):
    return jax.shard_map(
        local, mesh=mesh, in_specs=(P("row", "col"),), out_specs=P("row", "col"), check_vma=False
    )
```

time: 315 us -> 420 us (1.33)
  Pallas kernels: 120 us -> 223 us
  waiting for transfers between devices: 89 us -> 118 us
  starting transfers between devices: 80.9 us -> 52.1 us
  between operations: 0.36 us -> 13.8 us
  other arithmetic: 10.6 us -> 1.1 us
    pallas_call x11 -> x8, Pallas kernels: 86.6 us -> 190 us  [the longest x2 131 us: land(): pl.pallas_call(functools.partial(land_kernel, parts), out_shape=jax.Shape...]
    psum x0 -> x1, waiting for transfers between devices: none -> 36.2 us  [local(): row_packed = lax.psum(masked, 'col', axis_index_groups=alike)]
    ppermute x14 -> x7, waiting for transfers between devices: 35.5 us -> 10.8 us  [spread(): lax.ppermute(piece(shifted(member, offset)), AXES, group_pairs(group, off...]
    ppermute x22 -> x14, starting transfers between devices: 66.4 us -> 46.7 us  [the longest x7 29.6 us: spread(): lax.ppermute(own, AXES, group_pairs(group, offset, False))]
    ppermute x22 -> x14, waiting for transfers between devices: 53.5 us -> 71.2 us  [the longest x1 40.6 us: local(): far_second = lax.ppermute(to_send, 'col', chips)]
    ppermute x14 -> x7, starting transfers between devices: 14.2 us -> 5.36 us  [spread(): lax.ppermute(piece(shifted(member, offset)), AXES, group_pairs(group, off...]
    another operation x11 -> x0, other arithmetic: 6.94 us -> none  [scalars(): return jnp.stack([jnp.asarray(v, i32) for v in values])]
  transfers between devices with their start and end apart: 37 -> 23, of which waited for: 9 -> 6; matrix products, arithmetic and copies ran while one was open for 3% -> 0% of each run, Pallas kernels for 36% -> 44%
where the time goes in v2:
time: 420 us; the launch traced here: 417 us
  Pallas kernels  223 us (53%)
  waiting for transfers between devices  118 us (28%)
  starting transfers between devices  52.1 us (12%)
  between operations  13.8 us (3%)
  local copies, waits for them, and re-layouts  8.3 us (2%)
    pallas_call x2, Pallas kernels, land(): pl.pallas_call(functools.partial(land_kernel, parts), out_shape=jax.Shape...  131 us
    ppermute x1, waiting for transfers between devices, local(): far_second = lax.ppermute(to_send, 'col', chips)  40.6 us
    psum x1, waiting for transfers between devices, local(): row_packed = lax.psum(masked, 'col', axis_index_groups=alike)  36.2 us
    pallas_call x4, Pallas kernels, left(): pl.pallas_call(left_kernel, out_shape=[jax.ShapeDtypeStruct((half, half),...  33.1 us
    ppermute x7, starting transfers between devices, spread(): lax.ppermute(own, AXES, group_pairs(group, offset, False))  29.6 us
    pallas_call x2, Pallas kernels, rotation(): pl.pallas_call(functools.partial(rotation_kernel, sign, len(pieces), in_p...  27.7 us
    pallas_call x3, Pallas kernels, right(): pl.pallas_call(right_kernel, out_shape=jax.ShapeDtypeStruct((len(slots) *...  26.3 us
    ppermute x7, waiting for transfers between devices, spread(): lax.ppermute(own, AXES, group_pairs(group, offset, False))  16.8 us
  transfers between devices with their start and end apart: 23, of which 6 were waited for; matrix products, arithmetic and copies ran while one was open for 0% of the time, Pallas kernels for 44%

profile of v2, /device:TPU:8, one launch (start us, length us, event | category | flops | bytes accessed | tf_op | source)
XLA Modules:
  0.0 416.7 jit_solution(2917570403877096101)
XLA Ops:
  6.5 0.7 stack.110.info_ref
  7.2 5.4 %pack.1 = (f32[512,1024]{1,0:T(8,128)}, f32[512,1024]{1,0:T(8,128)}) custom-call(s32[26]{0:T(128)} %stack.110.info_ref, f32[2048,1024]{1,0:T(8,128)} %m_ref.5), custom_call_target="tpu_custom_call" | custom-call | flops 8388608 | bytes 8388608 | tf_op jit(solution)/shard_map/pack/pallas_call | solution.py:69
  12.6 1.5 constant_dynamic-slice_fusion.5
  14.2 0.7 collective-permute-start
  14.8 0.7 collective-permute-start.1
  15.5 0.7 collective-permute-start.2
  16.2 1.3 collective-permute-start.3
  17.5 0.7 collective-permute-start.4
  18.2 0.0 collective-permute-done
  18.2 0.7 collective-permute-start.5
  18.9 0.0 collective-permute-done.1
  18.9 0.7 collective-permute-start.6
  19.6 0.0 collective-permute-done.2
  19.6 10.8 %collective-permute-done.3 = f32[64,1024]{1,0:T(8,128)S(1)} collective-permute-done((f32[64,1024]{1,0:T(8,128)S(1)}, f32[64,1024]{1,0:T(8,128)S(1)}, u32[]{:S(2)}, u32[]{:S(2)}) %collective-permute-start.3) | collective-permute-done | bytes 262176 | tf_op jit(solution)/shard_map/ppermute | solution.py:330
  30.4 0.0 collective-permute-done.4
  30.4 0.0 collective-permute-done.5
  30.4 0.0 collective-permute-done.6
  30.4 1.1 add_select_fusion.refs_0_
  31.5 0.0 copy-start.5
  31.6 11.9 %collective-permute-start.10 = (f32[64,1024]{1,0:T(8,128)S(1)}, f32[64,1024]{1,0:T(8,128)S(1)}, u32[]{:S(2)}, u32[]{:S(2)}) collective-permute-start(f32[64,1024]{1,0:T(8,128)S(1)} %add_select_fusion.refs_0_), channel_id=1, source_target_pairs={{0,64},{1,65},{2,66},{3,67},{4,68},{5,69},{6,70},{7,71},{8,72},{9,... | collective-permute-start | bytes 786440 | tf_op jit(solution)/shard_map/ppermute | solution.py:335
  43.4 0.4 collective-permute-start.11
  43.9 5.2 %collective-permute-start.12 = (f32[64,1024]{1,0:T(8,128)S(1)}, f32[64,1024]{1,0:T(8,128)S(1)}, u32[]{:S(2)}, u32[]{:S(2)}) collective-permute-start(f32[64,1024]{1,0:T(8,128)S(1)} %add_select_fusion.refs_0_), channel_id=1, source_target_pairs={{0,112},{1,113},{2,114},{3,115},{4,116},{5,117},{6,118},{7,119},{8... | collective-permute-start | bytes 786440 | tf_op jit(solution)/shard_map/ppermute | solution.py:335
  49.1 5.2 %collective-permute-start.13 = (f32[64,1024]{1,0:T(8,128)S(1)}, f32[64,1024]{1,0:T(8,128)S(1)}, u32[]{:S(2)}, u32[]{:S(2)}) collective-permute-start(f32[64,1024]{1,0:T(8,128)S(1)} %add_select_fusion.refs_0_), channel_id=1, source_target_pairs={{0,96},{1,97},{2,98},{3,99},{4,100},{5,101},{6,102},{7,103},{8,104... | collective-permute-start | bytes 786440 | tf_op jit(solution)/shard_map/ppermute | solution.py:335
  54.3 0.0 collective-permute-start.7
  54.3 11.5 %collective-permute-done.10.refs_4_ = f32[64,1024]{1,0:T(8,128)S(1)} collective-permute-done((f32[64,1024]{1,0:T(8,128)S(1)}, f32[64,1024]{1,0:T(8,128)S(1)}, u32[]{:S(2)}, u32[]{:S(2)}) %collective-permute-start.10) | collective-permute-done | bytes 262176 | tf_op jit(solution)/shard_map/ppermute | solution.py:335
  65.7 0.0 collective-permute-start.8
  65.7 0.0 collective-permute-done.11.refs_5_
  65.7 6.9 %collective-permute-start.9 = (f32[64,1024]{1,0:T(8,128)S(1)}, f32[64,1024]{1,0:T(8,128)S(1)}, u32[]{:S(2)}, u32[]{:S(2)}) collective-permute-start(f32[64,1024]{1,0:T(8,128)S(1)} %add_select_fusion.refs_0_), channel_id=1, source_target_pairs={{0,32},{1,33},{2,34},{3,35},{4,36},{5,37},{6,38},{7,39},{8,40},{9,... | collective-permute-start | bytes 786440 | tf_op jit(solution)/shard_map/ppermute | solution.py:335
  72.7 0.0 all-reduce.2.cloned.1.call-update
  72.7 0.0 collective-permute-done.12.refs_6_
  72.7 0.0 collective-permute-done.13.refs_7_
  72.7 0.0 collective-permute-done.7.refs_1_
  72.8 5.3 %collective-permute-done.9.refs_3_ = f32[64,1024]{1,0:T(8,128)S(1)} collective-permute-done((f32[64,1024]{1,0:T(8,128)S(1)}, f32[64,1024]{1,0:T(8,128)S(1)}, u32[]{:S(2)}, u32[]{:S(2)}) %collective-permute-start.9) | collective-permute-done | bytes 262176 | tf_op jit(solution)/shard_map/ppermute | solution.py:335
  78.2 0.7 copy-done.12
  78.9 13.9 %column_rotation.1 = (bf16[1024,1024]{1,0:T(8,128)(2,1)}, bf16[1024,1024]{1,0:T(8,128)(2,1)}) custom-call(s32[26]{0:T(128)} %stack.110.info_ref, f32[64,1024]{1,0:T(8,128)} %copy-done.5, f32[64,1024]{1,0:T(8,128)} %copy-done.10, f32[64,1024]{1,0:T(8,128)} %copy-done.11, f32[64,1024]{1,0:T(8,128)} %copy-done.12, f32[64,1024]{1,0:T(8,128)} %copy-done.6, ...), custom_call_target="tpu_custom_call" | custom-call | flops 12884901888 | bytes 6291456 | tf_op jit(solution)/shard_map/column_rotation/pallas_call | solution.py:147
  92.8 7.5 %right_far_first.1.refs_0_ = f32[1024,512]{1,0:T(8,128)} custom-call(s32[26]{0:T(128)} %stack.110.info_ref, f32[2048,1024]{1,0:T(8,128)} %m_ref.5, bf16[1024,1024]{1,0:T(8,128)(2,1)} %get-tuple-element.19.high_ref, bf16[1024,1024]{1,0:T(8,128)(2,1)} %get-tuple-element.20.low_ref), custom_call_target="tpu_custom_call" | custom-call | flops 3221225472 | bytes 8388608 | tf_op jit(solution)/shard_map/right_far_first/pallas_call | solution.py:178
  100.3 11.3 %right_near.1.refs_0_ = f32[2048,512]{1,0:T(8,128)} custom-call(s32[26]{0:T(128)} %stack.110.info_ref, f32[2048,1024]{1,0:T(8,128)} %m_ref.5, bf16[1024,1024]{1,0:T(8,128)(2,1)} %get-tuple-element.19.high_ref, bf16[1024,1024]{1,0:T(8,128)(2,1)} %get-tuple-element.20.low_ref, f32[1024,512]{1,0:T(8,128)} %right_far_first.1.refs_0_), custom_call_target="tpu_custom_call" | custom-call | flops 6442450944 | bytes 8388608 | tf_op jit(solution)/shard_map/right_near/pallas_call | solution.py:178
  111.6 0.0 collective-permute-start.16
  111.6 7.5 %right_far_second.1.refs_1_ = f32[1024,512]{1,0:T(8,128)} custom-call(s32[26]{0:T(128)} %stack.110.info_ref, f32[2048,1024]{1,0:T(8,128)} %m_ref.5, bf16[1024,1024]{1,0:T(8,128)(2,1)} %get-tuple-element.19.high_ref, bf16[1024,1024]{1,0:T(8,128)(2,1)} %get-tuple-element.20.low_ref, f32[2048,512]{1,0:T(8,128)} %right_near.1.refs_0_), custom_call_target="tpu_custom_call" | custom-call | flops 3221225472 | bytes 8388608 | tf_op jit(solution)/shard_map/right_far_second/pallas_call | solution.py:178
  119.1 36.2 %all-reduce.2.cloned.1.call-done.refs_0_ = f32[512,1024]{1,0:T(8,128)} async-done(((f32[512,1024]{1,0:T(8,128)}), f32[512,1024]{1,0:T(8,128)}) %all-reduce.2.cloned.1.call-update) | async-done | bytes 2097168 | tf_op jit(solution)/shard_map/psum | solution.py:376
  155.3 13.8 %row_rotation.1.refs_0_ = f32[1024,1024]{1,0:T(8,128)} custom-call(s32[26]{0:T(128)} %stack.110.info_ref, f32[512,1024]{1,0:T(8,128)} %all-reduce.2.cloned.1.call-done.refs_0_, f32[1024,512]{1,0:T(8,128)} %right_far_second.1.refs_1_), custom_call_target="tpu_custom_call" | custom-call | flops 12884901888 | bytes 6291456 | tf_op jit(solution)/shard_map/row_rotation/pallas_call | solution.py:147
  169.1 0.0 collective-permute-start.14
  169.1 5.0 %collective-permute-start.17 = (f32[1024,512]{1,0:T(8,128)}, f32[1024,512]{1,0:T(8,128)}, u32[]{:S(2)}, u32[]{:S(2)}) collective-permute-start(f32[1024,512]{1,0:T(8,128)} %right_far_first.1.refs_0_), channel_id=1, source_target_pairs={{0,0},{15,15},{2,1},{4,3},{6,5},{8,7},{10,9},{12,11},{14,13},{1,2}... | collective-permute-start | bytes 6291464 | tf_op jit(solution)/shard_map/ppermute | solution.py:386
  174.1 2.6 collective-permute-start.15
  176.8 0.0 collective-permute-done.16.refs_1_
  176.8 8.2 %left_near_first.1 = (f32[512,512]{1,0:T(8,128)}, f32[2048,1024]{1,0:T(8,128)}) custom-call(s32[26]{0:T(128)} %stack.110.info_ref, f32[1024,1024]{1,0:T(8,128)} %row_rotation.1.refs_0_, f32[2048,512]{1,0:T(8,128)} %collective-permute-done.16.refs_1_), custom_call_target="tpu_custom_call" | custom-call | flops 3221225472 | bytes 10485760 | tf_op jit(solution)/shard_map/left_near_first/pallas_call | solution.py:234
  185.0 13.8 %collective-permute-done.17.refs_1_ = f32[1024,512]{1,0:T(8,128)} collective-permute-done((f32[1024,512]{1,0:T(8,128)}, f32[1024,512]{1,0:T(8,128)}, u32[]{:S(2)}, u32[]{:S(2)}) %collective-permute-start.17) | collective-permute-done | bytes 2097184 | tf_op jit(solution)/shard_map/ppermute | solution.py:386
  198.9 8.4 %left_far_first.1 = (f32[512,512]{1,0:T(8,128)}, f32[2048,1024]{1,0:T(8,128)}) custom-call(s32[26]{0:T(128)} %stack.110.info_ref, f32[1024,1024]{1,0:T(8,128)} %row_rotation.1.refs_0_, f32[1024,512]{1,0:T(8,128)} %collective-permute-done.17.refs_1_, f32[2048,1024]{1,0:T(8,128)} %get-tuple-element.21.refs_2_), custom_call_target="tpu_custom_call", output_to_operand_aliasing={{1}: (3, {})} | custom-call | flops 3221225472 | bytes 10485760 | tf_op jit(solution)/shard_map/left_far_first/pallas_call | solution.py:234
  207.2 1.5 collective-permute-start.20
  208.8 1.3 collective-permute-start.19
  210.1 0.0 collective-permute-done.14.refs_0_
  210.1 2.0 copy-done
  212.2 8.2 %left_near_second.1 = (f32[512,512]{1,0:T(8,128)}, f32[2048,1024]{1,0:T(8,128)}) custom-call(s32[26]{0:T(128)} %stack.110.info_ref, f32[1024,1024]{1,0:T(8,128)} %copy-done, f32[2048,512]{1,0:T(8,128)} %collective-permute-done.16.refs_1_, f32[2048,1024]{1,0:T(8,128)} %get-tuple-element.22.refs_2_), custom_call_target="tpu_custom_call", output_to_operand_aliasing={{1}: (3, {})} | custom-call | flops 3221225472 | bytes 10485760 | tf_op jit(solution)/shard_map/left_near_second/pallas_call | solution.py:234
  220.4 5.2 %collective-permute-start.21 = (f32[512,512]{1,0:T(8,128)}, f32[512,512]{1,0:T(8,128)S(1)}, u32[]{:S(2)}, u32[]{:S(2)}) collective-permute-start(f32[512,512]{1,0:T(8,128)} %get-tuple-element.27.refs_3_), channel_id=1, source_target_pairs={{0,16},{2,18},{4,20},{6,22},{8,24},{10,26},{12,28},{14,30},{16,32}... | collective-permute-start | bytes 3145736 | tf_op jit(solution)/shard_map/ppermute | solution.py:429
  225.6 40.6 %collective-permute-done.15.refs_1_ = f32[1024,512]{1,0:T(8,128)S(1)} collective-permute-done((f32[1024,512]{1,0:T(8,128)}, f32[1024,512]{1,0:T(8,128)S(1)}, u32[]{:S(2)}, u32[]{:S(2)}) %collective-permute-start.15) | collective-permute-done | bytes 2097184 | tf_op jit(solution)/shard_map/ppermute | solution.py:394
  266.2 1.4 copy-done.1
  267.5 8.2 %left_far_second.1 = (f32[512,512]{1,0:T(8,128)}, f32[2048,1024]{1,0:T(8,128)}) custom-call(s32[26]{0:T(128)} %stack.110.info_ref, f32[1024,1024]{1,0:T(8,128)} %copy-done, f32[1024,512]{1,0:T(8,128)} %copy-done.1, f32[2048,1024]{1,0:T(8,128)} %get-tuple-element.23.refs_2_), custom_call_target="tpu_custom_call", output_to_operand_aliasing={{1}: (3, {})} | custom-call | flops 3221225472 | bytes 10485760 | tf_op jit(solution)/shard_map/left_far_second/pallas_call | solution.py:234
  275.8 1.3 collective-permute-start.18
  277.1 0.0 collective-permute-done.19.refs_0_
  277.2 0.0 collective-permute-done.21.refs_2_
  277.2 1.0 copy-done.3
  278.2 97.1 %land_three.1.refs_2_ = f32[2048,1024]{1,0:T(8,128)} custom-call(s32[26]{0:T(128)} %stack.110.info_ref, f32[512,512]{1,0:T(8,128)} %collective-permute-done.19.refs_0_, f32[512,512]{1,0:T(8,128)} %collective-permute-done.20.refs_1_, f32[512,512]{1,0:T(8,128)} %copy-done.3, f32[512,512]{1,0:T(8,128)} %get-tuple-element.27.refs_3_, ...), custom_call_target="tpu_custom_call", output_to_operand_aliasing={{}: (7, {})} | custom-call | flops 262144 | bytes 6291456 | tf_op jit(solution)/shard_map/land_three/pallas_call | solution.py:287
  375.3 1.0 copy-done.4
  376.3 33.5 %land_last.1 = f32[2048,1024]{1,0:T(8,128)} custom-call(s32[26]{0:T(128)} %stack.110.info_ref, f32[512,512]{1,0:T(8,128)} %copy-done.4, f32[512,512]{1,0:T(8,128)} %get-tuple-element.25.refs_1_, f32[2048,1024]{1,0:T(8,128)} %land_three.1.refs_2_), custom_call_target="tpu_custom_call", output_to_operand_aliasing={{}: (3, {})} | custom-call | flops 262144 | bytes 2097152 | tf_op jit(solution)/shard_map/land_last/pallas_call | solution.py:287
  (24 shorter events, 0.1 us)
Async XLA Ops:
  6.5 148.8 %all-reduce.2.cloned.1.call-start = ((), (), s32[]{:S(2)}) async-start(), calls=%async_computation | async-start | bytes 4194304 | tf_op jit(solution)/shard_map/psum | solution.py:376
  14.2 4.0 collective-permute-start
  14.8 4.1 collective-permute-start.1
  15.5 4.1 collective-permute-start.2
  16.2 14.2 %collective-permute-start.3 = (f32[64,1024]{1,0:T(8,128)S(1)}, f32[64,1024]{1,0:T(8,128)S(1)}, u32[]{:S(2)}, u32[]{:S(2)}) collective-permute-start(f32[64,1024]{1,0:T(8,128)S(1)} %get-tuple-element.33), channel_id=1, source_target_pairs={{0,64},{1,65},{18,82},{19,83},{36,100},{37,101},{54,118},{55,119},... | collective-permute-start | bytes 786440 | tf_op jit(solution)/shard_map/ppermute | solution.py:330
  17.5 12.9 %collective-permute-start.4 = (f32[64,1024]{1,0:T(8,128)S(1)}, f32[64,1024]{1,0:T(8,128)S(1)}, u32[]{:S(2)}, u32[]{:S(2)}) collective-permute-start(f32[64,1024]{1,0:T(8,128)S(1)} %get-tuple-element.32), channel_id=1, source_target_pairs={{0,80},{1,81},{18,98},{19,99},{36,116},{37,117},{54,70},{55,71},{7... | collective-permute-start | bytes 786440 | tf_op jit(solution)/shard_map/ppermute | solution.py:330
  18.2 12.2 %collective-permute-start.5 = (f32[64,1024]{1,0:T(8,128)S(1)}, f32[64,1024]{1,0:T(8,128)S(1)}, u32[]{:S(2)}, u32[]{:S(2)}) collective-permute-start(f32[64,1024]{1,0:T(8,128)S(1)} %get-tuple-element.31), channel_id=1, source_target_pairs={{0,112},{1,113},{18,66},{19,67},{36,84},{37,85},{54,102},{55,103},... | collective-permute-start | bytes 786440 | tf_op jit(solution)/shard_map/ppermute | solution.py:330
  18.9 11.5 %collective-permute-start.6 = (f32[64,1024]{1,0:T(8,128)S(1)}, f32[64,1024]{1,0:T(8,128)S(1)}, u32[]{:S(2)}, u32[]{:S(2)}) collective-permute-start(f32[64,1024]{1,0:T(8,128)S(1)} %get-tuple-element.30), channel_id=1, source_target_pairs={{0,96},{1,97},{18,114},{19,115},{36,68},{37,69},{54,86},{55,87},{7... | collective-permute-start | bytes 786440 | tf_op jit(solution)/shard_map/ppermute | solution.py:330
  31.5 46.6 %copy-start.5 = (f32[64,1024]{1,0:T(8,128)}, f32[64,1024]{1,0:T(8,128)S(1)}, u32[]{:S(2)}) copy-start(f32[64,1024]{1,0:T(8,128)S(1)} %add_select_fusion.refs_0_) | copy-start | bytes 786436
  31.6 34.2 %collective-permute-start.10 = (f32[64,1024]{1,0:T(8,128)S(1)}, f32[64,1024]{1,0:T(8,128)S(1)}, u32[]{:S(2)}, u32[]{:S(2)}) collective-permute-start(f32[64,1024]{1,0:T(8,128)S(1)} %add_select_fusion.refs_0_), channel_id=1, source_target_pairs={{0,64},{1,65},{2,66},{3,67},{4,68},{5,69},{6,70},{7,71},{8,72},{9,... | collective-permute-start | bytes 786440 | tf_op jit(solution)/shard_map/ppermute | solution.py:335
  43.4 22.3 %collective-permute-start.11 = (f32[64,1024]{1,0:T(8,128)S(1)}, f32[64,1024]{1,0:T(8,128)S(1)}, u32[]{:S(2)}, u32[]{:S(2)}) collective-permute-start(f32[64,1024]{1,0:T(8,128)S(1)} %add_select_fusion.refs_0_), channel_id=1, source_target_pairs={{0,80},{1,81},{2,82},{3,83},{4,84},{5,85},{6,86},{7,87},{8,88},{9,... | collective-permute-start | bytes 786440 | tf_op jit(solution)/shard_map/ppermute | solution.py:335
  43.9 28.8 %collective-permute-start.12 = (f32[64,1024]{1,0:T(8,128)S(1)}, f32[64,1024]{1,0:T(8,128)S(1)}, u32[]{:S(2)}, u32[]{:S(2)}) collective-permute-start(f32[64,1024]{1,0:T(8,128)S(1)} %add_select_fusion.refs_0_), channel_id=1, source_target_pairs={{0,112},{1,113},{2,114},{3,115},{4,116},{5,117},{6,118},{7,119},{8... | collective-permute-start | bytes 786440 | tf_op jit(solution)/shard_map/ppermute | solution.py:335
  49.1 23.6 %collective-permute-start.13 = (f32[64,1024]{1,0:T(8,128)S(1)}, f32[64,1024]{1,0:T(8,128)S(1)}, u32[]{:S(2)}, u32[]{:S(2)}) collective-permute-start(f32[64,1024]{1,0:T(8,128)S(1)} %add_select_fusion.refs_0_), channel_id=1, source_target_pairs={{0,96},{1,97},{2,98},{3,99},{4,100},{5,101},{6,102},{7,103},{8,104... | collective-permute-start | bytes 786440 | tf_op jit(solution)/shard_map/ppermute | solution.py:335
  54.3 18.5 %collective-permute-start.7 = (f32[64,1024]{1,0:T(8,128)S(1)}, f32[64,1024]{1,0:T(8,128)S(1)}, u32[]{:S(2)}, u32[]{:S(2)}) collective-permute-start(f32[64,1024]{1,0:T(8,128)S(1)} %add_select_fusion.refs_0_), channel_id=1, source_target_pairs={{0,16},{1,17},{2,18},{3,19},{4,20},{5,21},{6,22},{7,23},{8,24},{9,... | collective-permute-start | bytes 786440 | tf_op jit(solution)/shard_map/ppermute | solution.py:335
  65.7 12.4 %copy-start.6 = (f32[64,1024]{1,0:T(8,128)}, f32[64,1024]{1,0:T(8,128)S(1)}, u32[]{:S(2)}) copy-start(f32[64,1024]{1,0:T(8,128)S(1)} %collective-permute-done.10.refs_4_) | copy-start | bytes 786436
  65.7 7.0 %collective-permute-start.8 = (f32[64,1024]{1,0:T(8,128)S(1)}, f32[64,1024]{1,0:T(8,128)S(1)}, u32[]{:S(2)}, u32[]{:S(2)}) collective-permute-start(f32[64,1024]{1,0:T(8,128)S(1)} %add_select_fusion.refs_0_), channel_id=1, source_target_pairs={{0,48},{1,49},{2,50},{3,51},{4,52},{5,53},{6,54},{7,55},{8,56},{9,... | collective-permute-start | bytes 786440 | tf_op jit(solution)/shard_map/ppermute | solution.py:335
  65.7 12.4 %copy-start.7 = (f32[64,1024]{1,0:T(8,128)}, f32[64,1024]{1,0:T(8,128)S(1)}, u32[]{:S(2)}) copy-start(f32[64,1024]{1,0:T(8,128)S(1)} %collective-permute-done.11.refs_5_) | copy-start | bytes 786436
  65.7 12.4 %collective-permute-start.9 = (f32[64,1024]{1,0:T(8,128)S(1)}, f32[64,1024]{1,0:T(8,128)S(1)}, u32[]{:S(2)}, u32[]{:S(2)}) collective-permute-start(f32[64,1024]{1,0:T(8,128)S(1)} %add_select_fusion.refs_0_), channel_id=1, source_target_pairs={{0,32},{1,33},{2,34},{3,35},{4,36},{5,37},{6,38},{7,39},{8,40},{9,... | collective-permute-start | bytes 786440 | tf_op jit(solution)/shard_map/ppermute | solution.py:335
  72.7 5.4 %copy-start.8 = (f32[64,1024]{1,0:T(8,128)}, f32[64,1024]{1,0:T(8,128)S(1)}, u32[]{:S(2)}) copy-start(f32[64,1024]{1,0:T(8,128)S(1)} %collective-permute-done.12.refs_6_) | copy-start | bytes 786436
  72.7 5.4 %copy-start.9 = (f32[64,1024]{1,0:T(8,128)}, f32[64,1024]{1,0:T(8,128)S(1)}, u32[]{:S(2)}) copy-start(f32[64,1024]{1,0:T(8,128)S(1)} %collective-permute-done.13.refs_7_) | copy-start | bytes 786436
  72.8 5.4 %copy-start.10 = (f32[64,1024]{1,0:T(8,128)}, f32[64,1024]{1,0:T(8,128)S(1)}, u32[]{:S(2)}) copy-start(f32[64,1024]{1,0:T(8,128)S(1)} %collective-permute-done.7.refs_1_) | copy-start | bytes 786436
  72.8 5.4 %copy-start.11 = (f32[64,1024]{1,0:T(8,128)}, f32[64,1024]{1,0:T(8,128)S(1)}, u32[]{:S(2)}) copy-start(f32[64,1024]{1,0:T(8,128)S(1)} %collective-permute-done.8.refs_2_) | copy-start | bytes 786436
  78.2 0.7 copy-start.12
  111.6 65.2 %collective-permute-start.16 = (f32[2048,512]{1,0:T(8,128)}, f32[2048,512]{1,0:T(8,128)}, u32[]{:S(2)}, u32[]{:S(2)}) collective-permute-start(f32[2048,512]{1,0:T(8,128)} %right_near.1.refs_0_), channel_id=1, source_target_pairs={{0,1},{1,0},{2,3},{3,2},{4,5},{5,4},{6,7},{7,6},{8,9},{9,8},{10,11... | collective-permute-start | bytes 12582920 | tf_op jit(solution)/shard_map/ppermute | solution.py:390
  169.1 41.0 %collective-permute-start.14 = (f32[1024,1024]{1,0:T(8,128)}, f32[1024,1024]{1,0:T(8,128)S(1)}, u32[]{:S(2)}, u32[]{:S(2)}) collective-permute-start(f32[1024,1024]{1,0:T(8,128)} %row_rotation.1.refs_0_), channel_id=1, source_target_pairs={{0,1},{1,0},{2,3},{3,2},{4,5},{5,4},{6,7},{7,6},{8,9},{9,8},{10,11... | collective-permute-start | bytes 12582920 | tf_op jit(solution)/shard_map/ppermute | solution.py:397
  169.1 29.8 %collective-permute-start.17 = (f32[1024,512]{1,0:T(8,128)}, f32[1024,512]{1,0:T(8,128)}, u32[]{:S(2)}, u32[]{:S(2)}) collective-permute-start(f32[1024,512]{1,0:T(8,128)} %right_far_first.1.refs_0_), channel_id=1, source_target_pairs={{0,0},{15,15},{2,1},{4,3},{6,5},{8,7},{10,9},{12,11},{14,13},{1,2}... | collective-permute-start | bytes 6291464 | tf_op jit(solution)/shard_map/ppermute | solution.py:386
  174.1 92.1 %collective-permute-start.15 = (f32[1024,512]{1,0:T(8,128)}, f32[1024,512]{1,0:T(8,128)S(1)}, u32[]{:S(2)}, u32[]{:S(2)}) collective-permute-start(f32[1024,512]{1,0:T(8,128)} %right_far_second.1.refs_1_), channel_id=1, source_target_pairs={{0,0},{15,15},{2,1},{4,3},{6,5},{8,7},{10,9},{12,11},{14,13},{1,2}... | collective-permute-start | bytes 6291464 | tf_op jit(solution)/shard_map/ppermute | solution.py:394
  198.9 9.9 %copy-start.2 = (f32[512,512]{1,0:T(8,128)S(1)}, f32[512,512]{1,0:T(8,128)}, u32[]{:S(2)}) copy-start(f32[512,512]{1,0:T(8,128)} %get-tuple-element.26.refs_5_) | copy-start | bytes 3145732
  207.2 69.9 %collective-permute-start.20 = (f32[512,512]{1,0:T(8,128)}, f32[512,512]{1,0:T(8,128)}, u32[]{:S(2)}, u32[]{:S(2)}) collective-permute-start(f32[512,512]{1,0:T(8,128)} %get-tuple-element.25.refs_1_), channel_id=1, source_target_pairs={{1,17},{3,19},{5,21},{7,23},{9,25},{11,27},{13,29},{15,31},{16,0},... | collective-permute-start | bytes 3145736 | tf_op jit(solution)/shard_map/ppermute | solution.py:429
  208.8 68.3 %collective-permute-start.19 = (f32[512,512]{1,0:T(8,128)S(1)}, f32[512,512]{1,0:T(8,128)}, u32[]{:S(2)}, u32[]{:S(2)}) collective-permute-start(f32[512,512]{1,0:T(8,128)S(1)} %copy-done.2), channel_id=1, source_target_pairs={{1,17},{3,19},{5,21},{7,23},{9,25},{11,27},{13,29},{15,31},{16,0},... | collective-permute-start | bytes 3145736 | tf_op jit(solution)/shard_map/ppermute | solution.py:429
  210.1 2.0 copy-start
  220.4 56.8 %collective-permute-start.21 = (f32[512,512]{1,0:T(8,128)}, f32[512,512]{1,0:T(8,128)S(1)}, u32[]{:S(2)}, u32[]{:S(2)}) collective-permute-start(f32[512,512]{1,0:T(8,128)} %get-tuple-element.27.refs_3_), channel_id=1, source_target_pairs={{0,16},{2,18},{4,20},{6,22},{8,24},{10,26},{12,28},{14,30},{16,32}... | collective-permute-start | bytes 3145736 | tf_op jit(solution)/shard_map/ppermute | solution.py:429
  266.2 1.4 copy-start.1
  275.8 99.5 %collective-permute-start.18 = (f32[512,512]{1,0:T(8,128)}, f32[512,512]{1,0:T(8,128)S(1)}, u32[]{:S(2)}, u32[]{:S(2)}) collective-permute-start(f32[512,512]{1,0:T(8,128)} %get-tuple-element.24.refs_4_), channel_id=1, source_target_pairs={{0,16},{2,18},{4,20},{6,22},{8,24},{10,26},{12,28},{14,30},{16,32}... | collective-permute-start | bytes 3145736 | tf_op jit(solution)/shard_map/ppermute | solution.py:429
  277.2 1.0 copy-start.3
  375.3 1.0 copy-start.4
Sparse Core Ops, SparseCore 0:
  72.8 82.4 all-reduce.1

commit v3 on v2

v3 whole, which is shorter than its diff:
```python
import functools

import jax
import jax.numpy as jnp
from jax import lax
from jax.experimental import pallas as pl
from jax.experimental.pallas import tpu as pltpu
from jax.sharding import PartitionSpec as P

f32, bf16, i32 = jnp.float32, jnp.bfloat16, jnp.int32
AXES = ("row", "col")
VMEM_LIMIT = 16 * 1024 * 1024


def cost(flops, nbytes):
    return pl.CostEstimate(flops=flops // 64, bytes_accessed=nbytes // 64, transcendentals=0)


def split(value):
    high = value.astype(bf16)
    return high, (value - high.astype(f32)).astype(bf16)


def dot(a, b):
    return jnp.dot(a, b, preferred_element_type=f32)


def dot3(a_high, a_low, b_high, b_low):
    return dot(a_high, b_high) + (dot(a_high, b_low) + dot(a_low, b_high))


CORE, SOURCE, SOURCE_PLANE, RING_COL, RING_ROW = range(5)
FAR_FIRST, FAR_SECOND, FAR_HALF, NEAR_HALF, NEAR_FIRST, NEAR_SECOND = range(5, 11)
MOVED_FIRST, MOVED_SECOND, STAYS_FIRST, STAYS_SECOND = range(11, 15)
KEPT_FIRST, KEPT_SECOND, NEAR_BLOCK, FAR_BLOCK = range(15, 19)
LAND_FIRST, LAND_SECOND, END_FIRST, END_SECOND = range(19, 23)
RINGS = (1, 3, 2)


def pack_kernel(info_ref, block_ref, *refs):
    out_refs, packed = refs[:4], refs[4]
    width = block_ref.shape[0]
    half = width // 2
    rows = lax.broadcasted_iota(i32, (half, half), 0)
    cols = lax.broadcasted_iota(i32, (half, half), 1)
    on_diagonal = rows == cols
    top = block_ref[:half, :half]
    bottom = block_ref[half:, half:]
    top_only = jnp.where(on_diagonal, top, 0.0)
    bottom_only = jnp.where(on_diagonal, bottom, 0.0)
    top_down = jnp.sum(top_only, axis=1, keepdims=True)
    top_across = jnp.sum(top_only, axis=0, keepdims=True)
    bottom_down = jnp.sum(bottom_only, axis=1, keepdims=True)
    bottom_across = jnp.sum(bottom_only, axis=0, keepdims=True)
    above = rows < cols
    value = jnp.where(above, top, bottom)
    spacing = jnp.where(above, top_across - top_down, bottom_across - bottom_down)
    packed[:, :half] = jnp.where(
        on_diagonal, 0.0, value / jnp.where(on_diagonal, 1.0, spacing)
    )
    packed[:, half:] = block_ref[:half, half:] / (bottom_across - top_down)
    depth = half // 4
    for out_ref, ring in zip(out_refs, (0,) + RINGS):
        at = pl.multiple_of(lax.rem(info_ref[RING_COL] + ring, 4) * depth, depth)
        out_ref[...] = packed[pl.ds(at, depth), :]


def pack(info, matrix):
    width = matrix.shape[1]
    half = width // 2
    out = jax.ShapeDtypeStruct((half // 4, width), f32)
    out_spec = pl.BlockSpec((half // 4, width), lambda i, info: (0, 0))
    return pl.pallas_call(
        pack_kernel,
        out_shape=[out] * 4,
        grid_spec=pltpu.PrefetchScalarGridSpec(
            num_scalar_prefetch=1,
            grid=(1,),
            in_specs=[pl.BlockSpec((width, width), lambda i, info: (info[CORE], 0))],
            out_specs=[out_spec] * 4,
            scratch_shapes=[pltpu.VMEM((half, width), f32)],
        ),
        compiler_params=pltpu.CompilerParams(vmem_limit_bytes=VMEM_LIMIT),
        cost_estimate=cost(8 * width * width, 6 * width * width),
        name="pack",
    )(info, matrix)


def merge_kernel(info_ref, own, *refs):
    for group in range(2):
        arrived = refs[3 * group : 3 * group + 3]
        total = arrived[0][...] + arrived[1][...] + arrived[2][...]
        refs[6 + group][...] = jnp.where(info_ref[SOURCE] > 0, own[...], total)


def choose_kernel(info_ref, *refs):
    for group in range(2):
        across, held, out = refs[group], refs[2 + group], refs[4 + group]
        out[...] = jnp.where(info_ref[SOURCE_PLANE] > 0, held[...], across[...])


def small(kernel, info, operands, outs, name):
    shape = operands[0].shape
    return pl.pallas_call(
        kernel,
        out_shape=[jax.ShapeDtypeStruct(shape, f32)] * outs,
        in_specs=[pl.BlockSpec(memory_space=pltpu.SMEM)]
        + [pl.BlockSpec(memory_space=pltpu.VMEM)] * len(operands),
        out_specs=[pl.BlockSpec(memory_space=pltpu.VMEM)] * outs,
        compiler_params=pltpu.CompilerParams(vmem_limit_bytes=VMEM_LIMIT),
        cost_estimate=cost(shape[0] * shape[1], 32 * shape[0] * shape[1]),
        name=name,
    )(info, *operands)


def rotation_kernel(sign, in_parts, ring, count, info_ref, *refs):
    outs = refs[-7:-5] if in_parts else refs[-6:-5]
    packed, e_high, e_low, t_high, t_low = refs[-5:]
    half, width = packed.shape
    depth = half // 4
    for k, offset in enumerate((0,) + RINGS):
        at = pl.multiple_of(lax.rem(info_ref[ring] + 4 - offset, 4) * depth, depth)
        if count == 1:
            packed[pl.ds(at, depth), :] = refs[0][k * depth : (k + 1) * depth, :]
        else:
            packed[pl.ds(at, depth), :] = refs[k][...]
    rows = lax.broadcasted_iota(i32, (half, half), 0)
    cols = lax.broadcasted_iota(i32, (half, half), 1)
    triangles = packed[:, :half]
    flipped = -triangles.T
    corner = packed[:, half:]

    def put(r, c, value):
        if sign < 0:
            value = -value
        high, low = split(value)
        e_high[r * half : (r + 1) * half, c * half : (c + 1) * half] = high
        e_low[r * half : (r + 1) * half, c * half : (c + 1) * half] = low

    put(0, 0, jnp.where(rows < cols, triangles, flipped))
    put(1, 1, jnp.where(rows > cols, triangles, flipped))
    put(0, 1, corner)
    put(1, 0, -corner.T)
    tile = 256

    for n in range(width // tile):
        lo, hi = n * tile, (n + 1) * tile
        square = 0.5 * dot3(e_high[:hi, :], e_low[:hi, :], e_high[:, lo:hi], e_low[:, lo:hi])
        t_high[:hi, lo:hi], t_low[:hi, lo:hi] = split(square)
        if n > 0:
            t_high[lo:hi, :lo], t_low[lo:hi, :lo] = split(square[:lo].T)

    def store(r0, r1, c0, c1, value):
        if in_parts:
            outs[0][r0:r1, c0:c1], outs[1][r0:r1, c0:c1] = split(value)
        else:
            outs[0][r0:r1, c0:c1] = value

    for n in range(width // tile):
        lo, hi = n * tile, (n + 1) * tile
        odd = dot3(e_high[:hi, :], e_low[:hi, :], t_high[:, lo:hi], t_low[:, lo:hi])
        odd = odd + (e_high[:hi, lo:hi].astype(f32) + e_low[:hi, lo:hi].astype(f32))
        even = t_high[:hi, lo:hi].astype(f32) + t_low[:hi, lo:hi].astype(f32)
        here = lax.broadcasted_iota(i32, (hi, tile), 0)
        there = lax.broadcasted_iota(i32, (hi, tile), 1) + lo
        store(0, hi, lo, hi, even + odd + jnp.where(here == there, 1.0, 0.0))
        if n > 0:
            store(lo, hi, 0, lo, (even[:lo] - odd[:lo]).T)


def rotation(info, pieces, ring, sign, in_parts, after, name):
    width = pieces[0].shape[1]
    square = (width, width)
    if in_parts:
        shapes = [jax.ShapeDtypeStruct(square, bf16)] * 2
    else:
        shapes = [jax.ShapeDtypeStruct(square, f32)]
    return pl.pallas_call(
        functools.partial(rotation_kernel, sign, in_parts, ring, len(pieces)),
        out_shape=shapes,
        in_specs=[pl.BlockSpec(memory_space=pltpu.SMEM)]
        + [pl.BlockSpec(memory_space=pltpu.VMEM)] * len(pieces)
        + [pl.BlockSpec(memory_space=pl.ANY)] * len(after),
        out_specs=[pl.BlockSpec(memory_space=pltpu.VMEM)] * len(shapes),
        scratch_shapes=[pltpu.VMEM((width // 2, width), f32)] + [pltpu.VMEM(square, bf16)] * 4,
        compiler_params=pltpu.CompilerParams(vmem_limit_bytes=7 * VMEM_LIMIT // 4),
        cost_estimate=cost(12 * width**3, 6 * width * width),
        name=name,
    )(info, *pieces, *after)


def right_kernel(slots, which, info_ref, m_ref, high_ref, low_ref, *refs):
    out_ref = refs[-1]
    width = high_ref.shape[0]
    half = width // 2
    cols = pl.ds(pl.multiple_of(info_ref[which] * half, half), half)
    for k, slot in enumerate(slots):
        rows = pl.ds(pl.multiple_of(info_ref[slot] * width, width), width)
        m_high, m_low = split(m_ref[rows, :])
        out_ref[k * width : (k + 1) * width, :] = dot3(
            m_high, m_low, high_ref[:, cols], low_ref[:, cols]
        )


def right(info, slots, which, matrix, r_high, r_low, after, name):
    width = matrix.shape[1]
    half = width // 2
    return pl.pallas_call(
        functools.partial(right_kernel, slots, which),
        out_shape=jax.ShapeDtypeStruct((len(slots) * width, half), f32),
        in_specs=[pl.BlockSpec(memory_space=pltpu.SMEM)]
        + [pl.BlockSpec(memory_space=pltpu.VMEM)] * 3
        + [pl.BlockSpec(memory_space=pl.ANY)] * len(after),
        out_specs=pl.BlockSpec(memory_space=pltpu.VMEM),
        compiler_params=pltpu.CompilerParams(vmem_limit_bytes=VMEM_LIMIT),
        cost_estimate=cost(3 * len(slots) * width**3, 8 * width * width),
        name=name,
    )(info, matrix, r_high, r_low, *after)


def left_kernel(rows, part_at, info_ref, turned_ref, part_ref, *refs):
    width = turned_ref.shape[0]
    half = width // 2
    at = pl.ds(pl.multiple_of(info_ref[rows] * half, half), half)
    t_high, t_low = split(turned_ref[at, :])
    p_high, p_low = split(part_ref[part_at * width : (part_at + 1) * width, :])
    refs[-1][...] = dot3(t_high, t_low, p_high, p_low)


def left(info, rows, turned, part, part_at, after, name, target=None):
    width = turned.shape[0]
    half = width // 2
    operands = [turned, part] + after
    anywhere = [pl.BlockSpec(memory_space=pl.ANY)] * len(after)
    kernel = functools.partial(left_kernel, rows, part_at)
    limit = VMEM_LIMIT if target is None else 7 * VMEM_LIMIT // 4
    common = dict(
        compiler_params=pltpu.CompilerParams(vmem_limit_bytes=limit),
        cost_estimate=cost(3 * width**3 // 2, 6 * width * width),
        name=name,
    )
    if target is None:
        return pl.pallas_call(
            kernel,
            out_shape=jax.ShapeDtypeStruct((half, half), f32),
            in_specs=[pl.BlockSpec(memory_space=pltpu.SMEM)]
            + [pl.BlockSpec(memory_space=pltpu.VMEM)] * 2
            + anywhere,
            out_specs=pl.BlockSpec(memory_space=pltpu.VMEM),
            **common,
        )(info, *operands)
    row, block, result, shape = target
    aliases = {}
    if result is not None:
        aliases = {1 + len(operands): 0}
        operands.append(result)
        anywhere.append(pl.BlockSpec(memory_space=pl.ANY))
    return pl.pallas_call(
        kernel,
        out_shape=jax.ShapeDtypeStruct(shape, f32),
        grid_spec=pltpu.PrefetchScalarGridSpec(
            num_scalar_prefetch=1,
            grid=(1,),
            in_specs=[
                pl.BlockSpec(turned.shape, lambda i, info: (0, 0)),
                pl.BlockSpec(part.shape, lambda i, info: (0, 0)),
            ]
            + anywhere,
            out_specs=pl.BlockSpec((half, half), lambda i, info: (info[row], info[block])),
        ),
        input_output_aliases=aliases,
        **common,
    )(info, *operands)


def land_kernel(end, info_ref, arrived_ref, own_ref, result_ref, out_ref):
    out_ref[...] = jnp.where(info_ref[end] > 0, own_ref[...], arrived_ref[...])


def land(info, row, block, end, arrived, own, result, name):
    half = arrived.shape[0]
    tile = 256
    per_half = half // tile
    part = pl.BlockSpec((tile, half), lambda i, info: (i, 0))
    return pl.pallas_call(
        functools.partial(land_kernel, end),
        out_shape=jax.ShapeDtypeStruct(result.shape, f32),
        grid_spec=pltpu.PrefetchScalarGridSpec(
            num_scalar_prefetch=1,
            grid=(per_half,),
            in_specs=[part, part, pl.BlockSpec(memory_space=pl.ANY)],
            out_specs=pl.BlockSpec(
                (tile, half), lambda i, info: (info[row] * per_half + i, info[block])
            ),
        ),
        input_output_aliases={3: 0},
        compiler_params=pltpu.CompilerParams(vmem_limit_bytes=VMEM_LIMIT),
        cost_estimate=cost(half * half, 12 * half * half),
        name=name,
    )(info, arrived, own, result)


def group_pairs(group, ring, plane, senders):
    pairs = []
    for row in range(8):
        for col in range(16):
            chip, core = col // 2, col % 2
            if not senders(row, chip):
                continue
            member = row if group == "row" else chip
            member = (member // 4 ^ plane) * 4 + (member + ring) % 4
            target = (member, col) if group == "row" else (row, 2 * member + core)
            pairs.append((row * 16 + col, target[0] * 16 + target[1]))
    return pairs


def is_source(row, chip):
    return row == chip


def in_source_plane(row, chip):
    return row // 4 == chip // 4


def anyone(row, chip):
    return True


def local(matrix):
    row = lax.axis_index("row")
    col = lax.axis_index("col")
    chip = col // 2
    core = col % 2
    rows_here = matrix.shape[0]
    at_end = (col == 0) | (col == 15)
    near_half = jnp.where((core == 1) | (col == 0), 1, 0)
    out_top = jnp.where(row == 0, 0, 1)
    moved_first = jnp.where(core == 0, out_top, 0)
    moved_second = jnp.where(core == 0, 0, out_top)
    values = {
        CORE: core,
        SOURCE: is_source(row, chip),
        SOURCE_PLANE: in_source_plane(row, chip),
        RING_COL: row % 4,
        RING_ROW: chip % 4,
        FAR_FIRST: jnp.where(at_end, core, 1 - core),
        FAR_SECOND: jnp.where(at_end, 1 - core, core),
        FAR_HALF: 1 - near_half,
        NEAR_HALF: near_half,
        NEAR_FIRST: 1 - core,
        NEAR_SECOND: core,
        MOVED_FIRST: moved_first,
        MOVED_SECOND: moved_second,
        STAYS_FIRST: 1 - moved_first,
        STAYS_SECOND: 1 - moved_second,
        KEPT_FIRST: jnp.where(core == 0, 2, 1),
        KEPT_SECOND: jnp.where(core == 0, 1, 2),
        NEAR_BLOCK: 1 - core,
        FAR_BLOCK: core,
        LAND_FIRST: jnp.where(core == 0, 3, 0),
        LAND_SECOND: jnp.where(core == 0, 0, 3),
        END_FIRST: jnp.where(core == 0, row == 7, row == 0),
        END_SECOND: jnp.where(core == 0, row == 0, row == 7),
    }
    info = jnp.stack([jnp.asarray(values[k], i32) for k in range(len(values))])

    own, *quarters = pack(info, matrix)
    arrived = [
        lax.ppermute(quarter, AXES, group_pairs(group, ring, 0, is_source))
        for group in AXES
        for ring, quarter in zip(RINGS, quarters)
    ]
    held = list(small(merge_kernel, info, [own] + arrived, 2, "merge"))
    across = [
        lax.ppermute(one, AXES, group_pairs(group, 0, 1, in_source_plane))
        for group, one in zip(AXES, held)
    ]
    col_own, row_own = small(choose_kernel, info, across + held, 2, "choose")
    col_pieces, row_pieces = (
        [one] + [lax.ppermute(one, AXES, group_pairs(group, ring, 0, anyone)) for ring in RINGS]
        for group, one in zip(AXES, (col_own, row_own))
    )

    swap = [(i, i ^ 1) for i in range(16)]
    row_all = jnp.concatenate(row_pieces, axis=0)
    row_other = lax.ppermute(row_all, "col", swap)

    r_high, r_low = rotation(info, col_pieces, RING_COL, 1, True, [row_all], "column_rotation")
    chips = [(0, 0), (15, 15)]
    chips += [(i, i - 1) for i in range(2, 16, 2)] + [(i, i + 1) for i in range(1, 15, 2)]
    parts = (matrix, r_high, r_low)
    sent = right(info, [FAR_FIRST], FAR_HALF, *parts, [], "right_far_first")
    far_first = lax.ppermute(sent, "col", chips)
    sent = right(info, [NEAR_FIRST, NEAR_SECOND], NEAR_HALF, *parts, [sent], "right_near")
    near = lax.ppermute(sent, "col", swap)
    sent = right(info, [FAR_SECOND], FAR_HALF, *parts, [sent], "right_far_second")
    far_second = lax.ppermute(sent, "col", chips)

    (turned,) = rotation(info, [row_all], RING_ROW, -1, False, [sent], "row_rotation")

    def row_pairs(down_core):
        pairs = []
        for r in range(8):
            for c in range(16):
                target = r - 1 if c % 2 == down_core else r + 1
                if 0 <= target < 8:
                    pairs.append((r * 16 + c, target * 16 + c))
        return pairs

    factors = ((turned, near, 0), (turned, far_first, 0))
    moved, landing, result = [], [], None

    def keep(k, after, result):
        target = (
            (KEPT_FIRST, KEPT_SECOND)[k // 2],
            (NEAR_BLOCK, FAR_BLOCK)[k % 2],
            result,
            (rows_here, matrix.shape[1]),
        )
        rows = (STAYS_FIRST, STAYS_SECOND)[k // 2]
        return left(info, rows, *factors[k], after, "keep_%d" % k, target)

    for k in range(4):
        rows = (MOVED_FIRST, MOVED_SECOND)[k // 2]
        if k == 2:
            (other_turned,) = rotation(
                info, [row_other], RING_ROW, -1, False, moved[1:], "other_row_rotation"
            )
            factors += ((other_turned, near, 1), (other_turned, far_second, 0))
        moved.append(left(info, rows, *factors[k], moved[-1:], "leave_%d" % k))
        landing.append(lax.ppermute(moved[-1], AXES, row_pairs(k // 2)))
    for k in range(4):
        result = keep(k, moved[-1:] if k == 3 else moved[1:2], result)
    for k in range(4):
        result = land(
            info,
            (LAND_FIRST, LAND_SECOND)[k // 2],
            (NEAR_BLOCK, FAR_BLOCK)[k % 2],
            (END_FIRST, END_SECOND)[k // 2],
            landing[k],
            moved[(k + 2) % 4],
            result,
            "land_%d" % k,
        )
    return result


def solution(mesh):
    return jax.shard_map(
        local, mesh=mesh, in_specs=(P("row", "col"),), out_specs=P("row", "col"), check_vma=False
    )
```

time: 420 us -> 242 us (0.58)
  Pallas kernels: 223 us -> 80.8 us
  waiting for transfers between devices: 118 us -> 97.4 us
  between operations: 13.8 us -> 0.61 us
  local copies, waits for them, and re-layouts: 8.3 us -> 3.65 us
    pallas_call x12 -> x21, Pallas kernels: 223 us -> 80.8 us  [the longest x3 33.4 us: rotation(): pl.pallas_call(functools.partial(rotation_kernel, sign, in_parts, ring, l...]
    psum x1 -> x0, waiting for transfers between devices: 36.2 us -> none  [local(): row_packed = lax.psum(masked, 'col', axis_index_groups=alike)]
    ppermute x22, waiting for transfers between devices: 82.1 us -> 97.4 us  [the longest x1 45.5 us: local(): far_second = lax.ppermute(sent, 'col', chips)]
  transfers between devices with their start and end apart: 23 -> 22, of which waited for: 6 -> 5; matrix products, arithmetic and copies ran while one was open for 0% -> 0% of each run, Pallas kernels for 44% -> 23%
where the time goes in v3:
time: 242 us; the launch traced here: 238 us
  waiting for transfers between devices  97.4 us (40%)
  Pallas kernels  80.8 us (33%)
  starting transfers between devices  55.5 us (23%)
  local copies, waits for them, and re-layouts  3.65 us (2%)
    ppermute x1, waiting for transfers between devices, local(): far_second = lax.ppermute(sent, 'col', chips)  45.5 us
    ppermute x2, waiting for transfers between devices, local(): lax.ppermute(one, AXES, group_pairs(group, 0, 1, in_source_plane))  43.2 us
    pallas_call x3, Pallas kernels, rotation(): pl.pallas_call(functools.partial(rotation_kernel, sign, in_parts, ring, l...  33.4 us
    ppermute x6, starting transfers between devices, local(): lax.ppermute(one, AXES, group_pairs(group, ring, 0, anyone))  30.8 us
    pallas_call x3, Pallas kernels, right(): pl.pallas_call(functools.partial(right_kernel, slots, which), out_shape=j...  15.6 us
    pallas_call x4, Pallas kernels, left(): pl.pallas_call(kernel, out_shape=jax.ShapeDtypeStruct(shape, f32), grid_s...  13.4 us
    pallas_call x4, Pallas kernels, left(): pl.pallas_call(kernel, out_shape=jax.ShapeDtypeStruct((half, half), f32),...  9.5 us
    ppermute x4, starting transfers between devices, local(): landing.append(lax.ppermute(moved[-1], AXES, row_pairs(k // 2)))  8.94 us
  transfers between devices with their start and end apart: 22, of which 5 were waited for; matrix products, arithmetic and copies ran while one was open for 0% of the time, Pallas kernels for 23%

profile of v3, /device:TPU:8, one launch (start us, length us, event | category | flops | bytes accessed | tf_op | source)
XLA Modules:
  0.0 238.1 jit_solution(14945267928938579873)
XLA Ops:
  0.0 0.1 stack.102.info_ref
  0.1 0.0 copy-start
  0.1 3.4 %copy-done = f32[2048,1024]{1,0:T(8,128)S(1)} copy-done((f32[2048,1024]{1,0:T(8,128)S(1)}, f32[2048,1024]{1,0:T(8,128)}, u32[]{:S(2)}) %copy-start) | copy-done | bytes 8388632
  3.5 1.3 pack.1
  4.8 0.7 collective-permute-start
  5.5 0.7 collective-permute-start.3
  6.2 0.7 collective-permute-start.1
  6.9 0.7 collective-permute-start.2
  7.6 0.7 collective-permute-start.4
  8.3 0.0 collective-permute-done.refs_0_
  8.3 0.7 collective-permute-start.5
  9.0 0.0 collective-permute-done.1.refs_1_
  9.0 0.0 collective-permute-done.2.refs_2_
  9.0 0.0 collective-permute-done.3.refs_3_
  9.0 0.0 collective-permute-done.5.refs_5_
  9.1 0.0 slice-start.1
  9.1 0.7 merge.1
  9.8 1.4 collective-permute-start.6
  11.2 1.3 collective-permute-start.7
  12.5 36.7 %collective-permute-done.6.refs_0_ = f32[128,1024]{1,0:T(8,128)S(1)} collective-permute-done((f32[128,1024]{1,0:T(8,128)S(1)}, f32[128,1024]{1,0:T(8,128)S(1)}, u32[]{:S(2)}, u32[]{:S(2)}) %collective-permute-start.6) | collective-permute-done | bytes 524320 | tf_op jit(solution)/shard_map/ppermute | solution.py:375
  49.2 6.5 %collective-permute-done.7.refs_1_ = f32[128,1024]{1,0:T(8,128)S(1)} collective-permute-done((f32[128,1024]{1,0:T(8,128)S(1)}, f32[128,1024]{1,0:T(8,128)S(1)}, u32[]{:S(2)}, u32[]{:S(2)}) %collective-permute-start.7) | collective-permute-done | bytes 524320 | tf_op jit(solution)/shard_map/ppermute | solution.py:375
  55.7 0.6 choose.1
  56.4 0.1 collective-permute-start.8
  56.5 3.2 %collective-permute-start.9 = (f32[128,1024]{1,0:T(8,128)S(1)}, f32[128,1024]{1,0:T(8,128)S(1)}, u32[]{:S(2)}, u32[]{:S(2)}) collective-permute-start(f32[128,1024]{1,0:T(8,128)S(1)} %get-tuple-element.21), channel_id=1, source_target_pairs={{0,6},{1,7},{2,0},{3,1},{4,2},{5,3},{6,4},{7,5},{8,14},{9,15},{10,... | collective-permute-start | bytes 1572872 | tf_op jit(solution)/shard_map/ppermute | solution.py:380
  59.7 5.6 %collective-permute-start.10 = (f32[128,1024]{1,0:T(8,128)S(1)}, f32[128,1024]{1,0:T(8,128)S(1)}, u32[]{:S(2)}, u32[]{:S(2)}) collective-permute-start(f32[128,1024]{1,0:T(8,128)S(1)} %get-tuple-element.21), channel_id=1, source_target_pairs={{0,4},{1,5},{2,6},{3,7},{4,0},{5,1},{6,2},{7,3},{8,12},{9,13},{10,... | collective-permute-start | bytes 1572872 | tf_op jit(solution)/shard_map/ppermute | solution.py:380
  65.3 4.2 %collective-permute-start.12 = (f32[128,1024]{1,0:T(8,128)S(1)}, f32[128,1024]{1,0:T(8,128)S(1)}, u32[]{:S(2)}, u32[]{:S(2)}) collective-permute-start(f32[128,1024]{1,0:T(8,128)S(1)} %get-tuple-element.22.refs_0_), channel_id=1, source_target_pairs={{0,16},{1,17},{2,18},{3,19},{4,20},{5,21},{6,22},{7,23},{8,24},{9,... | collective-permute-start | bytes 1572872 | tf_op jit(solution)/shard_map/ppermute | solution.py:380
  69.5 1.2 collective-permute-start.13
  70.8 16.4 %collective-permute-start.14 = (f32[128,1024]{1,0:T(8,128)S(1)}, f32[128,1024]{1,0:T(8,128)S(1)}, u32[]{:S(2)}, u32[]{:S(2)}) collective-permute-start(f32[128,1024]{1,0:T(8,128)S(1)} %get-tuple-element.22.refs_0_), channel_id=1, source_target_pairs={{0,32},{1,33},{2,34},{3,35},{4,36},{5,37},{6,38},{7,39},{8,40},{9,... | collective-permute-start | bytes 1572872 | tf_op jit(solution)/shard_map/ppermute | solution.py:380
  87.3 0.0 collective-permute-done.10
  87.4 0.0 collective-permute-done.12.refs_1_
  87.4 0.0 collective-permute-done.13.refs_2_
  87.4 6.9 %collective-permute-done.14.refs_3_ = f32[128,1024]{1,0:T(8,128)S(1)} collective-permute-done((f32[128,1024]{1,0:T(8,128)S(1)}, f32[128,1024]{1,0:T(8,128)S(1)}, u32[]{:S(2)}, u32[]{:S(2)}) %collective-permute-start.14) | collective-permute-done | bytes 524320 | tf_op jit(solution)/shard_map/ppermute | solution.py:380
  94.3 11.2 %column_rotation.1 = (bf16[1024,1024]{1,0:T(8,128)(2,1)S(1)}, bf16[1024,1024]{1,0:T(8,128)(2,1)S(1)}) custom-call(s32[23]{0:T(128)S(1)} %stack.102.info_ref, f32[128,1024]{1,0:T(8,128)S(1)} %get-tuple-element.22.refs_0_, f32[128,1024]{1,0:T(8,128)S(1)} %collective-permute-done.12.refs_1_, f32[128,1024]{1,0:T(8,128)S(1)} %collective-permute-done.13.refs_2_, ...), custom_call_target="tpu_custom_call" | custom-call | flops 201326592 | bytes 98304 | tf_op jit(solution)/shard_map/column_rotation/pallas_call | solution.py:178
  105.6 4.0 %right_far_first.1.refs_0_ = f32[1024,512]{1,0:T(8,128)S(1)} custom-call(s32[23]{0:T(128)S(1)} %stack.102.info_ref, f32[2048,1024]{1,0:T(8,128)S(1)} %bitcast.21, bf16[1024,1024]{1,0:T(8,128)(2,1)S(1)} %get-tuple-element.23.high_ref, bf16[1024,1024]{1,0:T(8,128)(2,1)S(1)} %get-tuple-element.24.low_ref), custom_call_target="tpu_custom_call" | custom-call | flops 50331648 | bytes 131072 | tf_op jit(solution)/shard_map/right_far_first/pallas_call | solution.py:208
  109.5 7.6 %right_near.1.refs_0_ = f32[2048,512]{1,0:T(8,128)S(1)} custom-call(s32[23]{0:T(128)S(1)} %stack.102.info_ref, f32[2048,1024]{1,0:T(8,128)S(1)} %bitcast.21, bf16[1024,1024]{1,0:T(8,128)(2,1)S(1)} %get-tuple-element.23.high_ref, bf16[1024,1024]{1,0:T(8,128)(2,1)S(1)} %get-tuple-element.24.low_ref, f32[1024,512]{1,0:T(8,128)S(1)} %right_far_first.1.refs_0_), custom_call_target="tpu_custom_call" | custom-call | flops 100663296 | bytes 131072 | tf_op jit(solution)/shard_map/right_near/pallas_call | solution.py:208
  117.2 0.1 collective-permute-start.16
  117.3 1.9 collective-permute-start.15
  119.2 2.9 %collective-permute-start.11 = (f32[512,1024]{1,0:T(8,128)S(1)}, f32[512,1024]{1,0:T(8,128)S(1)}, u32[]{:S(2)}, u32[]{:S(2)}) collective-permute-start(f32[512,1024]{1,0:T(8,128)S(1)} %constant_dynamic-update-slice_fusion.refs_4_.refs_0_), channel_id=1, source_target_pairs={{0,1},{1,0},{2,3},{3,2},{4,5},{5,4},{6,7},{7,6},{8,9},{9,8},{10,11... | collective-permute-start | bytes 6291464 | tf_op jit(solution)/shard_map/ppermute | solution.py:386
  122.1 4.0 %right_far_second.1.refs_1_ = f32[1024,512]{1,0:T(8,128)S(1)} custom-call(s32[23]{0:T(128)S(1)} %stack.102.info_ref, f32[2048,1024]{1,0:T(8,128)S(1)} %bitcast.21, bf16[1024,1024]{1,0:T(8,128)(2,1)S(1)} %get-tuple-element.23.high_ref, bf16[1024,1024]{1,0:T(8,128)(2,1)S(1)} %get-tuple-element.24.low_ref, f32[2048,512]{1,0:T(8,128)S(1)} %right_near.1.refs_0_), custom_call_target="tpu_custom_call" | custom-call | flops 50331648 | bytes 131072 | tf_op jit(solution)/shard_map/right_far_second/pallas_call | solution.py:208
  126.1 4.1 %collective-permute-start.17 = (f32[1024,512]{1,0:T(8,128)S(1)}, f32[1024,512]{1,0:T(8,128)S(1)}, u32[]{:S(2)}, u32[]{:S(2)}) collective-permute-start(f32[1024,512]{1,0:T(8,128)S(1)} %right_far_second.1.refs_1_), channel_id=1, source_target_pairs={{0,0},{15,15},{2,1},{4,3},{6,5},{8,7},{10,9},{12,11},{14,13},{1,2}... | collective-permute-start | bytes 6291464 | tf_op jit(solution)/shard_map/ppermute | solution.py:397
  130.1 11.1 %row_rotation.1.turned_ref = f32[1024,1024]{1,0:T(8,128)S(1)} custom-call(s32[23]{0:T(128)S(1)} %stack.102.info_ref, f32[512,1024]{1,0:T(8,128)S(1)} %constant_dynamic-update-slice_fusion.refs_4_.refs_0_, f32[1024,512]{1,0:T(8,128)S(1)} %right_far_second.1.refs_1_), custom_call_target="tpu_custom_call" | custom-call | flops 201326592 | bytes 98304 | tf_op jit(solution)/shard_map/row_rotation/pallas_call | solution.py:178
  141.2 0.0 collective-permute-done.16.part_ref
  141.2 2.4 leave_0.1.refs_0_.own_ref
  143.6 1.3 collective-permute-start.21
  144.9 1.8 collective-permute-done.15.part_ref
  146.7 2.4 leave_1.1.refs_1_.refs_0_.own_ref
  149.1 1.5 collective-permute-start.20
  150.6 0.0 collective-permute-done.11.refs_0_
  150.6 11.1 %other_row_rotation.1.turned_ref = f32[1024,1024]{1,0:T(8,128)S(1)} custom-call(s32[23]{0:T(128)S(1)} %stack.102.info_ref, f32[512,1024]{1,0:T(8,128)S(1)} %collective-permute-done.11.refs_0_, f32[512,512]{1,0:T(8,128)S(1)} %leave_1.1.refs_1_.refs_0_.own_ref), custom_call_target="tpu_custom_call" | custom-call | flops 201326592 | bytes 98304 | tf_op jit(solution)/shard_map/other_row_rotation/pallas_call | solution.py:178
  161.7 2.4 leave_2.1.refs_0_.own_ref
  164.1 4.6 %collective-permute-start.19 = (f32[512,512]{1,0:T(8,128)S(1)}, f32[512,512]{1,0:T(8,128)S(1)}, u32[]{:S(2)}, u32[]{:S(2)}) collective-permute-start(f32[512,512]{1,0:T(8,128)S(1)} %leave_2.1.refs_0_.own_ref), channel_id=1, source_target_pairs={{0,16},{2,18},{4,20},{6,22},{8,24},{10,26},{12,28},{14,30},{16,32}... | collective-permute-start | bytes 3145736 | tf_op jit(solution)/shard_map/ppermute | solution.py:431
  168.7 45.5 %collective-permute-done.17.part_ref = f32[1024,512]{1,0:T(8,128)S(1)} collective-permute-done((f32[1024,512]{1,0:T(8,128)S(1)}, f32[1024,512]{1,0:T(8,128)S(1)}, u32[]{:S(2)}, u32[]{:S(2)}) %collective-permute-start.17) | collective-permute-done | bytes 2097184 | tf_op jit(solution)/shard_map/ppermute | solution.py:397
  214.2 2.4 leave_3.1.refs_0_.own_ref
  216.5 1.6 collective-permute-start.18
  218.1 3.3 %keep_0.1.refs_1_ = f32[2048,1024]{1,0:T(8,128)} custom-call(s32[23]{0:T(128)S(1)} %stack.102.info_ref, f32[1024,1024]{1,0:T(8,128)S(1)} %row_rotation.1.turned_ref, f32[2048,512]{1,0:T(8,128)S(1)} %collective-permute-done.16.part_ref, f32[512,512]{1,0:T(8,128)S(1)} %leave_1.1.refs_1_.refs_0_.own_ref), custom_call_target="tpu_custom_call" | custom-call | flops 25165824 | bytes 98304 | tf_op jit(solution)/shard_map/keep_0/pallas_call | solution.py:258
  221.5 3.3 %keep_1.1.refs_1_ = f32[2048,1024]{1,0:T(8,128)} custom-call(s32[23]{0:T(128)S(1)} %stack.102.info_ref, f32[1024,1024]{1,0:T(8,128)S(1)} %row_rotation.1.turned_ref, f32[1024,512]{1,0:T(8,128)S(1)} %collective-permute-done.15.part_ref, f32[512,512]{1,0:T(8,128)S(1)} %leave_1.1.refs_1_.refs_0_.own_ref, ...), custom_call_target="tpu_custom_call", output_to_operand_aliasing={{}: (4, {})} | custom-call | flops 25165824 | bytes 98304 | tf_op jit(solution)/shard_map/keep_1/pallas_call | solution.py:258
  224.8 3.3 %keep_2.1.refs_1_ = f32[2048,1024]{1,0:T(8,128)} custom-call(s32[23]{0:T(128)S(1)} %stack.102.info_ref, f32[1024,1024]{1,0:T(8,128)S(1)} %other_row_rotation.1.turned_ref, f32[2048,512]{1,0:T(8,128)S(1)} %collective-permute-done.16.part_ref, f32[512,512]{1,0:T(8,128)S(1)} %leave_1.1.refs_1_.refs_0_.own_ref, ...), custom_call_target="tpu_custom_call", output_to_operand_aliasing={{}: (4, {})} | custom-call | flops 25165824 | bytes 98304 | tf_op jit(solution)/shard_map/keep_2/pallas_call | solution.py:258
  228.1 3.3 %keep_3.1.result_ref = f32[2048,1024]{1,0:T(8,128)} custom-call(s32[23]{0:T(128)S(1)} %stack.102.info_ref, f32[1024,1024]{1,0:T(8,128)S(1)} %other_row_rotation.1.turned_ref, f32[1024,512]{1,0:T(8,128)S(1)} %collective-permute-done.17.part_ref, f32[512,512]{1,0:T(8,128)S(1)} %leave_3.1.refs_0_.own_ref, ...), custom_call_target="tpu_custom_call", output_to_operand_aliasing={{}: (4, {})} | custom-call | flops 25165824 | bytes 98304 | tf_op jit(solution)/shard_map/keep_3/pallas_call | solution.py:258
  231.5 1.6 land_0.1.result_ref
  233.1 0.0 collective-permute-done.20.arrived_ref
  233.1 1.6 land_1.1.result_ref
  234.7 0.0 collective-permute-done.19.arrived_ref
  234.7 1.6 land_2.1.result_ref
  236.3 1.6 land_3.1
  (13 shorter events, 0.2 us)
Async XLA Ops:
  0.1 3.4 %copy-start = (f32[2048,1024]{1,0:T(8,128)S(1)}, f32[2048,1024]{1,0:T(8,128)}, u32[]{:S(2)}) copy-start(f32[2048,1024]{1,0:T(8,128)} %m_ref.5) | copy-start | bytes 25165828
  3.5 102.1 %slice-start = ((s8[8388608]{0:T(1024)(128)(4,1)}), s8[4194304]{0:T(1024)(128)(4,1)S(1)}, s32[]{:S(2)}) async-start(s8[8388608]{0:T(1024)(128)(4,1)} %bitcast.20), calls=%async_computation | async-start | bytes 8388608
  4.8 3.5 %collective-permute-start = (f32[128,1024]{1,0:T(8,128)S(1)}, f32[128,1024]{1,0:T(8,128)S(1)}, u32[]{:S(2)}, u32[]{:S(2)}) collective-permute-start(f32[128,1024]{1,0:T(8,128)S(1)} %get-tuple-element.16), channel_id=1, source_target_pairs={{0,16},{1,17},{18,34},{19,35},{36,52},{37,53},{54,6},{55,7},{72,88... | collective-permute-start | bytes 1572872 | tf_op jit(solution)/shard_map/ppermute | solution.py:369
  5.5 3.5 %collective-permute-start.3 = (f32[128,1024]{1,0:T(8,128)S(1)}, f32[128,1024]{1,0:T(8,128)S(1)}, u32[]{:S(2)}, u32[]{:S(2)}) collective-permute-start(f32[128,1024]{1,0:T(8,128)S(1)} %get-tuple-element.16), channel_id=1, source_target_pairs={{0,2},{1,3},{18,20},{19,21},{36,38},{37,39},{54,48},{55,49},{72,74... | collective-permute-start | bytes 1572872 | tf_op jit(solution)/shard_map/ppermute | solution.py:369
  6.2 2.8 %collective-permute-start.1 = (f32[128,1024]{1,0:T(8,128)S(1)}, f32[128,1024]{1,0:T(8,128)S(1)}, u32[]{:S(2)}, u32[]{:S(2)}) collective-permute-start(f32[128,1024]{1,0:T(8,128)S(1)} %get-tuple-element.17), channel_id=1, source_target_pairs={{0,48},{1,49},{18,2},{19,3},{36,20},{37,21},{54,38},{55,39},{72,12... | collective-permute-start | bytes 1572872 | tf_op jit(solution)/shard_map/ppermute | solution.py:369
  6.9 2.1 collective-permute-start.2
  7.6 1.4 collective-permute-start.4
  8.3 0.7 collective-permute-start.5
  9.1 96.5 %slice-start.1 = ((s8[8388608]{0:T(1024)(128)(4,1)}), s8[4194304]{0:T(1024)(128)(4,1)S(1)}, s32[]{:S(2)}) async-start(s8[8388608]{0:T(1024)(128)(4,1)} %bitcast.20), calls=%async_computation.1 | async-start | bytes 8388608
  9.8 39.4 %collective-permute-start.6 = (f32[128,1024]{1,0:T(8,128)S(1)}, f32[128,1024]{1,0:T(8,128)S(1)}, u32[]{:S(2)}, u32[]{:S(2)}) collective-permute-start(f32[128,1024]{1,0:T(8,128)S(1)} %get-tuple-element.19.refs_2_), channel_id=1, source_target_pairs={{0,64},{1,65},{2,66},{3,67},{4,68},{5,69},{6,70},{7,71},{16,80},{1... | collective-permute-start | bytes 1572872 | tf_op jit(solution)/shard_map/ppermute | solution.py:375
  11.2 44.5 %collective-permute-start.7 = (f32[128,1024]{1,0:T(8,128)S(1)}, f32[128,1024]{1,0:T(8,128)S(1)}, u32[]{:S(2)}, u32[]{:S(2)}) collective-permute-start(f32[128,1024]{1,0:T(8,128)S(1)} %get-tuple-element.20.refs_3_), channel_id=1, source_target_pairs={{0,8},{1,9},{2,10},{3,11},{4,12},{5,13},{6,14},{7,15},{16,24},{17,... | collective-permute-start | bytes 1572872 | tf_op jit(solution)/shard_map/ppermute | solution.py:375
  56.4 14.4 %collective-permute-start.8 = (f32[128,1024]{1,0:T(8,128)S(1)}, f32[128,1024]{1,0:T(8,128)S(1)}, u32[]{:S(2)}, u32[]{:S(2)}) collective-permute-start(f32[128,1024]{1,0:T(8,128)S(1)} %get-tuple-element.21), channel_id=1, source_target_pairs={{0,2},{1,3},{2,4},{3,5},{4,6},{5,7},{6,0},{7,1},{8,10},{9,11},{10,... | collective-permute-start | bytes 1572872 | tf_op jit(solution)/shard_map/ppermute | solution.py:380
  56.5 30.8 %collective-permute-start.9 = (f32[128,1024]{1,0:T(8,128)S(1)}, f32[128,1024]{1,0:T(8,128)S(1)}, u32[]{:S(2)}, u32[]{:S(2)}) collective-permute-start(f32[128,1024]{1,0:T(8,128)S(1)} %get-tuple-element.21), channel_id=1, source_target_pairs={{0,6},{1,7},{2,0},{3,1},{4,2},{5,3},{6,4},{7,5},{8,14},{9,15},{10,... | collective-permute-start | bytes 1572872 | tf_op jit(solution)/shard_map/ppermute | solution.py:380
  59.7 27.7 %collective-permute-start.10 = (f32[128,1024]{1,0:T(8,128)S(1)}, f32[128,1024]{1,0:T(8,128)S(1)}, u32[]{:S(2)}, u32[]{:S(2)}) collective-permute-start(f32[128,1024]{1,0:T(8,128)S(1)} %get-tuple-element.21), channel_id=1, source_target_pairs={{0,4},{1,5},{2,6},{3,7},{4,0},{5,1},{6,2},{7,3},{8,12},{9,13},{10,... | collective-permute-start | bytes 1572872 | tf_op jit(solution)/shard_map/ppermute | solution.py:380
  65.3 22.1 %collective-permute-start.12 = (f32[128,1024]{1,0:T(8,128)S(1)}, f32[128,1024]{1,0:T(8,128)S(1)}, u32[]{:S(2)}, u32[]{:S(2)}) collective-permute-start(f32[128,1024]{1,0:T(8,128)S(1)} %get-tuple-element.22.refs_0_), channel_id=1, source_target_pairs={{0,16},{1,17},{2,18},{3,19},{4,20},{5,21},{6,22},{7,23},{8,24},{9,... | collective-permute-start | bytes 1572872 | tf_op jit(solution)/shard_map/ppermute | solution.py:380
  69.5 17.9 %collective-permute-start.13 = (f32[128,1024]{1,0:T(8,128)S(1)}, f32[128,1024]{1,0:T(8,128)S(1)}, u32[]{:S(2)}, u32[]{:S(2)}) collective-permute-start(f32[128,1024]{1,0:T(8,128)S(1)} %get-tuple-element.22.refs_0_), channel_id=1, source_target_pairs={{0,48},{1,49},{2,50},{3,51},{4,52},{5,53},{6,54},{7,55},{8,56},{9,... | collective-permute-start | bytes 1572872 | tf_op jit(solution)/shard_map/ppermute | solution.py:380
  70.8 23.6 %collective-permute-start.14 = (f32[128,1024]{1,0:T(8,128)S(1)}, f32[128,1024]{1,0:T(8,128)S(1)}, u32[]{:S(2)}, u32[]{:S(2)}) collective-permute-start(f32[128,1024]{1,0:T(8,128)S(1)} %get-tuple-element.22.refs_0_), channel_id=1, source_target_pairs={{0,32},{1,33},{2,34},{3,35},{4,36},{5,37},{6,38},{7,39},{8,40},{9,... | collective-permute-start | bytes 1572872 | tf_op jit(solution)/shard_map/ppermute | solution.py:380
  117.2 24.0 %collective-permute-start.16 = (f32[2048,512]{1,0:T(8,128)S(1)}, f32[2048,512]{1,0:T(8,128)S(1)}, u32[]{:S(2)}, u32[]{:S(2)}) collective-permute-start(f32[2048,512]{1,0:T(8,128)S(1)} %right_near.1.refs_0_), channel_id=1, source_target_pairs={{0,1},{1,0},{2,3},{3,2},{4,5},{5,4},{6,7},{7,6},{8,9},{9,8},{10,11... | collective-permute-start | bytes 12582920 | tf_op jit(solution)/shard_map/ppermute | solution.py:395
  117.3 29.5 %collective-permute-start.15 = (f32[1024,512]{1,0:T(8,128)S(1)}, f32[1024,512]{1,0:T(8,128)S(1)}, u32[]{:S(2)}, u32[]{:S(2)}) collective-permute-start(f32[1024,512]{1,0:T(8,128)S(1)} %right_far_first.1.refs_0_), channel_id=1, source_target_pairs={{0,0},{15,15},{2,1},{4,3},{6,5},{8,7},{10,9},{12,11},{14,13},{1,2}... | collective-permute-start | bytes 6291464 | tf_op jit(solution)/shard_map/ppermute | solution.py:393
  119.2 31.4 %collective-permute-start.11 = (f32[512,1024]{1,0:T(8,128)S(1)}, f32[512,1024]{1,0:T(8,128)S(1)}, u32[]{:S(2)}, u32[]{:S(2)}) collective-permute-start(f32[512,1024]{1,0:T(8,128)S(1)} %constant_dynamic-update-slice_fusion.refs_4_.refs_0_), channel_id=1, source_target_pairs={{0,1},{1,0},{2,3},{3,2},{4,5},{5,4},{6,7},{7,6},{8,9},{9,8},{10,11... | collective-permute-start | bytes 6291464 | tf_op jit(solution)/shard_map/ppermute | solution.py:386
  126.1 88.1 %collective-permute-start.17 = (f32[1024,512]{1,0:T(8,128)S(1)}, f32[1024,512]{1,0:T(8,128)S(1)}, u32[]{:S(2)}, u32[]{:S(2)}) collective-permute-start(f32[1024,512]{1,0:T(8,128)S(1)} %right_far_second.1.refs_1_), channel_id=1, source_target_pairs={{0,0},{15,15},{2,1},{4,3},{6,5},{8,7},{10,9},{12,11},{14,13},{1,2}... | collective-permute-start | bytes 6291464 | tf_op jit(solution)/shard_map/ppermute | solution.py:397
  143.6 87.9 %collective-permute-start.21 = (f32[512,512]{1,0:T(8,128)S(1)}, f32[512,512]{1,0:T(8,128)S(1)}, u32[]{:S(2)}, u32[]{:S(2)}) collective-permute-start(f32[512,512]{1,0:T(8,128)S(1)} %leave_0.1.refs_0_.own_ref), channel_id=1, source_target_pairs={{1,17},{3,19},{5,21},{7,23},{9,25},{11,27},{13,29},{15,31},{16,0},... | collective-permute-start | bytes 3145736 | tf_op jit(solution)/shard_map/ppermute | solution.py:431
  149.1 84.0 %collective-permute-start.20 = (f32[512,512]{1,0:T(8,128)S(1)}, f32[512,512]{1,0:T(8,128)S(1)}, u32[]{:S(2)}, u32[]{:S(2)}) collective-permute-start(f32[512,512]{1,0:T(8,128)S(1)} %leave_1.1.refs_1_.refs_0_.own_ref), channel_id=1, source_target_pairs={{1,17},{3,19},{5,21},{7,23},{9,25},{11,27},{13,29},{15,31},{16,0},... | collective-permute-start | bytes 3145736 | tf_op jit(solution)/shard_map/ppermute | solution.py:431
  164.1 70.6 %collective-permute-start.19 = (f32[512,512]{1,0:T(8,128)S(1)}, f32[512,512]{1,0:T(8,128)S(1)}, u32[]{:S(2)}, u32[]{:S(2)}) collective-permute-start(f32[512,512]{1,0:T(8,128)S(1)} %leave_2.1.refs_0_.own_ref), channel_id=1, source_target_pairs={{0,16},{2,18},{4,20},{6,22},{8,24},{10,26},{12,28},{14,30},{16,32}... | collective-permute-start | bytes 3145736 | tf_op jit(solution)/shard_map/ppermute | solution.py:431
  216.5 19.7 %collective-permute-start.18 = (f32[512,512]{1,0:T(8,128)S(1)}, f32[512,512]{1,0:T(8,128)S(1)}, u32[]{:S(2)}, u32[]{:S(2)}) collective-permute-start(f32[512,512]{1,0:T(8,128)S(1)} %leave_3.1.refs_0_.own_ref), channel_id=1, source_target_pairs={{0,16},{2,18},{4,20},{6,22},{8,24},{10,26},{12,28},{14,30},{16,32}... | collective-permute-start | bytes 3145736 | tf_op jit(solution)/shard_map/ppermute | solution.py:431

commit v4 on v3

--- a/solution.py
+++ b/solution.py
@@ -93,10 +93,11 @@
         refs[6 + group][...] = jnp.where(info_ref[SOURCE] > 0, own[...], total)
 
 
-def choose_kernel(info_ref, *refs):
-    for group in range(2):
-        across, held, out = refs[group], refs[2 + group], refs[4 + group]
-        out[...] = jnp.where(info_ref[SOURCE_PLANE] > 0, held[...], across[...])
+def choose_kernel(info_ref, across, held, *refs):
+    outs = refs[len(refs) // 2 :]
+    outs[0][...] = jnp.where(info_ref[SOURCE_PLANE] > 0, held[...], across[...])
+    if len(refs) > 1:
+        outs[1][...] = refs[0][...]
 
 
 def small(kernel, info, operands, outs, name):
@@ -189,42 +190,47 @@
     )(info, *pieces, *after)
 
 
-def right_kernel(slots, which, info_ref, m_ref, high_ref, low_ref, *refs):
-    out_ref = refs[-1]
+def right_kernel(jobs, info_ref, m_ref, high_ref, low_ref, *refs):
     width = high_ref.shape[0]
     half = width // 2
-    cols = pl.ds(pl.multiple_of(info_ref[which] * half, half), half)
-    for k, slot in enumerate(slots):
-        rows = pl.ds(pl.multiple_of(info_ref[slot] * width, width), width)
-        m_high, m_low = split(m_ref[rows, :])
-        out_ref[k * width : (k + 1) * width, :] = dot3(
-            m_high, m_low, high_ref[:, cols], low_ref[:, cols]
-        )
-
-
-def right(info, slots, which, matrix, r_high, r_low, after, name):
+    for (slots, which), out_ref in zip(jobs, refs[-len(jobs) :]):
+        cols = pl.ds(pl.multiple_of(info_ref[which] * half, half), half)
+        for k, slot in enumerate(slots):
+            rows = pl.ds(pl.multiple_of(info_ref[slot] * width, width), width)
+            m_high, m_low = split(m_ref[rows, :])
+            out_ref[k * width : (k + 1) * width, :] = dot3(
+                m_high, m_low, high_ref[:, cols], low_ref[:, cols]
+            )
+
+
+def right(info, jobs, matrix, r_high, r_low, after, name):
     width = matrix.shape[1]
     half = width // 2
     return pl.pallas_call(
-        functools.partial(right_kernel, slots, which),
-        out_shape=jax.ShapeDtypeStruct((len(slots) * width, half), f32),
+        functools.partial(right_kernel, jobs),
+        out_shape=[jax.ShapeDtypeStruct((len(slots) * width, half), f32) for slots, _ in jobs],
         in_specs=[pl.BlockSpec(memory_space=pltpu.SMEM)]
         + [pl.BlockSpec(memory_space=pltpu.VMEM)] * 3
         + [pl.BlockSpec(memory_space=pl.ANY)] * len(after),
-        out_specs=pl.BlockSpec(memory_space=pltpu.VMEM),
+        out_specs=[pl.BlockSpec(memory_space=pltpu.VMEM)] * len(jobs),
         compiler_params=pltpu.CompilerParams(vmem_limit_bytes=VMEM_LIMIT),
-        cost_estimate=cost(3 * len(slots) * width**3, 8 * width * width),
+        cost_estimate=cost(9 * width**3, 8 * width * width),
         name=name,
     )(info, matrix, r_high, r_low, *after)
 
 
-def left_kernel(rows, part_at, info_ref, turned_ref, part_ref, *refs):
+def left_kernel(rows, part_at, to_result, info_ref, turned_ref, part_ref, *refs):
     width = turned_ref.shape[0]
     half = width // 2
     at = pl.ds(pl.multiple_of(info_ref[rows] * half, half), half)
     t_high, t_low = split(turned_ref[at, :])
     p_high, p_low = split(part_ref[part_at * width : (part_at + 1) * width, :])
-    refs[-1][...] = dot3(t_high, t_low, p_high, p_low)
+    value = dot3(t_high, t_low, p_high, p_low)
+    if to_result:
+        refs[-2][...] = value
+        refs[-1][...] = jnp.zeros_like(refs[-1])
+    else:
+        refs[-1][...] = value
 
 
 def left(info, rows, turned, part, part_at, after, name, target=None):
@@ -232,7 +238,7 @@
     half = width // 2
     operands = [turned, part] + after
     anywhere = [pl.BlockSpec(memory_space=pl.ANY)] * len(after)
-    kernel = functools.partial(left_kernel, rows, part_at)
+    kernel = functools.partial(left_kernel, rows, part_at, target is not None)
     limit = VMEM_LIMIT if target is None else 7 * VMEM_LIMIT // 4
     common = dict(
         compiler_params=pltpu.CompilerParams(vmem_limit_bytes=limit),
@@ -257,7 +263,7 @@
         anywhere.append(pl.BlockSpec(memory_space=pl.ANY))
     return pl.pallas_call(
         kernel,
-        out_shape=jax.ShapeDtypeStruct(shape, f32),
+        out_shape=[jax.ShapeDtypeStruct(shape, f32), jax.ShapeDtypeStruct((8, 128), f32)],
         grid_spec=pltpu.PrefetchScalarGridSpec(
             num_scalar_prefetch=1,
             grid=(1,),
@@ -266,7 +272,10 @@
                 pl.BlockSpec(part.shape, lambda i, info: (0, 0)),
             ]
             + anywhere,
-            out_specs=pl.BlockSpec((half, half), lambda i, info: (info[row], info[block])),
+            out_specs=[
+                pl.BlockSpec((half, half), lambda i, info: (info[row], info[block])),
+                pl.BlockSpec((8, 128), lambda i, info: (0, 0)),
+            ],
         ),
         input_output_aliases=aliases,
         **common,
@@ -371,32 +380,25 @@
         for ring, quarter in zip(RINGS, quarters)
     ]
     held = list(small(merge_kernel, info, [own] + arrived, 2, "merge"))
-    across = [
-        lax.ppermute(one, AXES, group_pairs(group, 0, 1, in_source_plane))
-        for group, one in zip(AXES, held)
-    ]
-    col_own, row_own = small(choose_kernel, info, across + held, 2, "choose")
-    col_pieces, row_pieces = (
-        [one] + [lax.ppermute(one, AXES, group_pairs(group, ring, 0, anyone)) for ring in RINGS]
-        for group, one in zip(AXES, (col_own, row_own))
+    def cross(group, one):
+        return lax.ppermute(one, AXES, group_pairs(group, 0, 1, in_source_plane))
+
+    def around(group, one):
+        return [one] + [
+            lax.ppermute(one, AXES, group_pairs(group, ring, 0, anyone)) for ring in RINGS
+        ]
+
+    col_held, row_held = held
+    col_own, row_held = small(
+        choose_kernel, info, [cross("row", col_held), col_held, row_held], 2, "choose_col"
     )
+    col_pieces = around("row", col_own)
+    (row_own,) = small(choose_kernel, info, [cross("col", row_held), row_held], 1, "choose_row")
+    row_pieces = around("col", row_own)
 
     swap = [(i, i ^ 1) for i in range(16)]
-    row_all = jnp.concatenate(row_pieces, axis=0)
-    row_other = lax.ppermute(row_all, "col", swap)
-
-    r_high, r_low = rotation(info, col_pieces, RING_COL, 1, True, [row_all], "column_rotation")
     chips = [(0, 0), (15, 15)]
     chips += [(i, i - 1) for i in range(2, 16, 2)] + [(i, i + 1) for i in range(1, 15, 2)]
-    parts = (matrix, r_high, r_low)
-    sent = right(info, [FAR_FIRST], FAR_HALF, *parts, [], "right_far_first")
-    far_first = lax.ppermute(sent, "col", chips)
-    sent = right(info, [NEAR_FIRST, NEAR_SECOND], NEAR_HALF, *parts, [sent], "right_near")
-    near = lax.ppermute(sent, "col", swap)
-    sent = right(info, [FAR_SECOND], FAR_HALF, *parts, [sent], "right_far_second")
-    far_second = lax.ppermute(sent, "col", chips)
-
-    (turned,) = rotation(info, [row_all], RING_ROW, -1, False, [sent], "row_rotation")
 
     def row_pairs(down_core):
         pairs = []
@@ -407,10 +409,12 @@
                     pairs.append((r * 16 + c, target * 16 + c))
         return pairs
 
-    factors = ((turned, near, 0), (turned, far_first, 0))
-    moved, landing, result = [], [], None
-
-    def keep(k, after, result):
+    def leave(k, turned, part, part_at, after):
+        rows = (MOVED_FIRST, MOVED_SECOND)[k // 2]
+        moved = left(info, rows, turned, part, part_at, after, "leave_%d" % k)
+        return moved, lax.ppermute(moved, AXES, row_pairs(k // 2))
+
+    def keep(k, turned, part, part_at, after, result):
         target = (
             (KEPT_FIRST, KEPT_SECOND)[k // 2],
             (NEAR_BLOCK, FAR_BLOCK)[k % 2],
@@ -418,19 +422,37 @@
             (rows_here, matrix.shape[1]),
         )
         rows = (STAYS_FIRST, STAYS_SECOND)[k // 2]
-        return left(info, rows, *factors[k], after, "keep_%d" % k, target)
-
-    for k in range(4):
-        rows = (MOVED_FIRST, MOVED_SECOND)[k // 2]
-        if k == 2:
-            (other_turned,) = rotation(
-                info, [row_other], RING_ROW, -1, False, moved[1:], "other_row_rotation"
-            )
-            factors += ((other_turned, near, 1), (other_turned, far_second, 0))
-        moved.append(left(info, rows, *factors[k], moved[-1:], "leave_%d" % k))
-        landing.append(lax.ppermute(moved[-1], AXES, row_pairs(k // 2)))
-    for k in range(4):
-        result = keep(k, moved[-1:] if k == 3 else moved[1:2], result)
+        return left(info, rows, turned, part, part_at, after, "keep_%d" % k, target)
+
+    row_all = jnp.concatenate(row_pieces, axis=0)
+    row_other = lax.ppermute(row_all, "col", swap)
+    r_high, r_low = rotation(info, col_pieces, RING_COL, 1, True, [row_own], "column_rotation")
+    factors = (matrix, r_high, r_low)
+    parts = []
+    for slot, which, name in (
+        (FAR_FIRST, FAR_HALF, "right_far_first"),
+        (FAR_SECOND, FAR_HALF, "right_far_second"),
+        (NEAR_FIRST, NEAR_HALF, "right_near_first"),
+        (NEAR_SECOND, NEAR_HALF, "right_near_second"),
+    ):
+        after = parts[-1:] if parts else [row_all]
+        (sent,) = right(info, [([slot], which)], *factors, after, name)
+        parts.append(sent)
+    far_first, far_second = (lax.ppermute(part, "col", chips) for part in parts[:2])
+    near_first, near_second = (lax.ppermute(part, "col", swap) for part in parts[2:])
+    (turned,) = rotation(info, [row_all], RING_ROW, -1, False, parts[3:], "row_rotation")
+    moved, landing = [None] * 4, [None] * 4
+    moved[1], landing[1] = leave(1, turned, far_first, 0, [])
+    moved[0], landing[0] = leave(0, turned, near_first, 0, [moved[1]])
+    (other_turned,) = rotation(
+        info, [row_other], RING_ROW, -1, False, [moved[0]], "other_row_rotation"
+    )
+    moved[2], landing[2] = leave(2, other_turned, near_second, 0, [])
+    result, _ = keep(0, turned, near_first, 0, [moved[2]], None)
+    result, _ = keep(1, turned, far_first, 0, [], result)
+    result, token = keep(2, other_turned, near_second, 0, [], result)
+    moved[3], landing[3] = leave(3, other_turned, far_second, 0, [token])
+    result, _ = keep(3, other_turned, far_second, 0, [moved[3]], result)
     for k in range(4):
         result = land(
             info,

time: 242 us -> 219 us (0.905)
  the two profiles are of different devices: /device:TPU:8 before, /device:TPU:30 now
where the time goes in v4:
time: 219 us; the launch traced here: 214 us
  Pallas kernels  81.9 us (37%)
  waiting for transfers between devices  69.3 us (32%)
  starting transfers between devices  59 us (27%)
  local copies, waits for them, and re-layouts  3.48 us (2%)
    pallas_call x3, Pallas kernels, rotation(): pl.pallas_call(functools.partial(rotation_kernel, sign, in_parts, ring, l...  33.4 us
    ppermute x2, waiting for transfers between devices, local(): lax.ppermute(part, 'col', chips)  31.5 us
    ppermute x6, starting transfers between devices, around(): lax.ppermute(one, AXES, group_pairs(group, ring, 0, anyone))  29.3 us
    pallas_call x4, Pallas kernels, right(): pl.pallas_call(functools.partial(right_kernel, jobs), out_shape=[jax.Shap...  15.9 us
    ppermute x6, waiting for transfers between devices, local(): lax.ppermute(quarter, AXES, group_pairs(group, ring, 0, is_source))  14 us
    pallas_call x4, Pallas kernels, left(): pl.pallas_call(kernel, out_shape=[jax.ShapeDtypeStruct(shape, f32), jax.S...  13.5 us
    ppermute x2, waiting for transfers between devices, cross(): return lax.ppermute(one, AXES, group_pairs(group, 0, 1, in_source_plane))  10.5 us
    pallas_call x4, Pallas kernels, left(): pl.pallas_call(kernel, out_shape=jax.ShapeDtypeStruct((half, half), f32),...  9.62 us
  transfers between devices with their start and end apart: 23, of which 8 were waited for; matrix products, arithmetic and copies ran while one was open for 0% of the time, Pallas kernels for 33%

profile of v4, /device:TPU:30, one launch (start us, length us, event | category | flops | bytes accessed | tf_op | source)
XLA Modules:
  0.0 214.5 jit_solution(4389061437629277444)
XLA Ops:
  0.0 0.1 stack.102.info_ref
  0.1 0.0 copy-start
  0.1 3.4 %copy-done = f32[2048,1024]{1,0:T(8,128)S(1)} copy-done((f32[2048,1024]{1,0:T(8,128)S(1)}, f32[2048,1024]{1,0:T(8,128)}, u32[]{:S(2)}) %copy-start) | copy-done | bytes 8388632
  3.5 1.3 pack.1
  4.8 0.7 collective-permute-start
  5.5 1.3 collective-permute-start.3
  6.8 1.3 collective-permute-start.1
  8.1 0.7 collective-permute-start.2
  8.8 0.7 collective-permute-start.4
  9.5 0.0 collective-permute-done.refs_0_
  9.5 0.7 collective-permute-start.5
  10.2 13.4 %collective-permute-done.1.refs_1_ = f32[128,1024]{1,0:T(8,128)S(1)} collective-permute-done((f32[128,1024]{1,0:T(8,128)S(1)}, f32[128,1024]{1,0:T(8,128)S(1)}, u32[]{:S(2)}, u32[]{:S(2)}) %collective-permute-start.1) | collective-permute-done | bytes 524320 | tf_op jit(solution)/shard_map/ppermute | solution.py:378
  23.6 0.6 collective-permute-done.3.refs_3_
  24.2 0.0 collective-permute-done.4.refs_4_
  24.2 0.0 collective-permute-done.5.refs_5_
  24.2 0.7 merge.1
  24.9 1.5 collective-permute-start.6
  26.4 10.5 %collective-permute-done.6.across = f32[128,1024]{1,0:T(8,128)S(1)} collective-permute-done((f32[128,1024]{1,0:T(8,128)S(1)}, f32[128,1024]{1,0:T(8,128)S(1)}, u32[]{:S(2)}, u32[]{:S(2)}) %collective-permute-start.6) | collective-permute-done | bytes 524320 | tf_op jit(solution)/shard_map/ppermute | solution.py:384
  36.9 0.6 choose_col.1
  37.5 3.5 %collective-permute-start.7 = (f32[128,1024]{1,0:T(8,128)S(1)}, f32[128,1024]{1,0:T(8,128)S(1)}, u32[]{:S(2)}, u32[]{:S(2)}) collective-permute-start(f32[128,1024]{1,0:T(8,128)S(1)} %get-tuple-element.26.held), channel_id=1, source_target_pairs={{0,8},{1,9},{2,10},{3,11},{4,12},{5,13},{6,14},{7,15},{16,24},{17,... | collective-permute-start | bytes 1572872 | tf_op jit(solution)/shard_map/ppermute | solution.py:384
  41.0 7.2 %collective-permute-start.12 = (f32[128,1024]{1,0:T(8,128)S(1)}, f32[128,1024]{1,0:T(8,128)S(1)}, u32[]{:S(2)}, u32[]{:S(2)}) collective-permute-start(f32[128,1024]{1,0:T(8,128)S(1)} %get-tuple-element.27.refs_0_), channel_id=1, source_target_pairs={{0,16},{1,17},{2,18},{3,19},{4,20},{5,21},{6,22},{7,23},{8,24},{9,... | collective-permute-start | bytes 1572872 | tf_op jit(solution)/shard_map/ppermute | solution.py:388
  48.2 4.5 %collective-permute-start.13 = (f32[128,1024]{1,0:T(8,128)S(1)}, f32[128,1024]{1,0:T(8,128)S(1)}, u32[]{:S(2)}, u32[]{:S(2)}) collective-permute-start(f32[128,1024]{1,0:T(8,128)S(1)} %get-tuple-element.27.refs_0_), channel_id=1, source_target_pairs={{0,48},{1,49},{2,50},{3,51},{4,52},{5,53},{6,54},{7,55},{8,56},{9,... | collective-permute-start | bytes 1572872 | tf_op jit(solution)/shard_map/ppermute | solution.py:388
  52.7 2.0 collective-permute-start.14
  54.7 0.6 choose_row.1.refs_4_
  55.3 2.0 collective-permute-start.10
  57.3 10.2 %collective-permute-start.8 = (f32[128,1024]{1,0:T(8,128)S(1)}, f32[128,1024]{1,0:T(8,128)S(1)}, u32[]{:S(2)}, u32[]{:S(2)}) collective-permute-start(f32[128,1024]{1,0:T(8,128)S(1)} %choose_row.1.refs_4_), channel_id=1, source_target_pairs={{0,2},{1,3},{2,4},{3,5},{4,6},{5,7},{6,0},{7,1},{8,10},{9,11},{10,... | collective-permute-start | bytes 1572872 | tf_op jit(solution)/shard_map/ppermute | solution.py:388
  67.5 3.4 %collective-permute-start.9 = (f32[128,1024]{1,0:T(8,128)S(1)}, f32[128,1024]{1,0:T(8,128)S(1)}, u32[]{:S(2)}, u32[]{:S(2)}) collective-permute-start(f32[128,1024]{1,0:T(8,128)S(1)} %choose_row.1.refs_4_), channel_id=1, source_target_pairs={{0,6},{1,7},{2,0},{3,1},{4,2},{5,3},{6,4},{7,5},{8,14},{9,15},{10,... | collective-permute-start | bytes 1572872 | tf_op jit(solution)/shard_map/ppermute | solution.py:388
  70.9 0.0 collective-permute-done.13.refs_2_
  70.9 3.8 %collective-permute-done.14.refs_3_ = f32[128,1024]{1,0:T(8,128)S(1)} collective-permute-done((f32[128,1024]{1,0:T(8,128)S(1)}, f32[128,1024]{1,0:T(8,128)S(1)}, u32[]{:S(2)}, u32[]{:S(2)}) %collective-permute-start.14) | collective-permute-done | bytes 524320 | tf_op jit(solution)/shard_map/ppermute | solution.py:388
  74.7 11.2 %column_rotation.1 = (bf16[1024,1024]{1,0:T(8,128)(2,1)S(1)}, bf16[1024,1024]{1,0:T(8,128)(2,1)S(1)}) custom-call(s32[23]{0:T(128)S(1)} %stack.102.info_ref, f32[128,1024]{1,0:T(8,128)S(1)} %get-tuple-element.27.refs_0_, f32[128,1024]{1,0:T(8,128)S(1)} %collective-permute-done.12.refs_1_, f32[128,1024]{1,0:T(8,128)S(1)} %collective-permute-done.13.refs_2_, ...), custom_call_target="tpu_custom_call" | custom-call | flops 201326592 | bytes 98304 | tf_op jit(solution)/shard_map/column_rotation/pallas_call | solution.py:179
  85.9 0.0 collective-permute-done.8
  85.9 2.2 %collective-permute-done.9 = f32[128,1024]{1,0:T(8,128)S(1)} collective-permute-done((f32[128,1024]{1,0:T(8,128)S(1)}, f32[128,1024]{1,0:T(8,128)S(1)}, u32[]{:S(2)}, u32[]{:S(2)}) %collective-permute-start.9) | collective-permute-done | bytes 524320 | tf_op jit(solution)/shard_map/ppermute | solution.py:388
  88.2 0.2 pad_maximum_fusion.refs_0_
  88.4 4.0 %right_far_first.1.refs_0_ = f32[1024,512]{1,0:T(8,128)S(1)} custom-call(s32[23]{0:T(128)S(1)} %stack.102.info_ref, f32[2048,1024]{1,0:T(8,128)S(1)} %bitcast.21, bf16[1024,1024]{1,0:T(8,128)(2,1)S(1)} %get-tuple-element.28.high_ref, bf16[1024,1024]{1,0:T(8,128)(2,1)S(1)} %get-tuple-element.29.low_ref, f32[512,1024]{1,0:T(8,128)S(1)} %pad_maximum_fusion.refs_0_), custom_call_target="tpu_custom_call" | custom-call | flops 150994944 | bytes 131072 | tf_op jit(solution)/shard_map/right_far_first/pallas_call | solution.py:209
  92.4 4.0 %right_far_second.1.refs_0_ = f32[1024,512]{1,0:T(8,128)S(1)} custom-call(s32[23]{0:T(128)S(1)} %stack.102.info_ref, f32[2048,1024]{1,0:T(8,128)S(1)} %bitcast.21, bf16[1024,1024]{1,0:T(8,128)(2,1)S(1)} %get-tuple-element.28.high_ref, bf16[1024,1024]{1,0:T(8,128)(2,1)S(1)} %get-tuple-element.29.low_ref, f32[1024,512]{1,0:T(8,128)S(1)} %right_far_first.1.refs_0_), custom_call_target="tpu_custom_call" | custom-call | flops 150994944 | bytes 131072 | tf_op jit(solution)/shard_map/right_far_second/pallas_call | solution.py:209
  96.4 6.5 %collective-permute-start.16 = (f32[1024,512]{1,0:T(8,128)S(1)}, f32[1024,512]{1,0:T(8,128)S(1)}, u32[]{:S(2)}, u32[]{:S(2)}) collective-permute-start(f32[1024,512]{1,0:T(8,128)S(1)} %right_far_first.1.refs_0_), channel_id=1, source_target_pairs={{0,0},{15,15},{2,1},{4,3},{6,5},{8,7},{10,9},{12,11},{14,13},{1,2}... | collective-permute-start | bytes 6291464 | tf_op jit(solution)/shard_map/ppermute | solution.py:441
  102.9 4.0 %right_near_first.1.refs_0_ = f32[1024,512]{1,0:T(8,128)S(1)} custom-call(s32[23]{0:T(128)S(1)} %stack.102.info_ref, f32[2048,1024]{1,0:T(8,128)S(1)} %bitcast.21, bf16[1024,1024]{1,0:T(8,128)(2,1)S(1)} %get-tuple-element.28.high_ref, bf16[1024,1024]{1,0:T(8,128)(2,1)S(1)} %get-tuple-element.29.low_ref, f32[1024,512]{1,0:T(8,128)S(1)} %right_far_second.1.refs_0_), custom_call_target="tpu_custom_call" | custom-call | flops 150994944 | bytes 131072 | tf_op jit(solution)/shard_map/right_near_first/pallas_call | solution.py:209
  106.9 0.7 collective-permute-start.15
  107.6 0.1 collective-permute-start.11
  107.7 4.0 %right_near_second.1.refs_1_ = f32[1024,512]{1,0:T(8,128)S(1)} custom-call(s32[23]{0:T(128)S(1)} %stack.102.info_ref, f32[2048,1024]{1,0:T(8,128)S(1)} %bitcast.21, bf16[1024,1024]{1,0:T(8,128)(2,1)S(1)} %get-tuple-element.28.high_ref, bf16[1024,1024]{1,0:T(8,128)(2,1)S(1)} %get-tuple-element.29.low_ref, f32[1024,512]{1,0:T(8,128)S(1)} %right_near_first.1.refs_0_), custom_call_target="tpu_custom_call" | custom-call | flops 150994944 | bytes 131072 | tf_op jit(solution)/shard_map/right_near_second/pallas_call | solution.py:209
  111.6 0.5 collective-permute-start.18
  112.1 2.2 %collective-permute-start.17 = (f32[1024,512]{1,0:T(8,128)S(1)}, f32[1024,512]{1,0:T(8,128)S(1)}, u32[]{:S(2)}, u32[]{:S(2)}) collective-permute-start(f32[1024,512]{1,0:T(8,128)S(1)} %right_far_second.1.refs_0_), channel_id=1, source_target_pairs={{0,0},{15,15},{2,1},{4,3},{6,5},{8,7},{10,9},{12,11},{14,13},{1,2}... | collective-permute-start | bytes 6291464 | tf_op jit(solution)/shard_map/ppermute | solution.py:441
  114.3 11.1 %row_rotation.1.turned_ref = f32[1024,1024]{1,0:T(8,128)S(1)} custom-call(s32[23]{0:T(128)S(1)} %stack.102.info_ref, f32[512,1024]{1,0:T(8,128)S(1)} %pad_maximum_fusion.refs_0_, f32[1024,512]{1,0:T(8,128)S(1)} %right_near_second.1.refs_1_), custom_call_target="tpu_custom_call" | custom-call | flops 201326592 | bytes 98304 | tf_op jit(solution)/shard_map/row_rotation/pallas_call | solution.py:179
  125.4 0.8 collective-permute-done.16.part_ref
  126.2 2.4 %leave_1.1.refs_0_.own_ref = f32[512,512]{1,0:T(8,128)S(1)} custom-call(s32[23]{0:T(128)S(1)} %stack.102.info_ref, f32[1024,1024]{1,0:T(8,128)S(1)} %row_rotation.1.turned_ref, f32[1024,512]{1,0:T(8,128)S(1)} %collective-permute-done.16.part_ref), custom_call_target="tpu_custom_call" | custom-call | flops 25165824 | bytes 98304 | tf_op jit(solution)/shard_map/leave_1/pallas_call | solution.py:249
  128.6 1.4 collective-permute-start.21
  130.0 2.4 %leave_0.1.refs_1_.own_ref = f32[512,512]{1,0:T(8,128)S(1)} custom-call(s32[23]{0:T(128)S(1)} %stack.102.info_ref, f32[1024,1024]{1,0:T(8,128)S(1)} %row_rotation.1.turned_ref, f32[1024,512]{1,0:T(8,128)S(1)} %collective-permute-done.15.part_ref, f32[512,512]{1,0:T(8,128)S(1)} %leave_1.1.refs_0_.own_ref), custom_call_target="tpu_custom_call" | custom-call | flops 25165824 | bytes 98304 | tf_op jit(solution)/shard_map/leave_0/pallas_call | solution.py:249
  132.4 5.3 %collective-permute-start.22 = (f32[512,512]{1,0:T(8,128)S(1)}, f32[512,512]{1,0:T(8,128)S(1)}, u32[]{:S(2)}, u32[]{:S(2)}) collective-permute-start(f32[512,512]{1,0:T(8,128)S(1)} %leave_0.1.refs_1_.own_ref), channel_id=1, source_target_pairs={{1,17},{3,19},{5,21},{7,23},{9,25},{11,27},{13,29},{15,31},{16,0},... | collective-permute-start | bytes 3145736 | tf_op jit(solution)/shard_map/ppermute | solution.py:415
  137.7 11.1 %other_row_rotation.1.turned_ref = f32[1024,1024]{1,0:T(8,128)S(1)} custom-call(s32[23]{0:T(128)S(1)} %stack.102.info_ref, f32[512,1024]{1,0:T(8,128)S(1)} %collective-permute-done.11.refs_0_, f32[512,512]{1,0:T(8,128)S(1)} %leave_0.1.refs_1_.own_ref), custom_call_target="tpu_custom_call" | custom-call | flops 201326592 | bytes 98304 | tf_op jit(solution)/shard_map/other_row_rotation/pallas_call | solution.py:179
  148.8 0.0 collective-permute-done.18.part_ref
  148.8 2.4 %leave_2.1.refs_0_.own_ref = f32[512,512]{1,0:T(8,128)S(1)} custom-call(s32[23]{0:T(128)S(1)} %stack.102.info_ref, f32[1024,1024]{1,0:T(8,128)S(1)} %other_row_rotation.1.turned_ref, f32[1024,512]{1,0:T(8,128)S(1)} %collective-permute-done.18.part_ref), custom_call_target="tpu_custom_call" | custom-call | flops 25165824 | bytes 98304 | tf_op jit(solution)/shard_map/leave_2/pallas_call | solution.py:249
  151.2 1.5 collective-permute-start.20
  152.7 3.4 %keep_0.1 = (f32[2048,1024]{1,0:T(8,128)}, f32[8,128]{1,0:T(8,128)}) custom-call(s32[23]{0:T(128)S(1)} %stack.102.info_ref, f32[1024,1024]{1,0:T(8,128)S(1)} %row_rotation.1.turned_ref, f32[1024,512]{1,0:T(8,128)S(1)} %collective-permute-done.15.part_ref, f32[512,512]{1,0:T(8,128)S(1)} %leave_2.1.refs_0_.own_ref), custom_call_target="tpu_custom_call" | custom-call | flops 25165824 | bytes 98304 | tf_op jit(solution)/shard_map/keep_0/pallas_call | solution.py:264
  156.1 3.4 %keep_1.1 = (f32[2048,1024]{1,0:T(8,128)}, f32[8,128]{1,0:T(8,128)}) custom-call(s32[23]{0:T(128)S(1)} %stack.102.info_ref, f32[1024,1024]{1,0:T(8,128)S(1)} %row_rotation.1.turned_ref, f32[1024,512]{1,0:T(8,128)S(1)} %collective-permute-done.16.part_ref, f32[2048,1024]{1,0:T(8,128)} %get-tuple-element.30.refs_0_), custom_call_target="tpu_custom_call", output_to_operand_aliasing={{0}: (3, {})} | custom-call | flops 25165824 | bytes 98304 | tf_op jit(solution)/shard_map/keep_1/pallas_call | solution.py:264
  159.5 3.4 %keep_2.1 = (f32[2048,1024]{1,0:T(8,128)}, f32[8,128]{1,0:T(8,128)S(1)}) custom-call(s32[23]{0:T(128)S(1)} %stack.102.info_ref, f32[1024,1024]{1,0:T(8,128)S(1)} %other_row_rotation.1.turned_ref, f32[1024,512]{1,0:T(8,128)S(1)} %collective-permute-done.18.part_ref, f32[2048,1024]{1,0:T(8,128)} %get-tuple-element.31.refs_0_), custom_call_target="tpu_custom_call", output_to_operand_aliasing={{0}: (3, {})} | custom-call | flops 25165824 | bytes 98304 | tf_op jit(solution)/shard_map/keep_2/pallas_call | solution.py:264
  162.9 30.7 %collective-permute-done.17.part_ref = f32[1024,512]{1,0:T(8,128)S(1)} collective-permute-done((f32[1024,512]{1,0:T(8,128)S(1)}, f32[1024,512]{1,0:T(8,128)S(1)}, u32[]{:S(2)}, u32[]{:S(2)}) %collective-permute-start.17) | collective-permute-done | bytes 2097184 | tf_op jit(solution)/shard_map/ppermute | solution.py:441
  193.6 2.4 %leave_3.1.refs_0_.own_ref = f32[512,512]{1,0:T(8,128)S(1)} custom-call(s32[23]{0:T(128)S(1)} %stack.102.info_ref, f32[1024,1024]{1,0:T(8,128)S(1)} %other_row_rotation.1.turned_ref, f32[1024,512]{1,0:T(8,128)S(1)} %collective-permute-done.17.part_ref, f32[8,128]{1,0:T(8,128)S(1)} %get-tuple-element.32.refs_0_), custom_call_target="tpu_custom_call" | custom-call | flops 25165824 | bytes 98304 | tf_op jit(solution)/shard_map/leave_3/pallas_call | solution.py:249
  196.0 1.3 collective-permute-start.19
  197.3 3.4 %keep_3.1 = (f32[2048,1024]{1,0:T(8,128)}, f32[8,128]{1,0:T(8,128)}) custom-call(s32[23]{0:T(128)S(1)} %stack.102.info_ref, f32[1024,1024]{1,0:T(8,128)S(1)} %other_row_rotation.1.turned_ref, f32[1024,512]{1,0:T(8,128)S(1)} %collective-permute-done.17.part_ref, f32[512,512]{1,0:T(8,128)S(1)} %leave_3.1.refs_0_.own_ref, ...), custom_call_target="tpu_custom_call", output_to_operand_aliasing={{0}: (4, {})} | custom-call | flops 25165824 | bytes 98304 | tf_op jit(solution)/shard_map/keep_3/pallas_call | solution.py:264
  200.7 1.6 land_0.1.result_ref
  202.3 1.6 land_1.1.result_ref
  203.8 1.6 land_2.1.result_ref
  205.4 7.3 %collective-permute-done.19.arrived_ref = f32[512,512]{1,0:T(8,128)S(1)} collective-permute-done((f32[512,512]{1,0:T(8,128)S(1)}, f32[512,512]{1,0:T(8,128)S(1)}, u32[]{:S(2)}, u32[]{:S(2)}) %collective-permute-start.19) | collective-permute-done | bytes 1048608 | tf_op jit(solution)/shard_map/ppermute | solution.py:415
  212.7 1.6 land_3.1
  (14 shorter events, 0.0 us)
Async XLA Ops:
  0.1 3.4 %copy-start = (f32[2048,1024]{1,0:T(8,128)S(1)}, f32[2048,1024]{1,0:T(8,128)}, u32[]{:S(2)}) copy-start(f32[2048,1024]{1,0:T(8,128)} %m_ref.7) | copy-start | bytes 25165828
  3.5 84.9 %slice-start = ((s8[8388608]{0:T(1024)(128)(4,1)}), s8[4194304]{0:T(1024)(128)(4,1)S(1)}, s32[]{:S(2)}) async-start(s8[8388608]{0:T(1024)(128)(4,1)} %bitcast.20), calls=%async_computation | async-start | bytes 8388608
  4.8 4.7 %collective-permute-start = (f32[128,1024]{1,0:T(8,128)S(1)}, f32[128,1024]{1,0:T(8,128)S(1)}, u32[]{:S(2)}, u32[]{:S(2)}) collective-permute-start(f32[128,1024]{1,0:T(8,128)S(1)} %get-tuple-element.21), channel_id=1, source_target_pairs={{0,16},{1,17},{18,34},{19,35},{36,52},{37,53},{54,6},{55,7},{72,88... | collective-permute-start | bytes 1572872 | tf_op jit(solution)/shard_map/ppermute | solution.py:378
  5.5 18.7 %collective-permute-start.3 = (f32[128,1024]{1,0:T(8,128)S(1)}, f32[128,1024]{1,0:T(8,128)S(1)}, u32[]{:S(2)}, u32[]{:S(2)}) collective-permute-start(f32[128,1024]{1,0:T(8,128)S(1)} %get-tuple-element.21), channel_id=1, source_target_pairs={{0,2},{1,3},{18,20},{19,21},{36,38},{37,39},{54,48},{55,49},{72,74... | collective-permute-start | bytes 1572872 | tf_op jit(solution)/shard_map/ppermute | solution.py:378
  6.8 16.8 %collective-permute-start.1 = (f32[128,1024]{1,0:T(8,128)S(1)}, f32[128,1024]{1,0:T(8,128)S(1)}, u32[]{:S(2)}, u32[]{:S(2)}) collective-permute-start(f32[128,1024]{1,0:T(8,128)S(1)} %get-tuple-element.22), channel_id=1, source_target_pairs={{0,48},{1,49},{18,2},{19,3},{36,20},{37,21},{54,38},{55,39},{72,12... | collective-permute-start | bytes 1572872 | tf_op jit(solution)/shard_map/ppermute | solution.py:378
  8.1 15.5 %collective-permute-start.2 = (f32[128,1024]{1,0:T(8,128)S(1)}, f32[128,1024]{1,0:T(8,128)S(1)}, u32[]{:S(2)}, u32[]{:S(2)}) collective-permute-start(f32[128,1024]{1,0:T(8,128)S(1)} %get-tuple-element.23), channel_id=1, source_target_pairs={{0,32},{1,33},{18,50},{19,51},{36,4},{37,5},{54,22},{55,23},{72,10... | collective-permute-start | bytes 1572872 | tf_op jit(solution)/shard_map/ppermute | solution.py:378
  8.8 15.4 %collective-permute-start.4 = (f32[128,1024]{1,0:T(8,128)S(1)}, f32[128,1024]{1,0:T(8,128)S(1)}, u32[]{:S(2)}, u32[]{:S(2)}) collective-permute-start(f32[128,1024]{1,0:T(8,128)S(1)} %get-tuple-element.22), channel_id=1, source_target_pairs={{0,6},{1,7},{18,16},{19,17},{36,34},{37,35},{54,52},{55,53},{72,78... | collective-permute-start | bytes 1572872 | tf_op jit(solution)/shard_map/ppermute | solution.py:378
  9.5 14.7 %collective-permute-start.5 = (f32[128,1024]{1,0:T(8,128)S(1)}, f32[128,1024]{1,0:T(8,128)S(1)}, u32[]{:S(2)}, u32[]{:S(2)}) collective-permute-start(f32[128,1024]{1,0:T(8,128)S(1)} %get-tuple-element.23), channel_id=1, source_target_pairs={{0,4},{1,5},{18,22},{19,23},{36,32},{37,33},{54,50},{55,51},{72,76... | collective-permute-start | bytes 1572872 | tf_op jit(solution)/shard_map/ppermute | solution.py:378
  24.2 64.3 %slice-start.1 = ((s8[8388608]{0:T(1024)(128)(4,1)}), s8[4194304]{0:T(1024)(128)(4,1)S(1)}, s32[]{:S(2)}) async-start(s8[8388608]{0:T(1024)(128)(4,1)} %bitcast.20), calls=%async_computation.1 | async-start | bytes 8388608
  24.9 12.0 %collective-permute-start.6 = (f32[128,1024]{1,0:T(8,128)S(1)}, f32[128,1024]{1,0:T(8,128)S(1)}, u32[]{:S(2)}, u32[]{:S(2)}) collective-permute-start(f32[128,1024]{1,0:T(8,128)S(1)} %get-tuple-element.24.held), channel_id=1, source_target_pairs={{0,64},{1,65},{2,66},{3,67},{4,68},{5,69},{6,70},{7,71},{16,80},{1... | collective-permute-start | bytes 1572872 | tf_op jit(solution)/shard_map/ppermute | solution.py:384
  37.5 17.2 %collective-permute-start.7 = (f32[128,1024]{1,0:T(8,128)S(1)}, f32[128,1024]{1,0:T(8,128)S(1)}, u32[]{:S(2)}, u32[]{:S(2)}) collective-permute-start(f32[128,1024]{1,0:T(8,128)S(1)} %get-tuple-element.26.held), channel_id=1, source_target_pairs={{0,8},{1,9},{2,10},{3,11},{4,12},{5,13},{6,14},{7,15},{16,24},{17,... | collective-permute-start | bytes 1572872 | tf_op jit(solution)/shard_map/ppermute | solution.py:384
  41.0 26.5 %collective-permute-start.12 = (f32[128,1024]{1,0:T(8,128)S(1)}, f32[128,1024]{1,0:T(8,128)S(1)}, u32[]{:S(2)}, u32[]{:S(2)}) collective-permute-start(f32[128,1024]{1,0:T(8,128)S(1)} %get-tuple-element.27.refs_0_), channel_id=1, source_target_pairs={{0,16},{1,17},{2,18},{3,19},{4,20},{5,21},{6,22},{7,23},{8,24},{9,... | collective-permute-start | bytes 1572872 | tf_op jit(solution)/shard_map/ppermute | solution.py:388
  48.2 22.7 %collective-permute-start.13 = (f32[128,1024]{1,0:T(8,128)S(1)}, f32[128,1024]{1,0:T(8,128)S(1)}, u32[]{:S(2)}, u32[]{:S(2)}) collective-permute-start(f32[128,1024]{1,0:T(8,128)S(1)} %get-tuple-element.27.refs_0_), channel_id=1, source_target_pairs={{0,48},{1,49},{2,50},{3,51},{4,52},{5,53},{6,54},{7,55},{8,56},{9,... | collective-permute-start | bytes 1572872 | tf_op jit(solution)/shard_map/ppermute | solution.py:388
  52.7 22.0 %collective-permute-start.14 = (f32[128,1024]{1,0:T(8,128)S(1)}, f32[128,1024]{1,0:T(8,128)S(1)}, u32[]{:S(2)}, u32[]{:S(2)}) collective-permute-start(f32[128,1024]{1,0:T(8,128)S(1)} %get-tuple-element.27.refs_0_), channel_id=1, source_target_pairs={{0,32},{1,33},{2,34},{3,35},{4,36},{5,37},{6,38},{7,39},{8,40},{9,... | collective-permute-start | bytes 1572872 | tf_op jit(solution)/shard_map/ppermute | solution.py:388
  55.3 30.6 %collective-permute-start.10 = (f32[128,1024]{1,0:T(8,128)S(1)}, f32[128,1024]{1,0:T(8,128)S(1)}, u32[]{:S(2)}, u32[]{:S(2)}) collective-permute-start(f32[128,1024]{1,0:T(8,128)S(1)} %choose_row.1.refs_4_), channel_id=1, source_target_pairs={{0,4},{1,5},{2,6},{3,7},{4,0},{5,1},{6,2},{7,3},{8,12},{9,13},{10,... | collective-permute-start | bytes 1572872 | tf_op jit(solution)/shard_map/ppermute | solution.py:388
  57.3 28.6 %collective-permute-start.8 = (f32[128,1024]{1,0:T(8,128)S(1)}, f32[128,1024]{1,0:T(8,128)S(1)}, u32[]{:S(2)}, u32[]{:S(2)}) collective-permute-start(f32[128,1024]{1,0:T(8,128)S(1)} %choose_row.1.refs_4_), channel_id=1, source_target_pairs={{0,2},{1,3},{2,4},{3,5},{4,6},{5,7},{6,0},{7,1},{8,10},{9,11},{10,... | collective-permute-start | bytes 1572872 | tf_op jit(solution)/shard_map/ppermute | solution.py:388
  67.5 20.7 %collective-permute-start.9 = (f32[128,1024]{1,0:T(8,128)S(1)}, f32[128,1024]{1,0:T(8,128)S(1)}, u32[]{:S(2)}, u32[]{:S(2)}) collective-permute-start(f32[128,1024]{1,0:T(8,128)S(1)} %choose_row.1.refs_4_), channel_id=1, source_target_pairs={{0,6},{1,7},{2,0},{3,1},{4,2},{5,3},{6,4},{7,5},{8,14},{9,15},{10,... | collective-permute-start | bytes 1572872 | tf_op jit(solution)/shard_map/ppermute | solution.py:388
  96.4 29.8 %collective-permute-start.16 = (f32[1024,512]{1,0:T(8,128)S(1)}, f32[1024,512]{1,0:T(8,128)S(1)}, u32[]{:S(2)}, u32[]{:S(2)}) collective-permute-start(f32[1024,512]{1,0:T(8,128)S(1)} %right_far_first.1.refs_0_), channel_id=1, source_target_pairs={{0,0},{15,15},{2,1},{4,3},{6,5},{8,7},{10,9},{12,11},{14,13},{1,2}... | collective-permute-start | bytes 6291464 | tf_op jit(solution)/shard_map/ppermute | solution.py:441
  106.9 23.0 %collective-permute-start.15 = (f32[1024,512]{1,0:T(8,128)S(1)}, f32[1024,512]{1,0:T(8,128)S(1)}, u32[]{:S(2)}, u32[]{:S(2)}) collective-permute-start(f32[1024,512]{1,0:T(8,128)S(1)} %right_near_first.1.refs_0_), channel_id=1, source_target_pairs={{0,1},{1,0},{2,3},{3,2},{4,5},{5,4},{6,7},{7,6},{8,9},{9,8},{10,11... | collective-permute-start | bytes 6291464 | tf_op jit(solution)/shard_map/ppermute | solution.py:442
  107.6 30.1 %collective-permute-start.11 = (f32[512,1024]{1,0:T(8,128)S(1)}, f32[512,1024]{1,0:T(8,128)S(1)}, u32[]{:S(2)}, u32[]{:S(2)}) collective-permute-start(f32[512,1024]{1,0:T(8,128)S(1)} %pad_maximum_fusion.refs_0_), channel_id=1, source_target_pairs={{0,1},{1,0},{2,3},{3,2},{4,5},{5,4},{6,7},{7,6},{8,9},{9,8},{10,11... | collective-permute-start | bytes 6291464 | tf_op jit(solution)/shard_map/ppermute | solution.py:428
  111.6 37.2 %collective-permute-start.18 = (f32[1024,512]{1,0:T(8,128)S(1)}, f32[1024,512]{1,0:T(8,128)S(1)}, u32[]{:S(2)}, u32[]{:S(2)}) collective-permute-start(f32[1024,512]{1,0:T(8,128)S(1)} %right_near_second.1.refs_1_), channel_id=1, source_target_pairs={{0,1},{1,0},{2,3},{3,2},{4,5},{5,4},{6,7},{7,6},{8,9},{9,8},{10,11... | collective-permute-start | bytes 6291464 | tf_op jit(solution)/shard_map/ppermute | solution.py:442
  112.1 81.5 %collective-permute-start.17 = (f32[1024,512]{1,0:T(8,128)S(1)}, f32[1024,512]{1,0:T(8,128)S(1)}, u32[]{:S(2)}, u32[]{:S(2)}) collective-permute-start(f32[1024,512]{1,0:T(8,128)S(1)} %right_far_second.1.refs_0_), channel_id=1, source_target_pairs={{0,0},{15,15},{2,1},{4,3},{6,5},{8,7},{10,9},{12,11},{14,13},{1,2}... | collective-permute-start | bytes 6291464 | tf_op jit(solution)/shard_map/ppermute | solution.py:441
  128.6 73.7 %collective-permute-start.21 = (f32[512,512]{1,0:T(8,128)S(1)}, f32[512,512]{1,0:T(8,128)S(1)}, u32[]{:S(2)}, u32[]{:S(2)}) collective-permute-start(f32[512,512]{1,0:T(8,128)S(1)} %leave_1.1.refs_0_.own_ref), channel_id=1, source_target_pairs={{1,17},{3,19},{5,21},{7,23},{9,25},{11,27},{13,29},{15,31},{16,0},... | collective-permute-start | bytes 3145736 | tf_op jit(solution)/shard_map/ppermute | solution.py:415
  132.4 68.3 %collective-permute-start.22 = (f32[512,512]{1,0:T(8,128)S(1)}, f32[512,512]{1,0:T(8,128)S(1)}, u32[]{:S(2)}, u32[]{:S(2)}) collective-permute-start(f32[512,512]{1,0:T(8,128)S(1)} %leave_0.1.refs_1_.own_ref), channel_id=1, source_target_pairs={{1,17},{3,19},{5,21},{7,23},{9,25},{11,27},{13,29},{15,31},{16,0},... | collective-permute-start | bytes 3145736 | tf_op jit(solution)/shard_map/ppermute | solution.py:415
  151.2 52.6 %collective-permute-start.20 = (f32[512,512]{1,0:T(8,128)S(1)}, f32[512,512]{1,0:T(8,128)S(1)}, u32[]{:S(2)}, u32[]{:S(2)}) collective-permute-start(f32[512,512]{1,0:T(8,128)S(1)} %leave_2.1.refs_0_.own_ref), channel_id=1, source_target_pairs={{0,16},{2,18},{4,20},{6,22},{8,24},{10,26},{12,28},{14,30},{16,32}... | collective-permute-start | bytes 3145736 | tf_op jit(solution)/shard_map/ppermute | solution.py:415
  196.0 16.7 %collective-permute-start.19 = (f32[512,512]{1,0:T(8,128)S(1)}, f32[512,512]{1,0:T(8,128)S(1)}, u32[]{:S(2)}, u32[]{:S(2)}) collective-permute-start(f32[512,512]{1,0:T(8,128)S(1)} %leave_3.1.refs_0_.own_ref), channel_id=1, source_target_pairs={{0,16},{2,18},{4,20},{6,22},{8,24},{10,26},{12,28},{14,30},{16,32}... | collective-permute-start | bytes 3145736 | tf_op jit(solution)/shard_map/ppermute | solution.py:415

commit v5 on v4

--- a/solution.py
+++ b/solution.py
@@ -12,8 +12,13 @@
 VMEM_LIMIT = 16 * 1024 * 1024
 
 
-def cost(flops, nbytes):
-    return pl.CostEstimate(flops=flops // 64, bytes_accessed=nbytes // 64, transcendentals=0)
+def cost(flops, nbytes, share=1 / 64):
+    return pl.CostEstimate(
+        flops=int(flops * share), bytes_accessed=int(nbytes * share), transcendentals=0
+    )
+
+
+LEFT_SHARE = 16
 
 
 def split(value):
@@ -33,7 +38,7 @@
 FAR_FIRST, FAR_SECOND, FAR_HALF, NEAR_HALF, NEAR_FIRST, NEAR_SECOND = range(5, 11)
 MOVED_FIRST, MOVED_SECOND, STAYS_FIRST, STAYS_SECOND = range(11, 15)
 KEPT_FIRST, KEPT_SECOND, NEAR_BLOCK, FAR_BLOCK = range(15, 19)
-LAND_FIRST, LAND_SECOND, END_FIRST, END_SECOND = range(19, 23)
+LAND_FIRST, LAND_SECOND, END_FIRST, END_SECOND, END_COL = range(19, 24)
 RINGS = (1, 3, 2)
 
 
@@ -100,6 +105,27 @@
         outs[1][...] = refs[0][...]
 
 
+def stack_kernel(info_ref, top, bottom, after, out):
+    rows = top.shape[0]
+    out[:rows, :] = top[...]
+    out[rows:, :] = bottom[...]
+
+
+def stacked(info, top, bottom, after):
+    rows, width = top.shape
+    return pl.pallas_call(
+        stack_kernel,
+        out_shape=jax.ShapeDtypeStruct((2 * rows, width), f32),
+        in_specs=[pl.BlockSpec(memory_space=pltpu.SMEM)]
+        + [pl.BlockSpec(memory_space=pltpu.VMEM)] * 2
+        + [pl.BlockSpec(memory_space=pl.ANY)],
+        out_specs=pl.BlockSpec(memory_space=pltpu.VMEM),
+        compiler_params=pltpu.CompilerParams(vmem_limit_bytes=VMEM_LIMIT),
+        cost_estimate=cost(rows * width, 16 * rows * width),
+        name="stacked",
+    )(info, top, bottom, after)
+
+
 def small(kernel, info, operands, outs, name):
     shape = operands[0].shape
     return pl.pallas_call(
@@ -184,7 +210,7 @@
         + [pl.BlockSpec(memory_space=pl.ANY)] * len(after),
         out_specs=[pl.BlockSpec(memory_space=pltpu.VMEM)] * len(shapes),
         scratch_shapes=[pltpu.VMEM((width // 2, width), f32)] + [pltpu.VMEM(square, bf16)] * 4,
-        compiler_params=pltpu.CompilerParams(vmem_limit_bytes=7 * VMEM_LIMIT // 4),
+        compiler_params=pltpu.CompilerParams(vmem_limit_bytes=5 * VMEM_LIMIT // 4),
         cost_estimate=cost(12 * width**3, 6 * width * width),
         name=name,
     )(info, *pieces, *after)
@@ -219,39 +245,51 @@
     )(info, matrix, r_high, r_low, *after)
 
 
-def left_kernel(rows, part_at, to_result, info_ref, turned_ref, part_ref, *refs):
+def left_kernel(rows, place, info_ref, turned_ref, part_ref, own_ref, *refs):
     width = turned_ref.shape[0]
     half = width // 2
     at = pl.ds(pl.multiple_of(info_ref[rows] * half, half), half)
     t_high, t_low = split(turned_ref[at, :])
-    p_high, p_low = split(part_ref[part_at * width : (part_at + 1) * width, :])
-    value = dot3(t_high, t_low, p_high, p_low)
-    if to_result:
-        refs[-2][...] = value
-        refs[-1][...] = jnp.zeros_like(refs[-1])
-    else:
+    part = part_ref[...]
+    if own_ref is not part_ref:
+        part = jnp.where(info_ref[END_COL] > 0, own_ref[...], part)
+    value = dot3(t_high, t_low, *split(part))
+    if place is None:
         refs[-1][...] = value
-
-
-def left(info, rows, turned, part, part_at, after, name, target=None):
+        return
+    out_ref, token_ref, kept, sem = refs[-4:]
+    kept[...] = value
+    row, block = place
+    out_rows = pl.ds(pl.multiple_of(info_ref[row] * half, half), half)
+    out_cols = pl.ds(pl.multiple_of(info_ref[block] * half, half), half)
+    copy = pltpu.make_async_copy(kept, out_ref.at[out_rows, out_cols], sem)
+    copy.start()
+    token_ref[...] = jnp.zeros_like(token_ref)
+    copy.wait()
+
+
+def near_kernel(rows, place, info_ref, turned_ref, part_ref, *refs):
+    left_kernel(rows, place, info_ref, turned_ref, part_ref, part_ref, *refs)
+
+
+def left(info, rows, turned, part, after, name, target=None):
     width = turned.shape[0]
     half = width // 2
-    operands = [turned, part] + after
-    anywhere = [pl.BlockSpec(memory_space=pl.ANY)] * len(after)
-    kernel = functools.partial(left_kernel, rows, part_at, target is not None)
-    limit = VMEM_LIMIT if target is None else 7 * VMEM_LIMIT // 4
+    operands = [turned] + list(part) + after
+    in_specs = [pl.BlockSpec(memory_space=pltpu.SMEM)]
+    in_specs += [pl.BlockSpec(memory_space=pltpu.VMEM)] * (1 + len(part))
+    in_specs += [pl.BlockSpec(memory_space=pl.ANY)] * len(after)
+    kernel = left_kernel if len(part) > 1 else near_kernel
     common = dict(
-        compiler_params=pltpu.CompilerParams(vmem_limit_bytes=limit),
-        cost_estimate=cost(3 * width**3 // 2, 6 * width * width),
+        compiler_params=pltpu.CompilerParams(vmem_limit_bytes=VMEM_LIMIT),
+        cost_estimate=cost(3 * width**3 // 2, 6 * width * width, LEFT_SHARE),
         name=name,
     )
     if target is None:
         return pl.pallas_call(
-            kernel,
+            functools.partial(kernel, rows, None),
             out_shape=jax.ShapeDtypeStruct((half, half), f32),
-            in_specs=[pl.BlockSpec(memory_space=pltpu.SMEM)]
-            + [pl.BlockSpec(memory_space=pltpu.VMEM)] * 2
-            + anywhere,
+            in_specs=in_specs,
             out_specs=pl.BlockSpec(memory_space=pltpu.VMEM),
             **common,
         )(info, *operands)
@@ -260,53 +298,51 @@
     if result is not None:
         aliases = {1 + len(operands): 0}
         operands.append(result)
-        anywhere.append(pl.BlockSpec(memory_space=pl.ANY))
-    return pl.pallas_call(
-        kernel,
+        in_specs.append(pl.BlockSpec(memory_space=pl.ANY))
+    return pl.pallas_call(
+        functools.partial(kernel, rows, (row, block)),
         out_shape=[jax.ShapeDtypeStruct(shape, f32), jax.ShapeDtypeStruct((8, 128), f32)],
-        grid_spec=pltpu.PrefetchScalarGridSpec(
-            num_scalar_prefetch=1,
-            grid=(1,),
-            in_specs=[
-                pl.BlockSpec(turned.shape, lambda i, info: (0, 0)),
-                pl.BlockSpec(part.shape, lambda i, info: (0, 0)),
-            ]
-            + anywhere,
-            out_specs=[
-                pl.BlockSpec((half, half), lambda i, info: (info[row], info[block])),
-                pl.BlockSpec((8, 128), lambda i, info: (0, 0)),
-            ],
-        ),
+        in_specs=in_specs,
+        out_specs=[pl.BlockSpec(memory_space=pl.ANY), pl.BlockSpec(memory_space=pltpu.VMEM)],
+        scratch_shapes=[pltpu.VMEM((half, half), f32), pltpu.SemaphoreType.DMA],
         input_output_aliases=aliases,
         **common,
     )(info, *operands)
 
 
-def land_kernel(end, info_ref, arrived_ref, own_ref, result_ref, out_ref):
-    out_ref[...] = jnp.where(info_ref[end] > 0, own_ref[...], arrived_ref[...])
-
-
-def land(info, row, block, end, arrived, own, result, name):
+def land_kernel(end, info_ref, arrived_ref, own_ref, *refs):
+    arrived = arrived_ref[...]
+    if len(refs) > 2:
+        arrived = arrived + refs[0][...]
+    refs[-1][...] = jnp.where(info_ref[end] > 0, own_ref[...], arrived)
+
+
+def land(info, row, block, end, arrived, own, late, result, name):
     half = arrived.shape[0]
     tile = 256
     per_half = half // tile
     part = pl.BlockSpec((tile, half), lambda i, info: (i, 0))
+    operands, in_specs = [arrived, own], [part, part]
+    if late is not None:
+        late, late_at = late
+        operands.append(late)
+        in_specs.append(pl.BlockSpec((tile, half), lambda i, info: (late_at * per_half + i, 0)))
     return pl.pallas_call(
         functools.partial(land_kernel, end),
         out_shape=jax.ShapeDtypeStruct(result.shape, f32),
         grid_spec=pltpu.PrefetchScalarGridSpec(
             num_scalar_prefetch=1,
             grid=(per_half,),
-            in_specs=[part, part, pl.BlockSpec(memory_space=pl.ANY)],
+            in_specs=in_specs + [pl.BlockSpec(memory_space=pl.ANY)],
             out_specs=pl.BlockSpec(
                 (tile, half), lambda i, info: (info[row] * per_half + i, info[block])
             ),
         ),
-        input_output_aliases={3: 0},
+        input_output_aliases={1 + len(operands): 0},
         compiler_params=pltpu.CompilerParams(vmem_limit_bytes=VMEM_LIMIT),
         cost_estimate=cost(half * half, 12 * half * half),
         name=name,
-    )(info, arrived, own, result)
+    )(info, *operands, result)
 
 
 def group_pairs(group, ring, plane, senders):
@@ -370,6 +406,7 @@
         LAND_SECOND: jnp.where(core == 0, 0, 3),
         END_FIRST: jnp.where(core == 0, row == 7, row == 0),
         END_SECOND: jnp.where(core == 0, row == 0, row == 7),
+        END_COL: at_end,
     }
     info = jnp.stack([jnp.asarray(values[k], i32) for k in range(len(values))])
 
@@ -397,24 +434,23 @@
     row_pieces = around("col", row_own)
 
     swap = [(i, i ^ 1) for i in range(16)]
-    chips = [(0, 0), (15, 15)]
-    chips += [(i, i - 1) for i in range(2, 16, 2)] + [(i, i + 1) for i in range(1, 15, 2)]
-
-    def row_pairs(down_core):
+    chips = [(i, i - 1) for i in range(2, 16, 2)] + [(i, i + 1) for i in range(1, 15, 2)]
+
+    def row_pairs(down_core, middle, others):
         pairs = []
         for r in range(8):
             for c in range(16):
                 target = r - 1 if c % 2 == down_core else r + 1
-                if 0 <= target < 8:
+                if 0 <= target < 8 and (middle if {r, target} == {3, 4} else others):
                     pairs.append((r * 16 + c, target * 16 + c))
         return pairs
 
-    def leave(k, turned, part, part_at, after):
+    def leave(k, turned, part, after):
         rows = (MOVED_FIRST, MOVED_SECOND)[k // 2]
-        moved = left(info, rows, turned, part, part_at, after, "leave_%d" % k)
-        return moved, lax.ppermute(moved, AXES, row_pairs(k // 2))
-
-    def keep(k, turned, part, part_at, after, result):
+        moved = left(info, rows, turned, part, after, "leave_%d" % k)
+        return moved, lax.ppermute(moved, AXES, row_pairs(k // 2, k // 2 == 1, True))
+
+    def keep(k, turned, part, after, result):
         target = (
             (KEPT_FIRST, KEPT_SECOND)[k // 2],
             (NEAR_BLOCK, FAR_BLOCK)[k % 2],
@@ -422,7 +458,7 @@
             (rows_here, matrix.shape[1]),
         )
         rows = (STAYS_FIRST, STAYS_SECOND)[k // 2]
-        return left(info, rows, turned, part, part_at, after, "keep_%d" % k, target)
+        return left(info, rows, turned, part, after, "keep_%d" % k, target)
 
     row_all = jnp.concatenate(row_pieces, axis=0)
     row_other = lax.ppermute(row_all, "col", swap)
@@ -438,22 +474,24 @@
         after = parts[-1:] if parts else [row_all]
         (sent,) = right(info, [([slot], which)], *factors, after, name)
         parts.append(sent)
-    far_first, far_second = (lax.ppermute(part, "col", chips) for part in parts[:2])
-    near_first, near_second = (lax.ppermute(part, "col", swap) for part in parts[2:])
+    far_first, far_second = ((lax.ppermute(part, "col", chips), part) for part in parts[:2])
+    near_first, near_second = ((lax.ppermute(part, "col", swap),) for part in parts[2:])
     (turned,) = rotation(info, [row_all], RING_ROW, -1, False, parts[3:], "row_rotation")
     moved, landing = [None] * 4, [None] * 4
-    moved[1], landing[1] = leave(1, turned, far_first, 0, [])
-    moved[0], landing[0] = leave(0, turned, near_first, 0, [moved[1]])
+    moved[1], landing[1] = leave(1, turned, far_first, [])
+    moved[0], landing[0] = leave(0, turned, near_first, [moved[1]])
+    late = stacked(info, moved[0], moved[1], moved[0])
     (other_turned,) = rotation(
-        info, [row_other], RING_ROW, -1, False, [moved[0]], "other_row_rotation"
+        info, [row_other], RING_ROW, -1, False, [late], "other_row_rotation"
     )
-    moved[2], landing[2] = leave(2, other_turned, near_second, 0, [])
-    result, _ = keep(0, turned, near_first, 0, [moved[2]], None)
-    result, _ = keep(1, turned, far_first, 0, [], result)
-    result, token = keep(2, other_turned, near_second, 0, [], result)
-    moved[3], landing[3] = leave(3, other_turned, far_second, 0, [token])
-    result, _ = keep(3, other_turned, far_second, 0, [moved[3]], result)
-    for k in range(4):
+    late = lax.ppermute(late, AXES, row_pairs(0, True, False))
+    moved[2], landing[2] = leave(2, other_turned, near_second, [])
+    result, token = keep(0, turned, near_first, [moved[2]], None)
+    moved[3], landing[3] = leave(3, other_turned, far_second, [token])
+    result, _ = keep(1, turned, far_first, [moved[3], landing[1]], result)
+    result, _ = keep(2, other_turned, near_second, [landing[0]], result)
+    result, _ = keep(3, other_turned, far_second, [], result)
+    for k in (2, 0, 1, 3):
         result = land(
             info,
             (LAND_FIRST, LAND_SECOND)[k // 2],
@@ -461,6 +499,7 @@
             (END_FIRST, END_SECOND)[k // 2],
             landing[k],
             moved[(k + 2) % 4],
+            (late, k) if k < 2 else None,
             result,
             "land_%d" % k,
         )

time: 219 us -> 202 us (0.922)
  the two profiles are of different devices: /device:TPU:30 before, /device:TPU:15 now
where the time goes in v5:
time: 202 us; the launch traced here: 198 us
  Pallas kernels  87.8 us (43%)
  starting transfers between devices  60.7 us (30%)
  waiting for transfers between devices  44.8 us (22%)
  local copies, waits for them, and re-layouts  3.49 us (2%)
    pallas_call x3, Pallas kernels, rotation(): pl.pallas_call(functools.partial(rotation_kernel, sign, in_parts, ring, l...  33.4 us
    ppermute x6, starting transfers between devices, around(): lax.ppermute(one, AXES, group_pairs(group, ring, 0, anyone))  30.3 us
    ppermute x2, waiting for transfers between devices, cross(): return lax.ppermute(one, AXES, group_pairs(group, 0, 1, in_source_plane))  26.9 us
    pallas_call x4, Pallas kernels, right(): pl.pallas_call(functools.partial(right_kernel, jobs), out_shape=[jax.Shap...  15.9 us
    pallas_call x4, Pallas kernels, left(): pl.pallas_call(functools.partial(kernel, rows, (row, block)), out_shape=[...  15.3 us
    pallas_call x4, Pallas kernels, left(): pl.pallas_call(functools.partial(kernel, rows, None), out_shape=jax.Shape...  9.56 us
    ppermute x4, waiting for transfers between devices, leave(): lax.ppermute(moved, AXES, row_pairs(k // 2, k // 2 == 1, True))  9.08 us
    ppermute x2, starting transfers between devices, local(): lax.ppermute(part, 'col', chips)  8.88 us
  transfers between devices with their start and end apart: 24, of which 5 were waited for; matrix products, arithmetic and copies ran while one was open for 0% of the time, Pallas kernels for 40%

profile of v5, /device:TPU:15, one launch (start us, length us, event | category | flops | bytes accessed | tf_op | source)
XLA Modules:
  0.0 197.7 jit_solution(11306547087413998520)
XLA Ops:
  0.0 0.1 stack.110.info_ref
  0.1 0.0 copy-start
  0.1 3.4 %copy-done = f32[2048,1024]{1,0:T(8,128)S(1)} copy-done((f32[2048,1024]{1,0:T(8,128)S(1)}, f32[2048,1024]{1,0:T(8,128)}, u32[]{:S(2)}) %copy-start) | copy-done | bytes 8388632
  3.5 1.3 pack.1
  4.8 0.7 collective-permute-start
  5.5 0.7 collective-permute-start.3
  6.2 0.7 collective-permute-start.1
  6.9 0.7 collective-permute-start.2
  7.6 0.7 collective-permute-start.4
  8.3 0.7 collective-permute-start.5
  9.0 0.0 collective-permute-done.1.refs_1_
  9.0 0.0 collective-permute-done.2.refs_2_
  9.0 0.0 collective-permute-done.4.refs_4_
  9.1 0.0 collective-permute-done.5.refs_5_
  9.1 0.0 slice-start.1
  9.1 0.7 merge.1
  9.8 1.4 collective-permute-start.6
  11.2 26.9 %collective-permute-done.6.across = f32[128,1024]{1,0:T(8,128)S(1)} collective-permute-done((f32[128,1024]{1,0:T(8,128)S(1)}, f32[128,1024]{1,0:T(8,128)S(1)}, u32[]{:S(2)}, u32[]{:S(2)}) %collective-permute-start.6) | collective-permute-done | bytes 524320 | tf_op jit(solution)/shard_map/ppermute | solution.py:421
  38.1 0.6 choose_col.1
  38.8 1.3 collective-permute-start.7
  40.1 5.8 %collective-permute-start.12 = (f32[128,1024]{1,0:T(8,128)S(1)}, f32[128,1024]{1,0:T(8,128)S(1)}, u32[]{:S(2)}, u32[]{:S(2)}) collective-permute-start(f32[128,1024]{1,0:T(8,128)S(1)} %get-tuple-element.27.refs_0_), channel_id=1, source_target_pairs={{0,16},{1,17},{2,18},{3,19},{4,20},{5,21},{6,22},{7,23},{8,24},{9,... | collective-permute-start | bytes 1572872 | tf_op jit(solution)/shard_map/ppermute | solution.py:425
  45.9 4.5 %collective-permute-start.13 = (f32[128,1024]{1,0:T(8,128)S(1)}, f32[128,1024]{1,0:T(8,128)S(1)}, u32[]{:S(2)}, u32[]{:S(2)}) collective-permute-start(f32[128,1024]{1,0:T(8,128)S(1)} %get-tuple-element.27.refs_0_), channel_id=1, source_target_pairs={{0,48},{1,49},{2,50},{3,51},{4,52},{5,53},{6,54},{7,55},{8,56},{9,... | collective-permute-start | bytes 1572872 | tf_op jit(solution)/shard_map/ppermute | solution.py:425
  50.4 1.7 collective-permute-start.14
  52.1 0.0 collective-permute-done.7.across
  52.1 0.6 choose_row.1.refs_4_
  52.7 2.8 %collective-permute-start.10 = (f32[128,1024]{1,0:T(8,128)S(1)}, f32[128,1024]{1,0:T(8,128)S(1)}, u32[]{:S(2)}, u32[]{:S(2)}) collective-permute-start(f32[128,1024]{1,0:T(8,128)S(1)} %choose_row.1.refs_4_), channel_id=1, source_target_pairs={{0,4},{1,5},{2,6},{3,7},{4,0},{5,1},{6,2},{7,3},{8,12},{9,13},{10,... | collective-permute-start | bytes 1572872 | tf_op jit(solution)/shard_map/ppermute | solution.py:425
  55.5 12.9 %collective-permute-start.8 = (f32[128,1024]{1,0:T(8,128)S(1)}, f32[128,1024]{1,0:T(8,128)S(1)}, u32[]{:S(2)}, u32[]{:S(2)}) collective-permute-start(f32[128,1024]{1,0:T(8,128)S(1)} %choose_row.1.refs_4_), channel_id=1, source_target_pairs={{0,2},{1,3},{2,4},{3,5},{4,6},{5,7},{6,0},{7,1},{8,10},{9,11},{10,... | collective-permute-start | bytes 1572872 | tf_op jit(solution)/shard_map/ppermute | solution.py:425
  68.5 0.0 collective-permute-done.12.refs_1_
  68.5 2.5 %collective-permute-start.9 = (f32[128,1024]{1,0:T(8,128)S(1)}, f32[128,1024]{1,0:T(8,128)S(1)}, u32[]{:S(2)}, u32[]{:S(2)}) collective-permute-start(f32[128,1024]{1,0:T(8,128)S(1)} %choose_row.1.refs_4_), channel_id=1, source_target_pairs={{0,6},{1,7},{2,0},{3,1},{4,2},{5,3},{6,4},{7,5},{8,14},{9,15},{10,... | collective-permute-start | bytes 1572872 | tf_op jit(solution)/shard_map/ppermute | solution.py:425
  71.0 1.1 collective-permute-done.14.refs_3_
  72.0 11.2 %column_rotation.1 = (bf16[1024,1024]{1,0:T(8,128)(2,1)S(1)}, bf16[1024,1024]{1,0:T(8,128)(2,1)S(1)}) custom-call(s32[24]{0:T(128)S(1)} %stack.110.info_ref, f32[128,1024]{1,0:T(8,128)S(1)} %get-tuple-element.27.refs_0_, f32[128,1024]{1,0:T(8,128)S(1)} %collective-permute-done.12.refs_1_, f32[128,1024]{1,0:T(8,128)S(1)} %collective-permute-done.13.refs_2_, ...), custom_call_target="tpu_custom_call" | custom-call | flops 201326592 | bytes 98304 | tf_op jit(solution)/shard_map/column_rotation/pallas_call | solution.py:205
  83.3 7.7 %collective-permute-done.9 = f32[128,1024]{1,0:T(8,128)S(1)} collective-permute-done((f32[128,1024]{1,0:T(8,128)S(1)}, f32[128,1024]{1,0:T(8,128)S(1)}, u32[]{:S(2)}, u32[]{:S(2)}) %collective-permute-start.9) | collective-permute-done | bytes 524320 | tf_op jit(solution)/shard_map/ppermute | solution.py:425
  91.0 0.2 pad_maximum_fusion.refs_0_
  91.3 4.0 %right_far_first.1.refs_0_.own_ref = f32[1024,512]{1,0:T(8,128)S(1)} custom-call(s32[24]{0:T(128)S(1)} %stack.110.info_ref, f32[2048,1024]{1,0:T(8,128)S(1)} %bitcast.22, bf16[1024,1024]{1,0:T(8,128)(2,1)S(1)} %get-tuple-element.28.high_ref, bf16[1024,1024]{1,0:T(8,128)(2,1)S(1)} %get-tuple-element.29.low_ref, f32[512,1024]{1,0:T(8,128)S(1)} %pad_maximum_fusion.refs_0_), custom_call_target="tpu_custom_call" | custom-call | flops 150994944 | bytes 131072 | tf_op jit(solution)/shard_map/right_far_first/pallas_call | solution.py:235
  95.2 6.3 %collective-permute-start.16 = (f32[1024,512]{1,0:T(8,128)S(1)}, f32[1024,512]{1,0:T(8,128)S(1)}, u32[]{:S(2)}, u32[]{:S(2)}) collective-permute-start(f32[1024,512]{1,0:T(8,128)S(1)} %right_far_first.1.refs_0_.own_ref), channel_id=1, source_target_pairs={{2,1},{4,3},{6,5},{8,7},{10,9},{12,11},{14,13},{1,2},{3,4},{5,6},{... | collective-permute-start | bytes 6291464 | tf_op jit(solution)/shard_map/ppermute | solution.py:477
  101.5 0.3 collective-permute-start.11
  101.9 4.0 %right_far_second.1.refs_0_.own_ref = f32[1024,512]{1,0:T(8,128)S(1)} custom-call(s32[24]{0:T(128)S(1)} %stack.110.info_ref, f32[2048,1024]{1,0:T(8,128)S(1)} %bitcast.22, bf16[1024,1024]{1,0:T(8,128)(2,1)S(1)} %get-tuple-element.28.high_ref, bf16[1024,1024]{1,0:T(8,128)(2,1)S(1)} %get-tuple-element.29.low_ref, f32[1024,512]{1,0:T(8,128)S(1)} %right_far_first.1.refs_0_.own_ref), custom_call_target="tpu_custom_call" | custom-call | flops 150994944 | bytes 131072 | tf_op jit(solution)/shard_map/right_far_second/pallas_call | solution.py:235
  105.8 2.6 %collective-permute-start.17 = (f32[1024,512]{1,0:T(8,128)S(1)}, f32[1024,512]{1,0:T(8,128)S(1)}, u32[]{:S(2)}, u32[]{:S(2)}) collective-permute-start(f32[1024,512]{1,0:T(8,128)S(1)} %right_far_second.1.refs_0_.own_ref), channel_id=1, source_target_pairs={{2,1},{4,3},{6,5},{8,7},{10,9},{12,11},{14,13},{1,2},{3,4},{5,6},{... | collective-permute-start | bytes 6291464 | tf_op jit(solution)/shard_map/ppermute | solution.py:477
  108.4 4.0 %right_near_first.1.refs_0_ = f32[1024,512]{1,0:T(8,128)S(1)} custom-call(s32[24]{0:T(128)S(1)} %stack.110.info_ref, f32[2048,1024]{1,0:T(8,128)S(1)} %bitcast.22, bf16[1024,1024]{1,0:T(8,128)(2,1)S(1)} %get-tuple-element.28.high_ref, bf16[1024,1024]{1,0:T(8,128)(2,1)S(1)} %get-tuple-element.29.low_ref, f32[1024,512]{1,0:T(8,128)S(1)} %right_far_second.1.refs_0_.own_ref), custom_call_target="tpu_custom_call" | custom-call | flops 150994944 | bytes 131072 | tf_op jit(solution)/shard_map/right_near_first/pallas_call | solution.py:235
  112.4 0.9 collective-permute-start.15
  113.3 4.0 %right_near_second.1.refs_1_ = f32[1024,512]{1,0:T(8,128)S(1)} custom-call(s32[24]{0:T(128)S(1)} %stack.110.info_ref, f32[2048,1024]{1,0:T(8,128)S(1)} %bitcast.22, bf16[1024,1024]{1,0:T(8,128)(2,1)S(1)} %get-tuple-element.28.high_ref, bf16[1024,1024]{1,0:T(8,128)(2,1)S(1)} %get-tuple-element.29.low_ref, f32[1024,512]{1,0:T(8,128)S(1)} %right_near_first.1.refs_0_), custom_call_target="tpu_custom_call" | custom-call | flops 150994944 | bytes 131072 | tf_op jit(solution)/shard_map/right_near_second/pallas_call | solution.py:235
  117.2 0.6 collective-permute-start.18
  117.8 11.1 %row_rotation.1.turned_ref = f32[1024,1024]{1,0:T(8,128)S(1)} custom-call(s32[24]{0:T(128)S(1)} %stack.110.info_ref, f32[512,1024]{1,0:T(8,128)S(1)} %pad_maximum_fusion.refs_0_, f32[1024,512]{1,0:T(8,128)S(1)} %right_near_second.1.refs_1_), custom_call_target="tpu_custom_call" | custom-call | flops 201326592 | bytes 98304 | tf_op jit(solution)/shard_map/row_rotation/pallas_call | solution.py:205
  128.9 2.4 %leave_1.1.refs_0_.bottom.own_ref = f32[512,512]{1,0:T(8,128)S(1)} custom-call(s32[24]{0:T(128)S(1)} %stack.110.info_ref, f32[1024,1024]{1,0:T(8,128)S(1)} %row_rotation.1.turned_ref, f32[1024,512]{1,0:T(8,128)S(1)} %collective-permute-done.16.part_ref, f32[1024,512]{1,0:T(8,128)S(1)} %right_far_first.1.refs_0_.own_ref), custom_call_target="tpu_custom_call" | custom-call | flops 25769803776 | bytes 100663296 | tf_op jit(solution)/shard_map/leave_1/pallas_call | solution.py:289
  131.3 2.4 %leave_0.1.top.after.own_ref = f32[512,512]{1,0:T(8,128)S(1)} custom-call(s32[24]{0:T(128)S(1)} %stack.110.info_ref, f32[1024,1024]{1,0:T(8,128)S(1)} %row_rotation.1.turned_ref, f32[1024,512]{1,0:T(8,128)S(1)} %collective-permute-done.15.part_ref, f32[512,512]{1,0:T(8,128)S(1)} %leave_1.1.refs_0_.bottom.own_ref), custom_call_target="tpu_custom_call" | custom-call | flops 25769803776 | bytes 100663296 | tf_op jit(solution)/shard_map/leave_0/pallas_call | solution.py:289
  133.7 1.3 collective-permute-start.20
  135.0 2.0 %stacked.1.refs_1_ = f32[1024,512]{1,0:T(8,128)} custom-call(s32[24]{0:T(128)S(1)} %stack.110.info_ref, f32[512,512]{1,0:T(8,128)S(1)} %leave_0.1.top.after.own_ref, f32[512,512]{1,0:T(8,128)S(1)} %leave_1.1.refs_0_.bottom.own_ref, f32[512,512]{1,0:T(8,128)S(1)} %leave_0.1.top.after.own_ref), custom_call_target="tpu_custom_call" | custom-call | flops 4096 | bytes 65536 | tf_op jit(solution)/shard_map/stacked/pallas_call | solution.py:116
  137.0 1.3 collective-permute-start.22
  138.3 5.8 %collective-permute-start.21 = (f32[1024,512]{1,0:T(8,128)}, f32[1024,512]{1,0:T(8,128)}, u32[]{:S(2)}, u32[]{:S(2)}) collective-permute-start(f32[1024,512]{1,0:T(8,128)} %stacked.1.refs_1_), channel_id=1, source_target_pairs={{49,65},{51,67},{53,69},{55,71},{57,73},{59,75},{61,77},{63,79},{6... | collective-permute-start | bytes 6291464 | tf_op jit(solution)/shard_map/ppermute | solution.py:487
  144.1 11.1 %other_row_rotation.1.turned_ref = f32[1024,1024]{1,0:T(8,128)S(1)} custom-call(s32[24]{0:T(128)S(1)} %stack.110.info_ref, f32[512,1024]{1,0:T(8,128)S(1)} %collective-permute-done.11.refs_0_, f32[1024,512]{1,0:T(8,128)} %stacked.1.refs_1_), custom_call_target="tpu_custom_call" | custom-call | flops 201326592 | bytes 98304 | tf_op jit(solution)/shard_map/other_row_rotation/pallas_call | solution.py:205
  155.2 2.4 %leave_2.1.refs_0_.own_ref = f32[512,512]{1,0:T(8,128)S(1)} custom-call(s32[24]{0:T(128)S(1)} %stack.110.info_ref, f32[1024,1024]{1,0:T(8,128)S(1)} %other_row_rotation.1.turned_ref, f32[1024,512]{1,0:T(8,128)S(1)} %collective-permute-done.18.part_ref), custom_call_target="tpu_custom_call" | custom-call | flops 25769803776 | bytes 100663296 | tf_op jit(solution)/shard_map/leave_2/pallas_call | solution.py:289
  157.6 1.9 collective-permute-start.23
  159.6 3.4 %keep_0.1 = (f32[2048,1024]{1,0:T(8,128)}, f32[8,128]{1,0:T(8,128)S(1)}) custom-call(s32[24]{0:T(128)S(1)} %stack.110.info_ref, f32[1024,1024]{1,0:T(8,128)S(1)} %row_rotation.1.turned_ref, f32[1024,512]{1,0:T(8,128)S(1)} %collective-permute-done.15.part_ref, f32[512,512]{1,0:T(8,128)S(1)} %leave_2.1.refs_0_.own_ref), custom_call_target="tpu_custom_call" | custom-call | flops 25769803776 | bytes 100663296 | tf_op jit(solution)/shard_map/keep_0/pallas_call | solution.py:302
  162.9 2.4 %leave_3.1.refs_0_.own_ref = f32[512,512]{1,0:T(8,128)S(1)} custom-call(s32[24]{0:T(128)S(1)} %stack.110.info_ref, f32[1024,1024]{1,0:T(8,128)S(1)} %other_row_rotation.1.turned_ref, f32[1024,512]{1,0:T(8,128)S(1)} %collective-permute-done.17.part_ref, f32[1024,512]{1,0:T(8,128)S(1)} %right_far_second.1.refs_0_.own_ref, f32[8,128]{1,0:T(8,128)S(1)} %get-tuple-element.30.refs_0_), custom_call_target="tpu_custom_call" | custom-call | flops 25769803776 | bytes 100663296 | tf_op jit(solution)/shard_map/leave_3/pallas_call | solution.py:289
  165.3 2.6 %collective-permute-start.19 = (f32[512,512]{1,0:T(8,128)S(1)}, f32[512,512]{1,0:T(8,128)S(1)}, u32[]{:S(2)}, u32[]{:S(2)}) collective-permute-start(f32[512,512]{1,0:T(8,128)S(1)} %leave_3.1.refs_0_.own_ref), channel_id=1, source_target_pairs={{0,16},{2,18},{4,20},{6,22},{8,24},{10,26},{12,28},{14,30},{16,32}... | collective-permute-start | bytes 3145736 | tf_op jit(solution)/shard_map/ppermute | solution.py:451
  168.0 4.0 %keep_1.1 = (f32[2048,1024]{1,0:T(8,128)}, f32[8,128]{1,0:T(8,128)}) custom-call(s32[24]{0:T(128)S(1)} %stack.110.info_ref, f32[1024,1024]{1,0:T(8,128)S(1)} %row_rotation.1.turned_ref, f32[1024,512]{1,0:T(8,128)S(1)} %collective-permute-done.16.part_ref, f32[1024,512]{1,0:T(8,128)S(1)} %right_far_first.1.refs_0_.own_ref, ...), custom_call_target="tpu_custom_call", output_to_operand_aliasing={{0}: (6, {})} | custom-call | flops 25769803776 | bytes 100663296 | tf_op jit(solution)/shard_map/keep_1/pallas_call | solution.py:302
  172.0 3.9 %keep_2.1 = (f32[2048,1024]{1,0:T(8,128)}, f32[8,128]{1,0:T(8,128)}) custom-call(s32[24]{0:T(128)S(1)} %stack.110.info_ref, f32[1024,1024]{1,0:T(8,128)S(1)} %other_row_rotation.1.turned_ref, f32[1024,512]{1,0:T(8,128)S(1)} %collective-permute-done.18.part_ref, ...), custom_call_target="tpu_custom_call", output_to_operand_aliasing={{0}: (4, {})} | custom-call | flops 25769803776 | bytes 100663296 | tf_op jit(solution)/shard_map/keep_2/pallas_call | solution.py:302
  175.9 4.0 %keep_3.1 = (f32[2048,1024]{1,0:T(8,128)}, f32[8,128]{1,0:T(8,128)}) custom-call(s32[24]{0:T(128)S(1)} %stack.110.info_ref, f32[1024,1024]{1,0:T(8,128)S(1)} %other_row_rotation.1.turned_ref, f32[1024,512]{1,0:T(8,128)S(1)} %collective-permute-done.17.part_ref, f32[1024,512]{1,0:T(8,128)S(1)} %right_far_second.1.refs_0_.own_ref, ...), custom_call_target="tpu_custom_call", output_to_operand_aliasing={{0}: (4, {})} | custom-call | flops 25769803776 | bytes 100663296 | tf_op jit(solution)/shard_map/keep_3/pallas_call | solution.py:302
  179.9 4.7 %collective-permute-done.23.arrived_ref = f32[512,512]{1,0:T(8,128)S(1)} collective-permute-done((f32[512,512]{1,0:T(8,128)S(1)}, f32[512,512]{1,0:T(8,128)S(1)}, u32[]{:S(2)}, u32[]{:S(2)}) %collective-permute-start.23) | collective-permute-done | bytes 1048608 | tf_op jit(solution)/shard_map/ppermute | solution.py:451
  184.6 1.6 land_2.1.refs_1_
  186.2 2.6 %land_0.1.refs_1_ = f32[2048,1024]{1,0:T(8,128)} custom-call(s32[24]{0:T(128)S(1)} %stack.110.info_ref, f32[512,512]{1,0:T(8,128)S(1)} %collective-permute-done.22.refs_0_.arrived_ref, f32[512,512]{1,0:T(8,128)S(1)} %leave_2.1.refs_0_.own_ref, f32[1024,512]{1,0:T(8,128)} %collective-permute-done.21.refs_0_, ...), custom_call_target="tpu_custom_call", output_to_operand_aliasing={{}: (4, {})} | custom-call | flops 4096 | bytes 49152 | tf_op jit(solution)/shard_map/land_0/pallas_call | solution.py:330
  188.9 2.6 %land_1.1.refs_0_ = f32[2048,1024]{1,0:T(8,128)} custom-call(s32[24]{0:T(128)S(1)} %stack.110.info_ref, f32[512,512]{1,0:T(8,128)S(1)} %collective-permute-done.20.refs_1_.arrived_ref, f32[512,512]{1,0:T(8,128)S(1)} %leave_3.1.refs_0_.own_ref, f32[1024,512]{1,0:T(8,128)} %collective-permute-done.21.refs_0_, ...), custom_call_target="tpu_custom_call", output_to_operand_aliasing={{}: (4, {})} | custom-call | flops 4096 | bytes 49152 | tf_op jit(solution)/shard_map/land_1/pallas_call | solution.py:330
  191.5 4.4 %collective-permute-done.19.arrived_ref = f32[512,512]{1,0:T(8,128)S(1)} collective-permute-done((f32[512,512]{1,0:T(8,128)S(1)}, f32[512,512]{1,0:T(8,128)S(1)}, u32[]{:S(2)}, u32[]{:S(2)}) %collective-permute-start.19) | collective-permute-done | bytes 1048608 | tf_op jit(solution)/shard_map/ppermute | solution.py:451
  195.9 1.6 land_3.1
  (17 shorter events, 0.0 us)
Async XLA Ops:
  0.1 3.4 %copy-start = (f32[2048,1024]{1,0:T(8,128)S(1)}, f32[2048,1024]{1,0:T(8,128)}, u32[]{:S(2)}) copy-start(f32[2048,1024]{1,0:T(8,128)} %m_ref.7) | copy-start | bytes 25165828
  3.5 87.7 %slice-start = ((s8[8388608]{0:T(1024)(128)(4,1)}), s8[4194304]{0:T(1024)(128)(4,1)S(1)}, s32[]{:S(2)}) async-start(s8[8388608]{0:T(1024)(128)(4,1)} %bitcast.21), calls=%async_computation | async-start | bytes 8388608
  4.8 3.5 %collective-permute-start = (f32[128,1024]{1,0:T(8,128)S(1)}, f32[128,1024]{1,0:T(8,128)S(1)}, u32[]{:S(2)}, u32[]{:S(2)}) collective-permute-start(f32[128,1024]{1,0:T(8,128)S(1)} %get-tuple-element.21), channel_id=1, source_target_pairs={{0,16},{1,17},{18,34},{19,35},{36,52},{37,53},{54,6},{55,7},{72,88... | collective-permute-start | bytes 1572872 | tf_op jit(solution)/shard_map/ppermute | solution.py:415
  5.5 3.5 %collective-permute-start.3 = (f32[128,1024]{1,0:T(8,128)S(1)}, f32[128,1024]{1,0:T(8,128)S(1)}, u32[]{:S(2)}, u32[]{:S(2)}) collective-permute-start(f32[128,1024]{1,0:T(8,128)S(1)} %get-tuple-element.21), channel_id=1, source_target_pairs={{0,2},{1,3},{18,20},{19,21},{36,38},{37,39},{54,48},{55,49},{72,74... | collective-permute-start | bytes 1572872 | tf_op jit(solution)/shard_map/ppermute | solution.py:415
  6.2 2.8 %collective-permute-start.1 = (f32[128,1024]{1,0:T(8,128)S(1)}, f32[128,1024]{1,0:T(8,128)S(1)}, u32[]{:S(2)}, u32[]{:S(2)}) collective-permute-start(f32[128,1024]{1,0:T(8,128)S(1)} %get-tuple-element.22), channel_id=1, source_target_pairs={{0,48},{1,49},{18,2},{19,3},{36,20},{37,21},{54,38},{55,39},{72,12... | collective-permute-start | bytes 1572872 | tf_op jit(solution)/shard_map/ppermute | solution.py:415
  6.9 2.1 %collective-permute-start.2 = (f32[128,1024]{1,0:T(8,128)S(1)}, f32[128,1024]{1,0:T(8,128)S(1)}, u32[]{:S(2)}, u32[]{:S(2)}) collective-permute-start(f32[128,1024]{1,0:T(8,128)S(1)} %get-tuple-element.23), channel_id=1, source_target_pairs={{0,32},{1,33},{18,50},{19,51},{36,4},{37,5},{54,22},{55,23},{72,10... | collective-permute-start | bytes 1572872 | tf_op jit(solution)/shard_map/ppermute | solution.py:415
  7.6 1.4 collective-permute-start.4
  8.3 0.7 collective-permute-start.5
  9.1 82.2 %slice-start.1 = ((s8[8388608]{0:T(1024)(128)(4,1)}), s8[4194304]{0:T(1024)(128)(4,1)S(1)}, s32[]{:S(2)}) async-start(s8[8388608]{0:T(1024)(128)(4,1)} %bitcast.21), calls=%async_computation.1 | async-start | bytes 8388608
  9.8 28.3 %collective-permute-start.6 = (f32[128,1024]{1,0:T(8,128)S(1)}, f32[128,1024]{1,0:T(8,128)S(1)}, u32[]{:S(2)}, u32[]{:S(2)}) collective-permute-start(f32[128,1024]{1,0:T(8,128)S(1)} %get-tuple-element.24.held), channel_id=1, source_target_pairs={{0,64},{1,65},{2,66},{3,67},{4,68},{5,69},{6,70},{7,71},{16,80},{1... | collective-permute-start | bytes 1572872 | tf_op jit(solution)/shard_map/ppermute | solution.py:421
  38.8 13.3 %collective-permute-start.7 = (f32[128,1024]{1,0:T(8,128)S(1)}, f32[128,1024]{1,0:T(8,128)S(1)}, u32[]{:S(2)}, u32[]{:S(2)}) collective-permute-start(f32[128,1024]{1,0:T(8,128)S(1)} %get-tuple-element.26.held), channel_id=1, source_target_pairs={{0,8},{1,9},{2,10},{3,11},{4,12},{5,13},{6,14},{7,15},{16,24},{17,... | collective-permute-start | bytes 1572872 | tf_op jit(solution)/shard_map/ppermute | solution.py:421
  40.1 28.4 %collective-permute-start.12 = (f32[128,1024]{1,0:T(8,128)S(1)}, f32[128,1024]{1,0:T(8,128)S(1)}, u32[]{:S(2)}, u32[]{:S(2)}) collective-permute-start(f32[128,1024]{1,0:T(8,128)S(1)} %get-tuple-element.27.refs_0_), channel_id=1, source_target_pairs={{0,16},{1,17},{2,18},{3,19},{4,20},{5,21},{6,22},{7,23},{8,24},{9,... | collective-permute-start | bytes 1572872 | tf_op jit(solution)/shard_map/ppermute | solution.py:425
  45.9 25.0 %collective-permute-start.13 = (f32[128,1024]{1,0:T(8,128)S(1)}, f32[128,1024]{1,0:T(8,128)S(1)}, u32[]{:S(2)}, u32[]{:S(2)}) collective-permute-start(f32[128,1024]{1,0:T(8,128)S(1)} %get-tuple-element.27.refs_0_), channel_id=1, source_target_pairs={{0,48},{1,49},{2,50},{3,51},{4,52},{5,53},{6,54},{7,55},{8,56},{9,... | collective-permute-start | bytes 1572872 | tf_op jit(solution)/shard_map/ppermute | solution.py:425
  50.4 21.6 %collective-permute-start.14 = (f32[128,1024]{1,0:T(8,128)S(1)}, f32[128,1024]{1,0:T(8,128)S(1)}, u32[]{:S(2)}, u32[]{:S(2)}) collective-permute-start(f32[128,1024]{1,0:T(8,128)S(1)} %get-tuple-element.27.refs_0_), channel_id=1, source_target_pairs={{0,32},{1,33},{2,34},{3,35},{4,36},{5,37},{6,38},{7,39},{8,40},{9,... | collective-permute-start | bytes 1572872 | tf_op jit(solution)/shard_map/ppermute | solution.py:425
  52.7 30.5 %collective-permute-start.10 = (f32[128,1024]{1,0:T(8,128)S(1)}, f32[128,1024]{1,0:T(8,128)S(1)}, u32[]{:S(2)}, u32[]{:S(2)}) collective-permute-start(f32[128,1024]{1,0:T(8,128)S(1)} %choose_row.1.refs_4_), channel_id=1, source_target_pairs={{0,4},{1,5},{2,6},{3,7},{4,0},{5,1},{6,2},{7,3},{8,12},{9,13},{10,... | collective-permute-start | bytes 1572872 | tf_op jit(solution)/shard_map/ppermute | solution.py:425
  55.5 27.7 %collective-permute-start.8 = (f32[128,1024]{1,0:T(8,128)S(1)}, f32[128,1024]{1,0:T(8,128)S(1)}, u32[]{:S(2)}, u32[]{:S(2)}) collective-permute-start(f32[128,1024]{1,0:T(8,128)S(1)} %choose_row.1.refs_4_), channel_id=1, source_target_pairs={{0,2},{1,3},{2,4},{3,5},{4,6},{5,7},{6,0},{7,1},{8,10},{9,11},{10,... | collective-permute-start | bytes 1572872 | tf_op jit(solution)/shard_map/ppermute | solution.py:425
  68.5 22.5 %collective-permute-start.9 = (f32[128,1024]{1,0:T(8,128)S(1)}, f32[128,1024]{1,0:T(8,128)S(1)}, u32[]{:S(2)}, u32[]{:S(2)}) collective-permute-start(f32[128,1024]{1,0:T(8,128)S(1)} %choose_row.1.refs_4_), channel_id=1, source_target_pairs={{0,6},{1,7},{2,0},{3,1},{4,2},{5,3},{6,4},{7,5},{8,14},{9,15},{10,... | collective-permute-start | bytes 1572872 | tf_op jit(solution)/shard_map/ppermute | solution.py:425
  95.2 33.7 %collective-permute-start.16 = (f32[1024,512]{1,0:T(8,128)S(1)}, f32[1024,512]{1,0:T(8,128)S(1)}, u32[]{:S(2)}, u32[]{:S(2)}) collective-permute-start(f32[1024,512]{1,0:T(8,128)S(1)} %right_far_first.1.refs_0_.own_ref), channel_id=1, source_target_pairs={{2,1},{4,3},{6,5},{8,7},{10,9},{12,11},{14,13},{1,2},{3,4},{5,6},{... | collective-permute-start | bytes 6291464 | tf_op jit(solution)/shard_map/ppermute | solution.py:477
  101.5 36.8 %collective-permute-start.11 = (f32[512,1024]{1,0:T(8,128)S(1)}, f32[512,1024]{1,0:T(8,128)S(1)}, u32[]{:S(2)}, u32[]{:S(2)}) collective-permute-start(f32[512,1024]{1,0:T(8,128)S(1)} %pad_maximum_fusion.refs_0_), channel_id=1, source_target_pairs={{0,1},{1,0},{2,3},{3,2},{4,5},{5,4},{6,7},{7,6},{8,9},{9,8},{10,11... | collective-permute-start | bytes 6291464 | tf_op jit(solution)/shard_map/ppermute | solution.py:464
  105.8 57.1 %collective-permute-start.17 = (f32[1024,512]{1,0:T(8,128)S(1)}, f32[1024,512]{1,0:T(8,128)S(1)}, u32[]{:S(2)}, u32[]{:S(2)}) collective-permute-start(f32[1024,512]{1,0:T(8,128)S(1)} %right_far_second.1.refs_0_.own_ref), channel_id=1, source_target_pairs={{2,1},{4,3},{6,5},{8,7},{10,9},{12,11},{14,13},{1,2},{3,4},{5,6},{... | collective-permute-start | bytes 6291464 | tf_op jit(solution)/shard_map/ppermute | solution.py:477
  112.4 18.9 %collective-permute-start.15 = (f32[1024,512]{1,0:T(8,128)S(1)}, f32[1024,512]{1,0:T(8,128)S(1)}, u32[]{:S(2)}, u32[]{:S(2)}) collective-permute-start(f32[1024,512]{1,0:T(8,128)S(1)} %right_near_first.1.refs_0_), channel_id=1, source_target_pairs={{0,1},{1,0},{2,3},{3,2},{4,5},{5,4},{6,7},{7,6},{8,9},{9,8},{10,11... | collective-permute-start | bytes 6291464 | tf_op jit(solution)/shard_map/ppermute | solution.py:478
  117.2 38.0 %collective-permute-start.18 = (f32[1024,512]{1,0:T(8,128)S(1)}, f32[1024,512]{1,0:T(8,128)S(1)}, u32[]{:S(2)}, u32[]{:S(2)}) collective-permute-start(f32[1024,512]{1,0:T(8,128)S(1)} %right_near_second.1.refs_1_), channel_id=1, source_target_pairs={{0,1},{1,0},{2,3},{3,2},{4,5},{5,4},{6,7},{7,6},{8,9},{9,8},{10,11... | collective-permute-start | bytes 6291464 | tf_op jit(solution)/shard_map/ppermute | solution.py:478
  133.7 34.2 %collective-permute-start.20 = (f32[512,512]{1,0:T(8,128)S(1)}, f32[512,512]{1,0:T(8,128)S(1)}, u32[]{:S(2)}, u32[]{:S(2)}) collective-permute-start(f32[512,512]{1,0:T(8,128)S(1)} %leave_1.1.refs_0_.bottom.own_ref), channel_id=1, source_target_pairs={{1,17},{3,19},{5,21},{7,23},{9,25},{11,27},{13,29},{15,31},{16,0},... | collective-permute-start | bytes 3145736 | tf_op jit(solution)/shard_map/ppermute | solution.py:451
  137.0 34.9 %collective-permute-start.22 = (f32[512,512]{1,0:T(8,128)S(1)}, f32[512,512]{1,0:T(8,128)S(1)}, u32[]{:S(2)}, u32[]{:S(2)}) collective-permute-start(f32[512,512]{1,0:T(8,128)S(1)} %leave_0.1.top.after.own_ref), channel_id=1, source_target_pairs={{1,17},{3,19},{5,21},{7,23},{9,25},{11,27},{13,29},{15,31},{16,0},... | collective-permute-start | bytes 3145736 | tf_op jit(solution)/shard_map/ppermute | solution.py:451
  138.3 47.9 %collective-permute-start.21 = (f32[1024,512]{1,0:T(8,128)}, f32[1024,512]{1,0:T(8,128)}, u32[]{:S(2)}, u32[]{:S(2)}) collective-permute-start(f32[1024,512]{1,0:T(8,128)} %stacked.1.refs_1_), channel_id=1, source_target_pairs={{49,65},{51,67},{53,69},{55,71},{57,73},{59,75},{61,77},{63,79},{6... | collective-permute-start | bytes 6291464 | tf_op jit(solution)/shard_map/ppermute | solution.py:487
  157.6 27.0 %collective-permute-start.23 = (f32[512,512]{1,0:T(8,128)S(1)}, f32[512,512]{1,0:T(8,128)S(1)}, u32[]{:S(2)}, u32[]{:S(2)}) collective-permute-start(f32[512,512]{1,0:T(8,128)S(1)} %leave_2.1.refs_0_.own_ref), channel_id=1, source_target_pairs={{0,16},{2,18},{4,20},{6,22},{8,24},{10,26},{12,28},{14,30},{16,32}... | collective-permute-start | bytes 3145736 | tf_op jit(solution)/shard_map/ppermute | solution.py:451
  165.3 30.5 %collective-permute-start.19 = (f32[512,512]{1,0:T(8,128)S(1)}, f32[512,512]{1,0:T(8,128)S(1)}, u32[]{:S(2)}, u32[]{:S(2)}) collective-permute-start(f32[512,512]{1,0:T(8,128)S(1)} %leave_3.1.refs_0_.own_ref), channel_id=1, source_target_pairs={{0,16},{2,18},{4,20},{6,22},{8,24},{10,26},{12,28},{14,30},{16,32}... | collective-permute-start | bytes 3145736 | tf_op jit(solution)/shard_map/ppermute | solution.py:451
